TPU v7x, 512 devices: a whole 4x8x8 slice. The times are simulated.
512 devices in a mesh: leaf: 16 (over y, z_lo), panel: 32 (over z_hi, x, core).
Axes of the slice: x: 4, y: 8, z: 8 (z_hi: 4, z_lo: 2; z = z_hi * 2 + z_lo), core: 2. Of those that a mesh axis runs over, the one named last changes fastest.
Arguments:
- child_stiff: bfloat16 [16, 4096, 4096], P('leaf', None, 'panel'), may hold values from -4 to 4
- child_bound: bfloat16 [16, 4096, 2048], P('leaf', 'panel'), may hold values from -6 to 6
- child_modes: bfloat16 [16, 2048, 512], P('leaf'), may hold values from -0.125 to 0.125
- child_inv_eig: float32 [16, 512], P('leaf'), may hold values from 0.005 to 0.1
- child_map: int32 [16, 32], P('leaf'), may hold values from 0 to 31
- parent_bound: bfloat16 [16, 4096, 2048], P('leaf', 'panel'), may hold values from -6 to 6
- parent_modes: bfloat16 [16, 2048, 256], P('leaf'), may hold values from -0.125 to 0.125
- parent_inv_eig: float32 [16, 256], P('leaf'), may hold values from 0.005 to 0.1
- parent_map: int32 [8, 32], replicated, may hold values from 0 to 31
- interface_basis: bfloat16 [16, 4096, 256], P('leaf', 'panel'), may hold values from -0.09375 to 0.09375
Outputs:
- reduced: float32 [16, 256, 1024], P('leaf', 'panel')
Inputs may be any that keep to these rules, and one draw needn't show every extreme that they name: `child_map`: each entry names a panel of the section below. `parent_map`: each entry names a panel of the parent section.
All inputs are finite; a program needn't handle non-finite values.
Results may differ from a plain program's by a relative error of at most 0.023.
Values may be sent and summed in bfloat16 or wider, within the bound.
No kernel may reach another device: no remote copies, remote signals or barrier semaphores. Data moves between devices by JAX's collectives and lax.ppermute only.
A program may use at most 128 MiB of HBM per device.

v0:
```python
import jax
import jax.numpy as jnp
from jax import lax
from jax.sharding import PartitionSpec as P


def partner(value, axis, apart):
    mask = 2**apart
    pairs = [(source, source ^ mask) for source in range(lax.axis_size(axis))]
    return lax.ppermute(value, axis, pairs)


def regroup(matrix, panel_index):
    panels = panel_index.shape[0]
    stacked = matrix.reshape(panels, matrix.shape[0] // panels, matrix.shape[1])
    return jnp.take(stacked, panel_index, axis=0).reshape(matrix.shape)


def scale_rows(coupling, inv_eig):
    return (coupling.astype(jnp.float32) * inv_eig[None, :]).astype(jnp.bfloat16)


def outer_rows(left_rows, right_rows):
    return jnp.einsum("rm,cm->rc", left_rows, right_rows, preferred_element_type=jnp.float32)


def shards(
    child_stiff,
    child_bound,
    child_modes,
    child_inv_eig,
    child_map,
    parent_bound,
    parent_modes,
    parent_inv_eig,
    parent_map,
    interface_basis,
):
    stiffness = child_stiff[0]
    leaf_index = lax.axis_index("leaf")
    child_side = leaf_index % 2
    parent_side = leaf_index // 2 % 2
    own_basis = interface_basis[0]
    section_modes = child_modes[0]
    coupling_rows = jnp.dot(
        child_bound[0], section_modes, preferred_element_type=jnp.float32
    ).astype(jnp.bfloat16)
    scaled_rows = scale_rows(coupling_rows, child_inv_eig[0])
    schur_block = stiffness.astype(jnp.float32)
    current = schur_block
    schur_block = current - outer_rows(
        lax.all_gather(coupling_rows, "panel", axis=0, tiled=True), scaled_rows
    )
    basis_all = lax.all_gather(own_basis, "panel", axis=0, tiled=True)
    schur_block, basis_all = (schur_block, basis_all)
    parent_rows = jnp.dot(
        parent_bound[0], parent_modes[0], preferred_element_type=jnp.float32
    ).astype(jnp.bfloat16)
    parent_scaled = scale_rows(parent_rows, parent_inv_eig[0])
    lifted = regroup(schur_block, child_map[0])
    own_parent_map = lax.dynamic_index_in_dim(parent_map, leaf_index // 2, 0, keepdims=False)
    sibling_rows, sibling_scaled = partner((parent_rows, parent_scaled), "leaf", 0)
    sibling_lifted, sibling_basis = (
        partner(lifted, "leaf", 0),
        partner(own_basis.astype(jnp.float32), "leaf", 0).astype(own_basis.dtype),
    )
    condensed = lifted + sibling_lifted
    pair_rows = jnp.concatenate([parent_rows, sibling_rows], axis=1)
    pair_scaled = jnp.concatenate([parent_scaled, sibling_scaled], axis=1)
    condensed = condensed - outer_rows(
        lax.all_gather(pair_rows, "panel", axis=0, tiled=True), pair_scaled
    )
    pair_basis = jnp.where(
        child_side == 0,
        jnp.concatenate([own_basis, sibling_basis], axis=1),
        jnp.concatenate([sibling_basis, own_basis], axis=1),
    )
    mapped = regroup(condensed, own_parent_map)
    far_block, far_basis = (
        partner(mapped, "leaf", 1),
        partner(pair_basis.astype(jnp.float32), "leaf", 1).astype(pair_basis.dtype),
    )
    grand = (mapped + far_block).astype(jnp.bfloat16)
    whole_basis = jnp.where(
        parent_side == 0,
        jnp.concatenate([pair_basis, far_basis], axis=1),
        jnp.concatenate([far_basis, pair_basis], axis=1),
    )
    projected = jnp.einsum(
        "bq,bc->qc", basis_all, grand, preferred_element_type=jnp.float32
    ).astype(jnp.bfloat16)
    reduced = lax.psum_scatter(
        jnp.dot(projected, whole_basis, preferred_element_type=jnp.float32).astype(jnp.bfloat16),
        "panel",
        scatter_dimension=0,
        tiled=True,
    ).astype(jnp.float32)
    return reduced[None]


def solution(mesh):
    placed = (
        P("leaf", None, "panel"),
        P("leaf", "panel", None),
        P("leaf", None, None),
        P("leaf", None),
        P("leaf", None),
        P("leaf", "panel", None),
        P("leaf", None, None),
        P("leaf", None),
        P(),
        P("leaf", "panel", None),
    )
    return jax.shard_map(
        shards, mesh=mesh, in_specs=placed, out_specs=P("leaf", "panel", None), check_vma=False
    )
```

profile of v0, /device:TPU:56, one launch (start us, length us, event | category | flops | bytes accessed | tf_op | source)
XLA Modules:
  0.0 337.6 jit_solution(17578813165512842508)
XLA Ops:
  6.6 1.5 copy-done
  8.1 2.1 fusion.4
  10.4 1.7 multiply_convert_fusion.2
  12.1 4.3 %collective-permute-start.1 = (bf16[128,256]{1,0:T(8,128)(2,1)S(1)}, bf16[128,256]{1,0:T(8,128)(2,1)S(1)}, u32[]{:S(2)}, u32[]{:S(2)}) collective-permute-start(bf16[128,256]{1,0:T(8,128)(2,1)S(1)} %get-tuple-element.9), channel_id=1, source_target_pairs={{0,32},{32,0},{64,96},{96,64},{128,160},{160,128},{192,224},{224,1... | collective-permute-start | bytes 196616 | tf_op jit(solution)/shard_map/ppermute | solution.py:10
  16.4 2.2 collective-permute-done.1
  19.4 61.4 %all-gather.5.cloned.1.call-done = bf16[4096,512]{1,0:T(8,128)(2,1)} async-done(((bf16[128,512]{1,0:T(8,128)(2,1)}), bf16[4096,512]{1,0:T(8,128)(2,1)}) %all-gather.5.cloned.1.call-update) | async-done | bytes 4194320 | tf_op jit(solution)/shard_map/all_gather | solution.py:52
  80.8 4.8 %convolution_subtract_fusion = f32[4096,128]{1,0:T(8,128)} fusion(bf16[4096,512]{1,0:T(8,128)(2,1)} %all-gather.5.cloned.1.call-done, bf16[1,4096,128]{2,1,0:T(8,128)(2,1)S(1)} %copy-done.1, bf16[128,512]{1,0:T(8,128)(2,1)S(1)} %copy-done.2, f32[512]{0:T(512)S(1)} %bitcast.53), kind=kOutput, calls=%fused_computation.2 | convolution fusion | flops 538116096 | bytes 7473152 | tf_op jit(solution)/shard_map/rm,cm->rc/dot_general | solution.py:24
  85.7 3.6 %gather_fusion = f32[32,128,128]{2,1,0:T(8,128)} fusion(f32[32,128,128]{2,1,0:T(8,128)} %bitcast.50, s32[1024]{0:T(1024)S(1)} %pad_clamp_fusion.1), kind=kCustom, calls=%fused_computation.clone | custom fusion | bytes 4194432 | tf_op jit(solution)/shard_map/jit(_take)/gather | solution.py:16
  89.3 3.2 broadcast_select_fusion.1
  92.4 2.9 collective-permute-start
  95.4 3.0 collective-permute-start.2
  98.4 0.7 compare_and_fusion
  99.1 65.7 %collective-permute-done.2 = bf16[128,256]{1,0:T(8,128)(2,1)S(1)} collective-permute-done((bf16[128,256]{1,0:T(8,128)(2,1)S(1)}, bf16[128,256]{1,0:T(8,128)(2,1)S(1)}, u32[]{:S(2)}, u32[]{:S(2)}) %collective-permute-start.2) | collective-permute-done | bytes 65568 | tf_op jit(solution)/shard_map/ppermute | solution.py:10
  164.8 6.1 %add_subtract_fusion = f32[4096,128]{1,0:T(8,128)} fusion(f32[4096,128]{1,0:T(8,128)} %bitcast.7, f32[4096,128]{1,0:T(8,128)} %collective-permute-done, bf16[4096,512]{1,0:T(8,128)(2,1)} %all-gather.7.cloned.1.call-done, bf16[128,256]{1,0:T(8,128)(2,1)S(1)} %collective-permute-done.2, bf16[128,256]{1,0:T(8,128)(2,1)S(1)} %get-tuple-element.8), kind=kOutput, calls=%fused_computation.8 | convolution fusion | flops 538181632 | bytes 10616832 | tf_op jit(solution)/shard_map/rm,cm->rc/dot_general | solution.py:24
  170.9 3.6 %gather_fusion.1 = f32[32,128,128]{2,1,0:T(8,128)} fusion(f32[32,128,128]{2,1,0:T(8,128)} %bitcast.49, s32[1024]{0:T(1024)S(1)} %pad_clamp_fusion), kind=kCustom, calls=%fused_computation.1.clone | custom fusion | bytes 4194432 | tf_op jit(solution)/shard_map/jit(_take)/gather | solution.py:16
  174.5 3.1 broadcast_select_fusion
  177.6 3.3 collective-permute-start.3
  181.0 2.9 collective-permute-start.4
  183.9 3.5 %collective-permute-done.4 = bf16[128,256]{1,0:T(8,128)(2,1)S(1)} collective-permute-done((bf16[128,256]{1,0:T(8,128)(2,1)S(1)}, bf16[128,256]{1,0:T(8,128)(2,1)S(1)}, u32[]{:S(2)}, u32[]{:S(2)}) %collective-permute-start.4) | collective-permute-done | bytes 65568 | tf_op jit(solution)/shard_map/ppermute | solution.py:10
  187.4 2.3 collective-permute-start.5
  189.7 39.8 %collective-permute-done.5 = bf16[128,512]{1,0:T(8,128)(2,1)S(1)} collective-permute-done((bf16[128,512]{1,0:T(8,128)(2,1)S(1)}, bf16[128,512]{1,0:T(8,128)(2,1)S(1)}, u32[]{:S(2)}, u32[]{:S(2)}) %collective-permute-start.5) | collective-permute-done | bytes 131104 | tf_op jit(solution)/shard_map/ppermute | solution.py:10
  229.6 4.7 %convolution_convert_fusion = bf16[256,1024]{1,0:T(8,128)(2,1)} fusion(bf16[1,4096,256]{2,1,0:T(8,128)(2,1)} %all-gather.9.cloned.1.call-done, f32[4096,128]{1,0:T(8,128)} %bitcast.12, f32[4096,128]{1,0:T(8,128)} %collective-permute-done.3, bf16[128,512]{1,0:T(8,128)(2,1)S(1)} %collective-permute-done.5, bf16[128,512]{1,0:T(8,128)(2,1)S(1)} %maximum_select_fusion.2, ...), kind=kOutput, calls=%fused_computation.9 | convolution fusion | flops 338067456 | bytes 7077889 | tf_op jit(solution)/shard_map/dot_general | solution.py:93
  234.3 95.4 %reduce-scatter.2.cloned.1.call-done = bf16[8,1024]{1,0:T(8,128)(2,1)} async-done(((bf16[256,1024]{1,0:T(8,128)(2,1)}), bf16[8,1024]{1,0:T(8,128)(2,1)}) %reduce-scatter.2.cloned.1.call-update) | async-done | bytes 16400 | tf_op jit(solution)/shard_map/reduce_scatter | solution.py:92
  329.7 1.3 bitcast_convert_fusion
  (31 shorter events, 1.0 us)
Async XLA Ops:
  6.5 1.6 copy-start
  6.5 3.8 %copy-start.5 = (f32[1,256]{1,0:T(1,128)S(1)}, f32[1,256]{1,0:T(1,128)}, u32[]{:S(2)}) copy-start(f32[1,256]{1,0:T(1,128)} %param.19) | copy-start | bytes 3076
  6.5 12.8 %copy-start.6 = (s32[1,32]{1,0:T(1,128)S(1)}, s32[1,32]{1,0:T(1,128)}, u32[]{:S(2)}) copy-start(s32[1,32]{1,0:T(1,128)} %param.16) | copy-start | bytes 388
  6.5 74.3 %copy-start.1 = (bf16[1,4096,128]{2,1,0:T(8,128)(2,1)S(1)}, bf16[1,4096,128]{2,1,0:T(8,128)(2,1)}, u32[]{:S(2)}) copy-start(bf16[1,4096,128]{2,1,0:T(8,128)(2,1)} %param.12) | copy-start | bytes 3145732
  6.5 74.3 %copy-start.4 = (f32[1,512]{1,0:T(1,128)S(1)}, f32[1,512]{1,0:T(1,128)}, u32[]{:S(2)}) copy-start(f32[1,512]{1,0:T(1,128)} %param.15) | copy-start | bytes 6148
  6.5 74.3 %all-gather.5.cloned.1.call-start = ((), (), s32[]{:S(2)}) async-start(), calls=%async_computation.1 | async-start | bytes 4325376 | tf_op jit(solution)/shard_map/all_gather | solution.py:52
  10.3 70.5 %copy-start.2 = (bf16[128,512]{1,0:T(8,128)(2,1)S(1)}, bf16[128,512]{1,0:T(8,128)(2,1)}, u32[]{:S(2)}) copy-start(bf16[128,512]{1,0:T(8,128)(2,1)} %fusion.4) | copy-start | bytes 393220
  10.3 154.5 %all-gather.7.cloned.1.call-start = ((), (), s32[]{:S(2)}) async-start(), calls=%async_computation.2 | async-start | bytes 4325376 | tf_op jit(solution)/shard_map/all_gather | solution.py:71
  12.1 6.5 %collective-permute-start.1 = (bf16[128,256]{1,0:T(8,128)(2,1)S(1)}, bf16[128,256]{1,0:T(8,128)(2,1)S(1)}, u32[]{:S(2)}, u32[]{:S(2)}) collective-permute-start(bf16[128,256]{1,0:T(8,128)(2,1)S(1)} %get-tuple-element.9), channel_id=1, source_target_pairs={{0,32},{32,0},{64,96},{96,64},{128,160},{160,128},{192,224},{224,1... | collective-permute-start | bytes 196616 | tf_op jit(solution)/shard_map/ppermute | solution.py:10
  19.3 210.3 %all-gather.9.cloned.1.call-start = ((), (), s32[]{:S(2)}) async-start(), calls=%async_computation.4 | async-start | bytes 2162688 | tf_op jit(solution)/shard_map/all_gather | solution.py:54
  92.4 72.4 %collective-permute-start = (f32[4096,128]{1,0:T(8,128)}, f32[4096,128]{1,0:T(8,128)}, u32[]{:S(2)}, u32[]{:S(2)}) collective-permute-start(f32[4096,128]{1,0:T(8,128)} %bitcast.7), channel_id=1, source_target_pairs={{0,32},{32,0},{64,96},{96,64},{128,160},{160,128},{192,224},{224,1... | collective-permute-start | bytes 6291464 | tf_op jit(solution)/shard_map/ppermute | solution.py:10
  95.3 234.4 %reduce-scatter.2.cloned.1.call-start = ((), (), s32[]{:S(2)}) async-start(), calls=%async_computation.3 | async-start | bytes 540672 | tf_op jit(solution)/shard_map/reduce_scatter | solution.py:92
  95.4 69.4 %collective-permute-start.2 = (bf16[128,256]{1,0:T(8,128)(2,1)S(1)}, bf16[128,256]{1,0:T(8,128)(2,1)S(1)}, u32[]{:S(2)}, u32[]{:S(2)}) collective-permute-start(bf16[128,256]{1,0:T(8,128)(2,1)S(1)} %get-tuple-element.8), channel_id=1, source_target_pairs={{0,32},{32,0},{64,96},{96,64},{128,160},{160,128},{192,224},{224,1... | collective-permute-start | bytes 196616 | tf_op jit(solution)/shard_map/ppermute | solution.py:10
  174.5 6.5 %copy-start.3 = (bf16[1,128,256]{2,1,0:T(8,128)(2,1)S(1)}, bf16[1,128,256]{2,1,0:T(8,128)(2,1)}, u32[]{:S(2)}) copy-start(bf16[1,128,256]{2,1,0:T(8,128)(2,1)} %param.21) | copy-start | bytes 196612
  177.6 51.9 %collective-permute-start.3 = (f32[4096,128]{1,0:T(8,128)}, f32[4096,128]{1,0:T(8,128)}, u32[]{:S(2)}, u32[]{:S(2)}) collective-permute-start(f32[4096,128]{1,0:T(8,128)} %bitcast.12), channel_id=1, source_target_pairs={{0,64},{32,96},{64,0},{96,32},{128,192},{160,224},{192,128},{224,1... | collective-permute-start | bytes 6291464 | tf_op jit(solution)/shard_map/ppermute | solution.py:10
  181.0 6.4 %collective-permute-start.4 = (bf16[128,256]{1,0:T(8,128)(2,1)S(1)}, bf16[128,256]{1,0:T(8,128)(2,1)S(1)}, u32[]{:S(2)}, u32[]{:S(2)}) collective-permute-start(bf16[128,256]{1,0:T(8,128)(2,1)S(1)} %bitcast.51), channel_id=1, source_target_pairs={{0,32},{32,0},{64,96},{96,64},{128,160},{160,128},{192,224},{224,1... | collective-permute-start | bytes 196616 | tf_op jit(solution)/shard_map/ppermute | solution.py:10
  187.4 42.2 %collective-permute-start.5 = (bf16[128,512]{1,0:T(8,128)(2,1)S(1)}, bf16[128,512]{1,0:T(8,128)(2,1)S(1)}, u32[]{:S(2)}, u32[]{:S(2)}) collective-permute-start(bf16[128,512]{1,0:T(8,128)(2,1)S(1)} %maximum_select_fusion.2), channel_id=1, source_target_pairs={{0,64},{32,96},{64,0},{96,32},{128,192},{160,224},{192,128},{224,1... | collective-permute-start | bytes 393224 | tf_op jit(solution)/shard_map/ppermute | solution.py:10
Sparse Core Ops, SparseCore 0:
  10.5 70.2 all-gather.4
  84.0 73.8 all-gather.6
  160.9 57.5 all-gather.8
  234.4 95.2 reduce-scatter.1
where the time goes:
time: 339 us; the launch traced here: 338 us
  waiting for transfers between devices  268 us (79%)
  matrix products  19.5 us (6%)
  starting transfers between devices  18.8 us (6%)
  between operations  13.3 us (4%)
  other arithmetic  9.05 us (3%)
  local copies, waits for them, and re-layouts  8.76 us (3%)
    ppermute x6, waiting for transfers between devices, partner(): return lax.ppermute(value, axis, pairs)  111 us
    reduce_scatter x1, waiting for transfers between devices, shards(): lax.psum_scatter(jnp.dot(projected, whole_basis, preferred_element_type=j...  95.4 us
    all_gather x1, waiting for transfers between devices, shards(): lax.all_gather(coupling_rows, 'panel', axis=0, tiled=True)  61.4 us
    ppermute x6, starting transfers between devices, partner(): return lax.ppermute(value, axis, pairs)  18.7 us
    dot_general x2, matrix products, outer_rows(): jnp.einsum('rm,cm->rc', left_rows, right_rows, preferred_element_type=jnp...  10.9 us
    gather x2, local copies, waits for them, and re-layouts, regroup(): return jnp.take(stacked, panel_index, axis=0).reshape(matrix.shape)  7.2 us
  transfers between devices with their start and end apart: 10, of which 6 were waited for; matrix products, arithmetic and copies ran while one was open for 8% of the time, Pallas kernels for 0%

commit v1 on v0

v1 whole, which is shorter than its diff:
```python
import jax
import jax.numpy as jnp
from jax import lax
from jax.sharding import Mesh
from jax.sharding import PartitionSpec as P

LEAF = ("b", "a")
PANEL = ("z", "x", "c")
GROUP = LEAF + PANEL
F32 = jnp.float32
BF16 = jnp.bfloat16


def exchange(value, axis):
    return lax.all_to_all(value, axis, 0, 0, tiled=True)


def spread(value, axis, count):
    return exchange(jnp.broadcast_to(value[None], (count,) + value.shape), axis)


def shards(
    child_stiff,
    child_bound,
    child_modes,
    child_inv_eig,
    child_map,
    parent_bound,
    parent_modes,
    parent_inv_eig,
    parent_map,
    interface_basis,
):
    panel = lax.axis_index(PANEL)
    core = lax.axis_index("c")
    grand_index = lax.axis_index("g")
    own_basis = interface_basis[0]
    width = own_basis.shape[1]
    pair_maps = lax.dynamic_slice_in_dim(parent_map, 2 * grand_index, 2, 0)
    leaf_maps = jnp.repeat(pair_maps, 2, axis=0)

    def coupling(modes, bound):
        return lax.dot_general(
            modes, bound, (((0,), (1,)), ((), ())), preferred_element_type=F32
        ).astype(BF16)

    child_t = coupling(child_modes[0], child_bound[0]).reshape(32, 16, 128)
    parent_t = coupling(parent_modes[0], parent_bound[0]).reshape(32, 8, 128)
    modes_t = jnp.concatenate([child_t, parent_t], axis=1)
    columns = exchange(jnp.broadcast_to(modes_t[None], (4, 32, 24, 128)).reshape(128, 24, 128), GROUP)
    columns = columns.reshape(4, 32, 24, 128)

    basis = spread(own_basis, "z", 4).reshape(4, 128, width)
    basis = spread(basis, "x", 4).reshape(4, 4, 128, width)
    other = lax.ppermute(basis, "c", [(0, 1), (1, 0)])
    both = jnp.where(core == 0, jnp.stack([basis, other]), jnp.stack([other, basis]))
    basis_all = both.transpose(2, 1, 0, 3, 4).reshape(32, 128, width)

    eig = jnp.concatenate([child_inv_eig[0], parent_inv_eig[0]]).reshape(3, width)
    eig_hi = eig.astype(BF16)
    eig_lo = (eig - eig_hi.astype(F32)).astype(BF16)
    map_row = jnp.pad(child_map.astype(BF16), ((0, 0), (0, width - child_map.shape[1])))
    extra = jnp.concatenate([eig_hi, eig_lo, map_row, jnp.zeros((9, width), BF16)], axis=0)
    quad = spread(jnp.concatenate([own_basis, extra], axis=0), LEAF, 4).reshape(4, 144, width)
    panel_basis = quad[:, :128]
    eigs = (quad[:, 128:131].astype(F32) + quad[:, 131:134].astype(F32)).reshape(4, 768)
    eigs = jnp.concatenate(
        [
            lax.dynamic_slice_in_dim(eigs, 16 * panel, 16, 1),
            lax.dynamic_slice_in_dim(eigs, 512 + 8 * panel, 8, 1),
        ],
        axis=1,
    )
    child_maps = quad[:, 134, :32].astype(jnp.int32)

    own_pmap = lax.dynamic_index_in_dim(pair_maps, lax.axis_index("b"), 0, keepdims=False)
    rows = child_map[0].at[own_pmap].get(mode="promise_in_bounds")
    stiff = child_stiff[0].reshape(32, 128, 128).at[rows].get(mode="promise_in_bounds")
    parts = exchange(stiff.reshape(4, 1024, 128), LEAF)
    summed = jnp.sum(parts.astype(F32), axis=0).astype(BF16)
    assembled = spread(summed, LEAF, 4).reshape(32, 128, 128)

    right = jnp.einsum("ljmr,jrc->lmc", columns, basis_all, preferred_element_type=F32)
    right = (-eigs[:, :, None] * right).astype(BF16).reshape(96, width)
    right = spread(right, LEAF, 4).reshape(4, 96, width)

    child_rows = jnp.take_along_axis(child_maps, leaf_maps, axis=1)
    take = jax.vmap(lambda part, index: part.at[index].get(mode="promise_in_bounds"))
    regrouped = jnp.concatenate(
        [take(columns[:, :, :16], child_rows), take(columns[:, :, 16:], leaf_maps)], axis=2
    )
    left = jnp.einsum("limr,irc->lmc", regrouped, basis_all, preferred_element_type=F32)
    left = left.astype(BF16).reshape(96, width)
    left_stiff = jnp.einsum("irk,irc->kc", assembled, basis_all, preferred_element_type=F32).astype(BF16)

    part = jnp.einsum("kc,qkd->cqd", left_stiff, panel_basis, preferred_element_type=F32)
    part = part + jnp.einsum("kc,qkd->cqd", left, right, preferred_element_type=F32)
    part = part.reshape(16, 2, 8, 1024)
    mine = lax.dynamic_index_in_dim(part, core, 1, keepdims=False)
    theirs = lax.dynamic_index_in_dim(part, 1 - core, 1, keepdims=False).astype(BF16)
    mine = mine + lax.ppermute(theirs, "c", [(0, 1), (1, 0)]).astype(F32)
    pieces = exchange(mine.astype(BF16), ("z", "x"))
    return jnp.sum(pieces.astype(F32), axis=0)[None]


def solution(mesh):
    names = ("g", "b", "a", "z", "x", "c")
    split = Mesh(mesh.devices.reshape(4, 2, 2, 4, 4, 2), names)
    leaf = ("g", "b", "a")
    placed = (
        P(leaf, None, PANEL),
        P(leaf, PANEL, None),
        P(leaf, None, None),
        P(leaf, None),
        P(leaf, None),
        P(leaf, PANEL, None),
        P(leaf, None, None),
        P(leaf, None),
        P(),
        P(leaf, PANEL, None),
    )
    return jax.shard_map(
        shards, mesh=split, in_specs=placed, out_specs=P(leaf, PANEL, None), check_vma=False
    )
```

time: 339 us -> 158 us (0.47)
  waiting for transfers between devices: 268 us -> 42.4 us
  blocking collectives: 0 us -> 25.2 us
  local copies, waits for them, and re-layouts: 8.76 us -> 30.1 us
  starting transfers between devices: 18.8 us -> 39.2 us
  between operations: 13.3 us -> 0.25 us
  matrix products: 19.5 us -> 9.91 us
    ppermute x6 -> x2, waiting for transfers between devices: 111 us -> 1.5 us  [the longest x1 1.5 us: shards(): mine = mine + lax.ppermute(theirs, 'c', [(0, 1), (1, 0)]).astype(F32)]
    reduce_scatter x1 -> x0, waiting for transfers between devices: 95.4 us -> none  [shards(): lax.psum_scatter(jnp.dot(projected, whole_basis, preferred_element_type=j...]
    all_gather x3 -> x0, waiting for transfers between devices: 61.4 us -> none  [the longest x1 61.4 us: shards(): lax.all_gather(coupling_rows, 'panel', axis=0, tiled=True)]
    all_to_all x0 -> x6, waiting for transfers between devices: none -> 40.9 us  [exchange(): return lax.all_to_all(value, axis, 0, 0, tiled=True)]
    all_to_all x0 -> x6, starting transfers between devices: none -> 35.3 us  [exchange(): return lax.all_to_all(value, axis, 0, 0, tiled=True)]
    all_to_all x0 -> x2, blocking collectives: none -> 25.2 us  [exchange(): return lax.all_to_all(value, axis, 0, 0, tiled=True)]
    ppermute x6 -> x2, starting transfers between devices: 18.7 us -> 3.98 us  [the longest x1 2.06 us: shards(): other = lax.ppermute(basis, 'c', [(0, 1), (1, 0)])]
    dot_general x5 -> x6, matrix products: 19.5 us -> 9.91 us  [the longest x2 3.63 us: coupling(): lax.dot_general(modes, bound, (((0,), (1,)), ((), ())), preferred_element...]
  transfers between devices with their start and end apart: 10 -> 8, of which waited for: 6 -> 6; matrix products, arithmetic and copies ran while one was open for 8% -> 23% of each run, Pallas kernels for 0% -> 0%
where the time goes in v1:
time: 158 us; the launch traced here: 156 us
  waiting for transfers between devices  42.4 us (27%)
  starting transfers between devices  39.2 us (25%)
  local copies, waits for them, and re-layouts  30.1 us (19%)
  blocking collectives  25.2 us (16%)
  matrix products  9.91 us (6%)
  other arithmetic  8.71 us (6%)
    all_to_all x6, waiting for transfers between devices, exchange(): return lax.all_to_all(value, axis, 0, 0, tiled=True)  40.9 us
    all_to_all x6, starting transfers between devices, exchange(): return lax.all_to_all(value, axis, 0, 0, tiled=True)  35.3 us
    all_to_all x2, blocking collectives, exchange(): return lax.all_to_all(value, axis, 0, 0, tiled=True)  25.2 us
    broadcast_in_dim x5, local copies, waits for them, and re-layouts, spread(): return exchange(jnp.broadcast_to(value[None], (count,) + value.shape), axis)  5.58 us
    gather x3, local copies, waits for them, and re-layouts, shards(): part.at[index].get(mode='promise_in_bounds')  5.36 us
    dot_general x2, matrix products, coupling(): lax.dot_general(modes, bound, (((0,), (1,)), ((), ())), preferred_element...  3.63 us
  transfers between devices with their start and end apart: 8, of which 6 were waited for; matrix products, arithmetic and copies ran while one was open for 23% of the time, Pallas kernels for 0%

profile of v1, /device:TPU:56, one launch (start us, length us, event | category | flops | bytes accessed | tf_op | source)
XLA Modules:
  0.0 155.8 jit_solution(10700872354721837278)
XLA Ops:
  1.7 10.3 %all-to-all-start.2 = ((bf16[4,128,256]{2,1,0:T(8,128)(2,1)}), bf16[4,128,256]{2,1,0:T(8,128)(2,1)S(1)}, u32[]{:S(2)}, u32[]{:S(2)}) async-start(bf16[4,128,256]{2,1,0:T(8,128)(2,1)} %broadcast_in_dim.27), calls=%async_computation.2 | async-start | bytes 524288 | tf_op jit(solution)/shard_map/all_to_all | solution.py:15
  14.4 8.8 %all-to-all-done.2 = bf16[4,128,256]{2,1,0:T(8,128)(2,1)S(1)} async-done(((bf16[4,128,256]{2,1,0:T(8,128)(2,1)}), bf16[4,128,256]{2,1,0:T(8,128)(2,1)S(1)}, u32[]{:S(2)}, u32[]{:S(2)}) %all-to-all-start.2) | async-done | bytes 262176 | tf_op jit(solution)/shard_map/all_to_all | solution.py:15
  23.2 8.5 %all_to_all.40 = bf16[4,144,256]{2,1,0:T(8,128)(2,1)S(1)} all-to-all(bf16[4,144,256]{2,1,0:T(8,128)(2,1)S(1)} %broadcast_in_dim.31), channel_id=1, replica_groups=mesh['g'=4,'b'=2,'a'=2,'z'=4,'x'=4,'c'=2] {'b','a'}, dimensions={0} | all-to-all | bytes 589824 | tf_op jit(solution)/shard_map/all_to_all | solution.py:15
  32.8 4.3 %all-to-all-start.3 = ((bf16[4,4,128,256]{3,2,1,0:T(8,128)(2,1)}), bf16[4,4,128,256]{3,2,1,0:T(8,128)(2,1)S(1)}, u32[]{:S(2)}, u32[]{:S(2)}) async-start(bf16[4,4,128,256]{3,2,1,0:T(8,128)(2,1)} %broadcast_in_dim.29), calls=%async_computation.3 | async-start | bytes 2097152 | tf_op jit(solution)/shard_map/all_to_all | solution.py:15
  38.5 2.9 %gather_fusion.1 = bf16[32,128,128]{2,1,0:T(8,128)(2,1)} fusion(bf16[32,128,128]{2,1,0:T(8,128)(2,1)} %bitcast.107, s32[1024]{0:T(1024)S(1)} %pad_clamp_fusion), kind=kCustom, calls=%fused_computation.1 | custom fusion | bytes 2097280 | tf_op jit(solution)/shard_map/gather | solution.py:78
  41.4 8.7 %all-to-all-done.3 = bf16[4,4,128,256]{3,2,1,0:T(8,128)(2,1)S(1)} async-done(((bf16[4,4,128,256]{3,2,1,0:T(8,128)(2,1)}), bf16[4,4,128,256]{3,2,1,0:T(8,128)(2,1)S(1)}, u32[]{:S(2)}, u32[]{:S(2)}) %all-to-all-start.3) | async-done | bytes 1048608 | tf_op jit(solution)/shard_map/all_to_all | solution.py:15
  51.1 4.6 %all-to-all-start = ((bf16[4,1024,128]{2,1,0:T(8,128)(2,1)}), bf16[4,1024,128]{2,1,0:T(8,128)(2,1)S(1)}, u32[]{:S(2)}, u32[]{:S(2)}) async-start(bf16[4,1024,128]{2,1,0:T(8,128)(2,1)} %bitcast.6), calls=%async_computation | async-start | bytes 2097152 | tf_op jit(solution)/shard_map/all_to_all | solution.py:15
  55.6 1.8 %fusion.9 = bf16[32,8,128]{2,1,0:T(8,128)(2,1)S(1)} fusion(bf16[1,2048,256]{2,1,0:T(8,128)(2,1)} %param.16, bf16[1,128,2048]{2,1,0:T(8,128)(2,1)} %param.15), kind=kOutput, calls=%fused_computation.18 | convolution fusion | flops 134250496 | bytes 1638400 | tf_op jit(solution)/shard_map/dot_general | solution.py:43
  60.0 5.0 %all-to-all-done = bf16[4,1024,128]{2,1,0:T(8,128)(2,1)S(1)} async-done(((bf16[4,1024,128]{2,1,0:T(8,128)(2,1)}), bf16[4,1024,128]{2,1,0:T(8,128)(2,1)S(1)}, u32[]{:S(2)}, u32[]{:S(2)}) %all-to-all-start) | async-done | bytes 1048608 | tf_op jit(solution)/shard_map/all_to_all | solution.py:15
  65.0 2.1 %broadcast_in_dim.62 = bf16[4,32,24,128]{3,2,1,0:T(8,128)(2,1)} broadcast(bf16[32,24,128]{2,1,0:T(8,128)(2,1)} %pad_maximum_fusion), dimensions={1,2,3} | broadcast | bytes 983040 | tf_op jit(solution)/shard_map/broadcast_in_dim | solution.py:50
  67.2 7.7 %all-to-all-start.5 = ((bf16[128,24,128]{2,1,0:T(8,128)(2,1)}), bf16[128,24,128]{2,1,0:T(8,128)(2,1)}, u32[]{:S(2)}, u32[]{:S(2)}) async-start(bf16[128,24,128]{2,1,0:T(8,128)(2,1)} %bitcast.106), calls=%async_computation.5 | async-start | bytes 1572864 | tf_op jit(solution)/shard_map/all_to_all | solution.py:15
  76.9 2.1 %collective-permute-start = (bf16[4,4,128,256]{3,2,0,1:T(8,128)(2,1)S(1)}, bf16[4,4,128,256]{3,2,0,1:T(8,128)(2,1)}, u32[]{:S(2)}, u32[]{:S(2)}) collective-permute-start(bf16[4,4,128,256]{3,2,0,1:T(8,128)(2,1)S(1)} %copy.27), channel_id=1, source_target_pairs={{0,1},{1,0},{2,3},{3,2},{4,5},{5,4},{6,7},{7,6},{8,9},{9,8},{10,11... | collective-permute-start | bytes 3145736 | tf_op jit(solution)/shard_map/ppermute | solution.py:55
  79.1 2.2 %reduce_sum.21 = bf16[1024,128]{1,0:T(8,128)(2,1)} reduce(bf16[4,1024,128]{2,1,0:T(8,128)(2,1)} %copy-done.3, bf16[]{:T(256)} %constant.73.clone.1), dimensions={0}, to_apply=%region_0.1 | reduce | flops 393216 | bytes 1310722 | tf_op jit(solution)/shard_map/reduce_sum | solution.py:80
  81.2 16.9 %all-to-all-done.5 = bf16[128,24,128]{2,1,0:T(8,128)(2,1)} async-done(((bf16[128,24,128]{2,1,0:T(8,128)(2,1)}), bf16[128,24,128]{2,1,0:T(8,128)(2,1)}, u32[]{:S(2)}, u32[]{:S(2)}) %all-to-all-start.5) | async-done | bytes 786464 | tf_op jit(solution)/shard_map/all_to_all | solution.py:15
  98.2 2.1 %broadcast_in_dim.25 = bf16[4,1024,128]{2,1,0:T(8,128)(2,1)} broadcast(bf16[1024,128]{1,0:T(8,128)(2,1)} %reduce_sum.21), dimensions={1,2} | broadcast | bytes 1310720 | tf_op jit(solution)/shard_map/broadcast_in_dim | solution.py:19
  100.3 4.3 %all-to-all-start.1 = ((bf16[4,1024,128]{2,1,0:T(8,128)(2,1)}), bf16[4,1024,128]{2,1,0:T(8,128)(2,1)}, u32[]{:S(2)}, u32[]{:S(2)}) async-start(bf16[4,1024,128]{2,1,0:T(8,128)(2,1)} %broadcast_in_dim.25), calls=%async_computation.1 | async-start | bytes 2097152 | tf_op jit(solution)/shard_map/all_to_all | solution.py:15
  106.5 1.9 %slice.35 = bf16[4,32,16,128]{3,2,1,0:T(8,128)(2,1)} slice(bf16[4,32,24,128]{3,2,1,0:T(8,128)(2,1)} %bitcast.24), slice={[0:4], [0:32], [0:16], [0:128]} | slice | bytes 1048576 | tf_op jit(solution)/shard_map/slice | solution.py:90
  110.1 2.5 %gather_fusion.4 = bf16[128,8,128]{2,1,0:T(8,128)(2,1)} fusion(bf16[4,32,8,128]{3,2,1,0:T(8,128)(2,1)} %slice.37, s32[128]{0:T(128)S(1)} %reshape.201), kind=kCustom, calls=%fused_computation.4 | custom fusion | bytes 525312 | tf_op jit(solution)/shard_map/vmap()/gather | solution.py:88
  112.6 2.7 %gather_fusion.3 = bf16[128,16,128]{2,1,0:T(8,128)(2,1)} fusion(bf16[4,32,16,128]{3,2,1,0:T(8,128)(2,1)} %slice.35, s32[128]{0:T(128)S(1)} %reshape.207), kind=kCustom, calls=%fused_computation.3 | custom fusion | bytes 1049600 | tf_op jit(solution)/shard_map/vmap()/gather | solution.py:88
  115.3 1.9 %maximum_select_fusion = bf16[2,4,4,128,256]{4,3,0,1,2:T(8,128)(2,1)S(1)} fusion(bf16[1,4,4,128,256]{4,3,0,1,2:T(8,128)(2,1)} %bitcast.10, bf16[1,4,4,128,256]{4,3,0,1,2:T(8,128)(2,1)S(1)} %bitcast.105, pred[]{:T(512)S(6)} %eq.3), kind=kLoop, calls=%fused_computation.5 | loop fusion | flops 3145728 | bytes 4194305 | tf_op jit(solution)/shard_map/jit(_where)/select_n | solution.py:56
  120.9 4.2 %all-to-all-start.6 = ((bf16[4,96,256]{2,1,0:T(8,128)(2,1)}), bf16[4,96,256]{2,1,0:T(8,128)(2,1)}, u32[]{:S(2)}, u32[]{:S(2)}) async-start(bf16[4,96,256]{2,1,0:T(8,128)(2,1)} %broadcast_in_dim.66), calls=%async_computation.6 | async-start | bytes 393216 | tf_op jit(solution)/shard_map/all_to_all | solution.py:15
  125.0 2.9 %fusion.12 = f32[256,4,256]{2,0,1:T(8,128)S(1)} fusion(bf16[32,128,128]{2,1,0:T(8,128)(2,1)} %bitcast.7, bf16[32,128,256]{2,1,0:T(8,128)(2,1)} %bitcast.104, bf16[4,144,256]{2,1,0:T(8,128)(2,1)S(1)} %all_to_all.40), kind=kOutput, calls=%fused_computation.21 | convolution fusion | flops 335577088 | bytes 4456448 | tf_op jit(solution)/shard_map/kc,qkd->cqd/dot_general | solution.py:96
  133.9 1.9 %collective-permute-start.1 = (bf16[16,8,1024]{2,1,0:T(8,128)(2,1)S(1)}, bf16[16,8,1024]{2,1,0:T(8,128)(2,1)S(1)}, u32[]{:S(2)}, u32[]{:S(2)}) collective-permute-start(bf16[16,8,1024]{2,1,0:T(8,128)(2,1)S(1)} %fusion.19), channel_id=1, source_target_pairs={{0,1},{1,0},{2,3},{3,2},{4,5},{5,4},{6,7},{7,6},{8,9},{9,8},{10,11... | collective-permute-start | bytes 786440 | tf_op jit(solution)/shard_map/ppermute | solution.py:101
  138.5 16.7 %all_to_all.41 = bf16[16,8,1024]{2,1,0:T(8,128)(2,1)S(1)} all-to-all(bf16[16,8,1024]{2,1,0:T(8,128)(2,1)S(1)} %fusion.16), channel_id=1, replica_groups=mesh['g'=4,'b'=2,'a'=2,'z'=4,'x'=4,'c'=2] {'z','x'}, dimensions={0} | all-to-all | bytes 524288 | tf_op jit(solution)/shard_map/all_to_all | solution.py:15
  (60 shorter events, 28.6 us)
Async XLA Ops:
  0.0 57.5 %copy-start = (bf16[1,2048,512]{2,1,0:T(8,128)(2,1)S(1)}, bf16[1,2048,512]{2,1,0:T(8,128)(2,1)}, u32[]{:S(2)}) copy-start(bf16[1,2048,512]{2,1,0:T(8,128)(2,1)} %param.12) | copy-start | bytes 6291460
  1.7 21.5 %all-to-all-start.2 = ((bf16[4,128,256]{2,1,0:T(8,128)(2,1)}), bf16[4,128,256]{2,1,0:T(8,128)(2,1)S(1)}, u32[]{:S(2)}, u32[]{:S(2)}) async-start(bf16[4,128,256]{2,1,0:T(8,128)(2,1)} %broadcast_in_dim.27), calls=%async_computation.2 | async-start | bytes 524288 | tf_op jit(solution)/shard_map/all_to_all | solution.py:15
  23.2 14.6 %copy-start.1 = (s32[1,32]{1,0:T(1,128)S(1)}, s32[1,32]{1,0:T(1,128)}, u32[]{:S(2)}) copy-start(s32[1,32]{1,0:T(1,128)} %param.14) | copy-start | bytes 388
  32.8 17.3 %all-to-all-start.3 = ((bf16[4,4,128,256]{3,2,1,0:T(8,128)(2,1)}), bf16[4,4,128,256]{3,2,1,0:T(8,128)(2,1)S(1)}, u32[]{:S(2)}, u32[]{:S(2)}) async-start(bf16[4,4,128,256]{3,2,1,0:T(8,128)(2,1)} %broadcast_in_dim.29), calls=%async_computation.3 | async-start | bytes 2097152 | tf_op jit(solution)/shard_map/all_to_all | solution.py:15
  50.1 1.0 copy-start.4
  51.1 14.0 %all-to-all-start = ((bf16[4,1024,128]{2,1,0:T(8,128)(2,1)}), bf16[4,1024,128]{2,1,0:T(8,128)(2,1)S(1)}, u32[]{:S(2)}, u32[]{:S(2)}) async-start(bf16[4,1024,128]{2,1,0:T(8,128)(2,1)} %bitcast.6), calls=%async_computation | async-start | bytes 2097152 | tf_op jit(solution)/shard_map/all_to_all | solution.py:15
  65.0 9.8 %copy-start.3 = (bf16[4,1024,128]{2,1,0:T(8,128)(2,1)}, bf16[4,1024,128]{2,1,0:T(8,128)(2,1)S(1)}, u32[]{:S(2)}) copy-start(bf16[4,1024,128]{2,1,0:T(8,128)(2,1)S(1)} %all-to-all-done) | copy-start | bytes 3145732
  67.2 31.0 %all-to-all-start.5 = ((bf16[128,24,128]{2,1,0:T(8,128)(2,1)}), bf16[128,24,128]{2,1,0:T(8,128)(2,1)}, u32[]{:S(2)}, u32[]{:S(2)}) async-start(bf16[128,24,128]{2,1,0:T(8,128)(2,1)} %bitcast.106), calls=%async_computation.5 | async-start | bytes 1572864 | tf_op jit(solution)/shard_map/all_to_all | solution.py:15
  76.9 38.5 %collective-permute-start = (bf16[4,4,128,256]{3,2,0,1:T(8,128)(2,1)S(1)}, bf16[4,4,128,256]{3,2,0,1:T(8,128)(2,1)}, u32[]{:S(2)}, u32[]{:S(2)}) collective-permute-start(bf16[4,4,128,256]{3,2,0,1:T(8,128)(2,1)S(1)} %copy.27), channel_id=1, source_target_pairs={{0,1},{1,0},{2,3},{3,2},{4,5},{5,4},{6,7},{7,6},{8,9},{9,8},{10,11... | collective-permute-start | bytes 3145736 | tf_op jit(solution)/shard_map/ppermute | solution.py:55
  100.3 19.9 %all-to-all-start.1 = ((bf16[4,1024,128]{2,1,0:T(8,128)(2,1)}), bf16[4,1024,128]{2,1,0:T(8,128)(2,1)}, u32[]{:S(2)}, u32[]{:S(2)}) async-start(bf16[4,1024,128]{2,1,0:T(8,128)(2,1)} %broadcast_in_dim.25), calls=%async_computation.1 | async-start | bytes 2097152 | tf_op jit(solution)/shard_map/all_to_all | solution.py:15
  115.3 1.9 %copy-start.5 = (bf16[128,16,128]{2,1,0:T(8,128)(2,1)S(1)}, bf16[128,16,128]{2,1,0:T(8,128)(2,1)}, u32[]{:S(2)}) copy-start(bf16[128,16,128]{2,1,0:T(8,128)(2,1)} %gather_fusion.3) | copy-start | bytes 1572868
  115.3 1.9 %copy-start.6 = (bf16[128,8,128]{2,1,0:T(8,128)(2,1)S(1)}, bf16[128,8,128]{2,1,0:T(8,128)(2,1)}, u32[]{:S(2)}) copy-start(bf16[128,8,128]{2,1,0:T(8,128)(2,1)} %gather_fusion.4) | copy-start | bytes 786436
  117.2 1.3 copy-start.2
  120.9 8.5 %all-to-all-start.6 = ((bf16[4,96,256]{2,1,0:T(8,128)(2,1)}), bf16[4,96,256]{2,1,0:T(8,128)(2,1)}, u32[]{:S(2)}, u32[]{:S(2)}) async-start(bf16[4,96,256]{2,1,0:T(8,128)(2,1)} %broadcast_in_dim.66), calls=%async_computation.6 | async-start | bytes 393216 | tf_op jit(solution)/shard_map/all_to_all | solution.py:15
  133.9 3.4 %collective-permute-start.1 = (bf16[16,8,1024]{2,1,0:T(8,128)(2,1)S(1)}, bf16[16,8,1024]{2,1,0:T(8,128)(2,1)S(1)}, u32[]{:S(2)}, u32[]{:S(2)}) collective-permute-start(bf16[16,8,1024]{2,1,0:T(8,128)(2,1)S(1)} %fusion.19), channel_id=1, source_target_pairs={{0,1},{1,0},{2,3},{3,2},{4,5},{5,4},{6,7},{7,6},{8,9},{9,8},{10,11... | collective-permute-start | bytes 786440 | tf_op jit(solution)/shard_map/ppermute | solution.py:101

commit v2 on v1

v2 whole, which is shorter than its diff:
```python
import functools

import jax
import jax.numpy as jnp
from jax import lax
from jax.experimental import pallas as pl
from jax.experimental.pallas import tpu as pltpu
from jax.sharding import Mesh
from jax.sharding import PartitionSpec as P

PANEL = ("z", "x", "c")
GROUP = ("b", "a") + PANEL
F32 = jnp.float32
BF16 = jnp.bfloat16
VM = pl.BlockSpec(memory_space=pltpu.VMEM)
SM = pl.BlockSpec(memory_space=pltpu.SMEM)


def call(body, outs, specs, name, flops, *args):
    shapes = [jax.ShapeDtypeStruct(s, t) for s, t in outs]
    moved = sum(a.size * a.dtype.itemsize for a in args)
    return pl.pallas_call(
        body,
        out_shape=shapes,
        in_specs=specs,
        out_specs=[VM] * len(outs),
        compiler_params=pltpu.CompilerParams(vmem_limit_bytes=32 << 20),
        cost_estimate=pl.CostEstimate(flops=flops, bytes_accessed=moved, transcendentals=0),
        name=name,
    )(*args)


def dot(left, right):
    return jnp.dot(left, right, preferred_element_type=F32)


def coupling_body(cm_ref, cb_ref, ce_ref, pm_ref, pb_ref, pe_ref, out_ref, child_ref, parent_ref):
    step = pl.program_id(0)

    @pl.when(step == 0)
    def _():
        child_ref[...] = jnp.zeros_like(child_ref)
        parent_ref[...] = jnp.zeros_like(parent_ref)

    child_ref[...] += dot(cb_ref[...], cm_ref[...])
    parent_ref[...] += dot(pb_ref[...], pm_ref[...])

    @pl.when(step == pl.num_programs(0) - 1)
    def _():
        child = child_ref[...] * jnp.sqrt(ce_ref[...])
        parent = parent_ref[...] * jnp.sqrt(pe_ref[...])
        both = jnp.concatenate(
            [child.T.reshape(32, 16, 128), parent.T.reshape(32, 8, 128)], axis=1
        ).astype(BF16)
        for q in range(4):
            out_ref[q] = both


def couple(child_modes, child_bound, child_eig, parent_modes, parent_bound, parent_eig):
    steps = 4
    depth = child_modes.shape[0] // steps
    modes = lambda width: pl.BlockSpec((depth, width), lambda i: (i, 0))
    bound = pl.BlockSpec((128, depth), lambda i: (0, i))
    eig = lambda width: pl.BlockSpec((1, width), lambda i: (0, 0))
    return pl.pallas_call(
        coupling_body,
        grid=(steps,),
        out_shape=jax.ShapeDtypeStruct((4, 32, 24, 128), BF16),
        in_specs=[modes(512), bound, eig(512), modes(256), bound, eig(256)],
        out_specs=pl.BlockSpec((4, 32, 24, 128), lambda i: (0, 0, 0, 0)),
        scratch_shapes=[pltpu.VMEM((128, 512), F32), pltpu.VMEM((128, 256), F32)],
        compiler_params=pltpu.CompilerParams(vmem_limit_bytes=60 << 20),
        cost_estimate=pl.CostEstimate(flops=400_000_000, bytes_accessed=5_000_000, transcendentals=0),
        name="coupling",
    )(child_modes, child_bound, child_eig, parent_modes, parent_bound, parent_eig)


def join_body(a_ref, b_ref, c_ref, d_ref, out_ref):
    for k, ref in enumerate((a_ref, b_ref, c_ref, d_ref)):
        out_ref[512 * k : 512 * (k + 1), :] = ref[...]


def stiff_body(stiff_ref, cmap_ref, pmap_ref, row_ref, basis_ref, out_ref):
    def place(i, carry):
        row = cmap_ref[0, pmap_ref[0, i]]
        out_ref[pl.ds(pl.multiple_of(i * 128, 128), 128), :] = stiff_ref[
            pl.ds(pl.multiple_of(row * 128, 128), 128), :
        ]
        return carry

    lax.fori_loop(0, 32, place, 0)
    out_ref[4096:4224, :] = basis_ref[:, :128]
    out_ref[4224:4352, :] = basis_ref[:, 128:]
    row = jnp.concatenate([row_ref[...], jnp.zeros((1, 96), jnp.int32)], axis=1).astype(F32)
    out_ref[4352:4368, :] = jnp.broadcast_to(row, (16, 128)).astype(BF16)


def add_body(own_ref, got_ref, out_ref):
    def add(i, carry):
        at = pl.ds(pl.multiple_of(i * 512, 512), 512)
        out_ref[at, :] = (own_ref[at, :].astype(F32) + got_ref[at, :].astype(F32)).astype(BF16)
        return carry

    lax.fori_loop(0, 8, add, 0)
    out_ref[4096:4368, :] = own_ref[4096:, :]
    out_ref[4368:, :] = got_ref[4096:, :]


def block_index(pos_ref, half, k):
    return (k % 4) * 8 + (pos_ref[0] ^ (k // 4)) * 2 + (pos_ref[1] ^ half)


def right_body(pos_ref, col_ref, mine_ref, other_ref, out_ref):
    total = jnp.zeros((96, 256), F32)
    for half, ref in enumerate((mine_ref, other_ref)):
        for k in range(0, 16, 2):
            cols = [
                col_ref[:, block_index(pos_ref, half, k + s)].astype(F32).reshape(96, 128)
                for s in (0, 1)
            ]
            left = jnp.concatenate(cols, axis=1).astype(BF16)
            total = total + dot(left, ref[pl.ds(k * 128, 256), :])
    total = total.astype(BF16)
    for q in range(4):
        out_ref[q] = total


def left_body(pos_ref, cmaps_ref, pmaps_ref, col_ref, mine_ref, other_ref, own_ref, far_ref, out_ref):
    modes = jnp.zeros((96, 256), F32)
    stiff = jnp.zeros((128, 256), F32)
    q = pos_ref[2]
    for half, ref in enumerate((mine_ref, other_ref)):
        for k in range(0, 16, 2):
            pair, rows = [], []
            for s in (0, 1):
                i = block_index(pos_ref, half, k + s)
                for_leaf = []
                for leaf in range(4):
                    row = pmaps_ref[leaf // 2, i]
                    for_leaf.append(col_ref[leaf, cmaps_ref[leaf ^ q, row]].astype(F32)[:16])
                    for_leaf.append(col_ref[leaf, row].astype(F32)[16:])
                pair.append(jnp.concatenate(for_leaf, axis=0))
                at = pl.ds(pl.multiple_of(i * 128, 128), 128)
                rows.append((own_ref[at, :].astype(F32) + far_ref[at, :].astype(F32)).T)
            block = ref[pl.ds(k * 128, 256), :]
            modes = modes + dot(jnp.concatenate(pair, axis=1).astype(BF16), block)
            stiff = stiff + dot(jnp.concatenate(rows, axis=1).astype(BF16), block)
    out_ref[:128, :] = stiff
    out_ref[128:, :] = -modes


def final_body(pos_ref, left_ref, right_ref, w0_ref, w1_ref, mine_ref, theirs_ref, all_ref):
    left = left_ref[...].T.astype(BF16)
    q = pos_ref[2]
    for rel in range(4):
        at = q ^ rel
        w_ref = (w0_ref, w1_ref)[rel % 2]
        base = 272 * (rel // 2) + 4096
        basis = jnp.concatenate([w_ref[base : base + 128, :], w_ref[base + 128 : base + 256, :]], axis=1)
        stacked = jnp.concatenate([basis.astype(F32), right_ref[at].astype(F32)], axis=0).astype(BF16)
        all_ref[:, pl.ds(pl.multiple_of(at * 256, 256), 256)] = dot(left, stacked)
    c = pos_ref[1]
    mine, theirs = [], []
    for t in range(16):
        mine.append(all_ref[pl.ds(pl.multiple_of(16 * t + 8 * c, 8), 8), :])
        theirs.append(all_ref[pl.ds(pl.multiple_of(16 * t + 8 * (1 - c), 8), 8), :])
    mine_ref[...] = jnp.concatenate(mine, axis=0)
    theirs_ref[...] = jnp.concatenate(theirs, axis=0).astype(BF16)


def swap(value, axis, mask):
    size = lax.axis_size(axis)
    return lax.ppermute(value, axis, [(i, i ^ mask) for i in range(size)])


def exchange(value, axis):
    return lax.all_to_all(value, axis, 0, 0, tiled=True)


def shards(
    child_stiff,
    child_bound,
    child_modes,
    child_inv_eig,
    child_map,
    parent_bound,
    parent_modes,
    parent_inv_eig,
    parent_map,
    interface_basis,
):
    quad_place = 2 * lax.axis_index("b") + lax.axis_index("a")
    pos = jnp.stack([lax.axis_index("x"), lax.axis_index("c"), quad_place])
    own_basis = interface_basis[0]
    pair_maps = lax.dynamic_slice_in_dim(parent_map, 2 * lax.axis_index("g"), 2, 0)
    own_pmap = lax.dynamic_slice_in_dim(pair_maps, lax.axis_index("b"), 1, 0)

    modes_t = couple(
        child_modes[0], child_bound[0], child_inv_eig, parent_modes[0], parent_bound[0], parent_inv_eig
    )
    columns = exchange(modes_t.reshape(128, 24, 128), GROUP).reshape(4, 32, 24, 128)

    by_z = exchange(jnp.broadcast_to(own_basis[None], (4, 128, 256)), "z").reshape(512, 256)
    (mine,) = call(
        join_body, [((2048, 256), BF16)], [VM] * 4, "join", 1_000_000,
        by_z, *[swap(by_z, "x", d) for d in (1, 2, 3)],
    )
    other = swap(mine, "c", 1)

    (stiff,) = call(
        stiff_body, [((4368, 128), BF16)], [VM, SM, SM, VM, VM], "regroup", 1_000_000,
        child_stiff[0], child_map, own_pmap, child_map, own_basis,
    )
    (near,) = call(add_body, [((4640, 128), BF16)], [VM] * 2, "add", 1_000_000, stiff, swap(stiff, "b", 1))
    far = swap(near, "a", 1)

    (right,) = call(
        right_body, [((4, 96, 256), BF16)], [SM, VM, VM, VM], "right", 200_000_000, pos, columns, mine, other
    )
    child_maps = jnp.stack(
        [near[4352, :32], far[4352, :32], near[4624, :32], far[4624, :32]]
    ).astype(jnp.int32)
    right = exchange(right.reshape(384, 256), ("b", "a")).reshape(4, 96, 256)
    (left,) = call(
        left_body, [((224, 256), F32)], [SM, SM, SM] + [VM] * 5, "left", 500_000_000,
        pos, child_maps, pair_maps, columns, mine, other, near, far,
    )
    kept, sent = pl.pallas_call(
        final_body,
        out_shape=[jax.ShapeDtypeStruct((128, 1024), F32), jax.ShapeDtypeStruct((128, 1024), BF16)],
        in_specs=[SM] + [VM] * 4,
        out_specs=[VM, VM],
        scratch_shapes=[pltpu.VMEM((256, 1024), F32)],
        compiler_params=pltpu.CompilerParams(vmem_limit_bytes=32 << 20),
        cost_estimate=pl.CostEstimate(flops=120_000_000, bytes_accessed=2_000_000, transcendentals=0),
        name="product",
    )(pos, left, right, near, far)
    total = (kept + swap(sent, "c", 1).astype(F32)).astype(BF16)
    pieces = exchange(total.reshape(16, 8, 1024), ("z", "x"))
    return jnp.sum(pieces.astype(F32), axis=0)[None]


def solution(mesh):
    names = ("g", "b", "a", "z", "x", "c")
    split = Mesh(mesh.devices.reshape(4, 2, 2, 4, 4, 2), names)
    leaf = ("g", "b", "a")
    placed = (
        P(leaf, None, PANEL),
        P(leaf, PANEL, None),
        P(leaf, None, None),
        P(leaf, None),
        P(leaf, None),
        P(leaf, PANEL, None),
        P(leaf, None, None),
        P(leaf, None),
        P(),
        P(leaf, PANEL, None),
    )
    return jax.shard_map(
        shards, mesh=split, in_specs=placed, out_specs=P(leaf, PANEL, None), check_vma=False
    )
```

time: 158 us -> 115 us (0.73)
  local copies, waits for them, and re-layouts: 30.1 us -> 8.33 us
  waiting for transfers between devices: 42.4 us -> 27 us
  Pallas kernels: 0 us -> 12.3 us
  matrix products: 9.91 us -> 0 us
  other arithmetic: 8.71 us -> 0.81 us
  starting transfers between devices: 39.2 us -> 44.1 us
  blocking collectives: 25.2 us -> 21.4 us
    all_to_all x6 -> x3, waiting for transfers between devices: 40.9 us -> 6.46 us  [exchange(): return lax.all_to_all(value, axis, 0, 0, tiled=True)]
    ppermute x2 -> x7, waiting for transfers between devices: 1.5 us -> 20.5 us  [swap(): return lax.ppermute(value, axis, [(i, i ^ mask) for i in range(size)])]
    ppermute x2 -> x7, starting transfers between devices: 3.98 us -> 21.1 us  [swap(): return lax.ppermute(value, axis, [(i, i ^ mask) for i in range(size)])]
    pallas_call x0 -> x7, Pallas kernels: none -> 12.3 us  [the longest x5 6.17 us: call(): pl.pallas_call(body, out_shape=shapes, in_specs=specs, out_specs=[VM] * l...]
    all_to_all x6 -> x3, starting transfers between devices: 35.3 us -> 23 us  [exchange(): return lax.all_to_all(value, axis, 0, 0, tiled=True)]
    gather x8 -> x0, local copies, waits for them, and re-layouts: 10.6 us -> none  [the longest x3 5.36 us: shards(): part.at[index].get(mode='promise_in_bounds')]
    dot_general x6 -> x0, matrix products: 9.91 us -> none  [the longest x2 3.63 us: coupling(): lax.dot_general(modes, bound, (((0,), (1,)), ((), ())), preferred_element...]
    broadcast_in_dim x8 -> x1, local copies, waits for them, and re-layouts: 7.7 us -> 0.73 us  [shards(): jnp.broadcast_to(own_basis[None], (4, 128, 256))]
  transfers between devices with their start and end apart: 8 -> 10, of which waited for: 6 -> 6; matrix products, arithmetic and copies ran while one was open for 23% -> 1% of each run, Pallas kernels for 0% -> 9%
where the time goes in v2:
time: 115 us; the launch traced here: 114 us
  starting transfers between devices  44.1 us (38%)
  waiting for transfers between devices  27 us (23%)
  blocking collectives  21.4 us (19%)
  Pallas kernels  12.3 us (11%)
  local copies, waits for them, and re-layouts  8.33 us (7%)
    all_to_all x3, starting transfers between devices, exchange(): return lax.all_to_all(value, axis, 0, 0, tiled=True)  23 us
    all_to_all x1, blocking collectives, exchange(): return lax.all_to_all(value, axis, 0, 0, tiled=True)  21.4 us
    ppermute x7, starting transfers between devices, swap(): return lax.ppermute(value, axis, [(i, i ^ mask) for i in range(size)])  21.1 us
    ppermute x7, waiting for transfers between devices, swap(): return lax.ppermute(value, axis, [(i, i ^ mask) for i in range(size)])  20.5 us
    unnamed x16, local copies, waits for them, and re-layouts  6.9 us
    all_to_all x3, waiting for transfers between devices, exchange(): return lax.all_to_all(value, axis, 0, 0, tiled=True)  6.46 us
    pallas_call x5, Pallas kernels, call(): pl.pallas_call(body, out_shape=shapes, in_specs=specs, out_specs=[VM] * l...  6.17 us
    pallas_call x1, Pallas kernels, couple(): pl.pallas_call(coupling_body, grid=(steps,), out_shape=jax.ShapeDtypeStru...  4.45 us
  transfers between devices with their start and end apart: 10, of which 6 were waited for; matrix products, arithmetic and copies ran while one was open for 1% of the time, Pallas kernels for 9%

profile of v2, /device:TPU:56, one launch (start us, length us, event | category | flops | bytes accessed | tf_op | source)
XLA Modules:
  0.0 114.1 jit_solution(17039762926065084095)
XLA Ops:
  0.7 1.2 %copy-done.5 = bf16[1,4096,128]{2,1,0:T(8,128)(2,1)S(1)} copy-done((bf16[1,4096,128]{2,1,0:T(8,128)(2,1)S(1)}, bf16[1,4096,128]{2,1,0:T(8,128)(2,1)}, u32[]{:S(2)}) %copy-start.5) | copy-done | bytes 1048600
  4.3 3.3 %collective-permute-start = (bf16[4368,128]{1,0:T(8,128)(2,1)S(1)}, bf16[4368,128]{1,0:T(8,128)(2,1)S(1)}, u32[]{:S(2)}, u32[]{:S(2)}) collective-permute-start(bf16[4368,128]{1,0:T(8,128)(2,1)S(1)} %regroup.1.own_ref), channel_id=1, source_target_pairs={{0,64},{64,0},{1,65},{65,1},{2,66},{66,2},{3,67},{67,3},{4,68},{68... | collective-permute-start | bytes 3354632 | tf_op jit(solution)/shard_map/ppermute | solution.py:173
  8.3 10.3 %all-to-all-start.1 = ((bf16[4,128,256]{2,1,0:T(8,128)(2,1)}), bf16[4,128,256]{2,1,0:T(8,128)(2,1)S(1)}, u32[]{:S(2)}, u32[]{:S(2)}) async-start(bf16[4,128,256]{2,1,0:T(8,128)(2,1)} %broadcast_in_dim.8), calls=%async_computation.1 | async-start | bytes 524288 | tf_op jit(solution)/shard_map/all_to_all | solution.py:177
  18.6 4.4 %coupling.1 = bf16[4,32,24,128]{3,2,1,0:T(8,128)(2,1)} custom-call(bf16[2048,512]{1,0:T(8,128)(2,1)} %bitcast.25, bf16[128,2048]{1,0:T(8,128)(2,1)} %bitcast.27, f32[1,512]{1,0:T(1,128)} %ce_ref.1, bf16[2048,256]{1,0:T(8,128)(2,1)} %bitcast.26, bf16[128,2048]{1,0:T(8,128)(2,1)} %bitcast.28, f32[1,256]{1,0:T(1,128)} %pe_ref.1), custom_call_target="tpu_custom_call" | custom-call | flops 400000000 | bytes 5000000 | tf_op jit(solution)/shard_map/coupling/pallas_call | solution.py:65
  23.1 6.5 %all-to-all-done.1 = bf16[4,128,256]{2,1,0:T(8,128)(2,1)S(1)} async-done(((bf16[4,128,256]{2,1,0:T(8,128)(2,1)}), bf16[4,128,256]{2,1,0:T(8,128)(2,1)S(1)}, u32[]{:S(2)}, u32[]{:S(2)}) %all-to-all-start.1) | async-done | bytes 262176 | tf_op jit(solution)/shard_map/all_to_all | solution.py:177
  29.5 8.4 %all-to-all-start = ((bf16[128,24,128]{2,1,0:T(8,128)(2,1)}), bf16[128,24,128]{2,1,0:T(8,128)(2,1)S(1)}, u32[]{:S(2)}, u32[]{:S(2)}) async-start(bf16[128,24,128]{2,1,0:T(8,128)(2,1)} %bitcast.24), calls=%async_computation | async-start | bytes 1572864 | tf_op jit(solution)/shard_map/all_to_all | solution.py:177
  37.9 3.4 %collective-permute-start.2 = (bf16[512,256]{1,0:T(8,128)(2,1)S(1)}, bf16[512,256]{1,0:T(8,128)(2,1)S(1)}, u32[]{:S(2)}, u32[]{:S(2)}) collective-permute-start(bf16[512,256]{1,0:T(8,128)(2,1)S(1)} %bitcast.18), channel_id=1, source_target_pairs={{0,2},{2,0},{4,6},{6,4},{1,3},{3,1},{5,7},{7,5},{8,10},{10,8},{12,... | collective-permute-start | bytes 786440 | tf_op jit(solution)/shard_map/ppermute | solution.py:173
  41.3 4.6 %collective-permute-start.3 = (bf16[512,256]{1,0:T(8,128)(2,1)S(1)}, bf16[512,256]{1,0:T(8,128)(2,1)S(1)}, u32[]{:S(2)}, u32[]{:S(2)}) collective-permute-start(bf16[512,256]{1,0:T(8,128)(2,1)S(1)} %bitcast.19), channel_id=1, source_target_pairs={{0,4},{2,6},{4,0},{6,2},{1,5},{3,7},{5,1},{7,3},{8,12},{10,14},{12... | collective-permute-start | bytes 786440 | tf_op jit(solution)/shard_map/ppermute | solution.py:173
  45.9 2.4 %collective-permute-start.4 = (bf16[512,256]{1,0:T(8,128)(2,1)S(1)}, bf16[512,256]{1,0:T(8,128)(2,1)S(1)}, u32[]{:S(2)}, u32[]{:S(2)}) collective-permute-start(bf16[512,256]{1,0:T(8,128)(2,1)S(1)} %bitcast.20), channel_id=1, source_target_pairs={{0,6},{2,4},{4,2},{6,0},{1,7},{3,5},{5,3},{7,1},{8,14},{10,12},{12... | collective-permute-start | bytes 786440 | tf_op jit(solution)/shard_map/ppermute | solution.py:173
  49.4 1.2 %copy-done.2 = bf16[4368,128]{1,0:T(8,128)(2,1)S(1)} copy-done((bf16[4368,128]{1,0:T(8,128)(2,1)S(1)}, bf16[4368,128]{1,0:T(8,128)(2,1)}, u32[]{:S(2)}) %copy-start.2) | copy-done | bytes 1118232
  50.6 1.2 %copy-done.4 = bf16[4368,128]{1,0:T(8,128)(2,1)S(1)} copy-done((bf16[4368,128]{1,0:T(8,128)(2,1)S(1)}, bf16[4368,128]{1,0:T(8,128)(2,1)}, u32[]{:S(2)}) %copy-start.4) | copy-done | bytes 1118232
  52.2 3.6 %collective-permute-start.1 = (bf16[4640,128]{1,0:T(8,128)(2,1)S(1)}, bf16[4640,128]{1,0:T(8,128)(2,1)}, u32[]{:S(2)}, u32[]{:S(2)}) collective-permute-start(bf16[4640,128]{1,0:T(8,128)(2,1)S(1)} %add.26.own_ref.w0_ref), channel_id=1, source_target_pairs={{0,32},{32,0},{1,33},{33,1},{2,34},{34,2},{3,35},{35,3},{4,36},{36... | collective-permute-start | bytes 3563528 | tf_op jit(solution)/shard_map/ppermute | solution.py:173
  55.8 7.7 %collective-permute-done.3.c_ref = bf16[512,256]{1,0:T(8,128)(2,1)S(1)} collective-permute-done((bf16[512,256]{1,0:T(8,128)(2,1)S(1)}, bf16[512,256]{1,0:T(8,128)(2,1)S(1)}, u32[]{:S(2)}, u32[]{:S(2)}) %collective-permute-start.3) | collective-permute-done | bytes 262176 | tf_op jit(solution)/shard_map/ppermute | solution.py:173
  63.5 2.7 %collective-permute-done.4.d_ref = bf16[512,256]{1,0:T(8,128)(2,1)S(1)} collective-permute-done((bf16[512,256]{1,0:T(8,128)(2,1)S(1)}, bf16[512,256]{1,0:T(8,128)(2,1)S(1)}, u32[]{:S(2)}, u32[]{:S(2)}) %collective-permute-start.4) | collective-permute-done | bytes 262176 | tf_op jit(solution)/shard_map/ppermute | solution.py:173
  66.3 1.9 %collective-permute-start.5 = (bf16[2048,256]{1,0:T(8,128)(2,1)S(1)}, bf16[2048,256]{1,0:T(8,128)(2,1)}, u32[]{:S(2)}, u32[]{:S(2)}) collective-permute-start(bf16[2048,256]{1,0:T(8,128)(2,1)S(1)} %join.1.mine_ref), channel_id=1, source_target_pairs={{0,1},{1,0},{2,3},{3,2},{4,5},{5,4},{6,7},{7,6},{8,9},{9,8},{10,11... | collective-permute-start | bytes 3145736 | tf_op jit(solution)/shard_map/ppermute | solution.py:173
  68.3 2.6 %collective-permute-done.5.other_ref = bf16[2048,256]{1,0:T(8,128)(2,1)} collective-permute-done((bf16[2048,256]{1,0:T(8,128)(2,1)S(1)}, bf16[2048,256]{1,0:T(8,128)(2,1)}, u32[]{:S(2)}, u32[]{:S(2)}) %collective-permute-start.5) | collective-permute-done | bytes 1048608 | tf_op jit(solution)/shard_map/ppermute | solution.py:173
  71.0 2.4 %right.1 = bf16[4,96,256]{2,1,0:T(8,128)(2,1)} custom-call(s32[3]{0:T(128)S(1)} %pad_add_fusion.pos_ref, bf16[4,32,24,128]{3,2,1,0:T(8,128)(2,1)S(1)} %bitcast.15, bf16[2048,256]{1,0:T(8,128)(2,1)S(1)} %join.1.mine_ref, bf16[2048,256]{1,0:T(8,128)(2,1)} %collective-permute-done.5.other_ref), custom_call_target="tpu_custom_call" | custom-call | flops 200000000 | bytes 2883596 | tf_op jit(solution)/shard_map/right/pallas_call | solution.py:22
  73.4 4.3 %all-to-all-start.2 = ((bf16[4,96,256]{2,1,0:T(8,128)(2,1)}), bf16[4,96,256]{2,1,0:T(8,128)(2,1)S(1)}, u32[]{:S(2)}, u32[]{:S(2)}) async-start(bf16[4,96,256]{2,1,0:T(8,128)(2,1)} %right.1), calls=%async_computation.2 | async-start | bytes 393216 | tf_op jit(solution)/shard_map/all_to_all | solution.py:177
  77.7 6.0 %collective-permute-done.1.far_ref.w1_ref = bf16[4640,128]{1,0:T(8,128)(2,1)} collective-permute-done((bf16[4640,128]{1,0:T(8,128)(2,1)S(1)}, bf16[4640,128]{1,0:T(8,128)(2,1)}, u32[]{:S(2)}, u32[]{:S(2)}) %collective-permute-start.1) | collective-permute-done | bytes 1187872 | tf_op jit(solution)/shard_map/ppermute | solution.py:173
  84.3 2.5 %left.1.left_ref = f32[224,256]{1,0:T(8,128)S(1)} custom-call(s32[3]{0:T(128)S(1)} %pad_add_fusion.pos_ref, s32[4,32]{1,0:T(4,128)S(1)} %maximum_convert_fusion.cmaps_ref, s32[2,32]{1,0:T(2,128)S(1)} %constant_dynamic-slice_fusion.pmaps_ref, bf16[4,32,24,128]{3,2,1,0:T(8,128)(2,1)S(1)} %bitcast.16, bf16[2048,256]{1,0:T(8,128)(2,1)S(1)} %join.1.mine_ref, ...), custom_call_target="tpu_custom_call" | custom-call | flops 500000000 | bytes 5260044 | tf_op jit(solution)/shard_map/left/pallas_call | solution.py:22
  86.8 1.7 %product.1 = (f32[128,1024]{1,0:T(8,128)S(1)}, bf16[128,1024]{1,0:T(8,128)(2,1)S(1)}) custom-call(s32[3]{0:T(128)S(1)} %pad_add_fusion.pos_ref, f32[224,256]{1,0:T(8,128)S(1)} %left.1.left_ref, bf16[4,96,256]{2,1,0:T(8,128)(2,1)S(1)} %all-to-all-done.2.right_ref, bf16[4640,128]{1,0:T(8,128)(2,1)S(1)} %add.26.own_ref.w0_ref, ...), custom_call_target="tpu_custom_call" | custom-call | flops 120000000 | bytes 2000000 | tf_op jit(solution)/shard_map/product/pallas_call | solution.py:228
  88.6 1.9 %collective-permute-start.6 = (bf16[128,1024]{1,0:T(8,128)(2,1)S(1)}, bf16[128,1024]{1,0:T(8,128)(2,1)S(1)}, u32[]{:S(2)}, u32[]{:S(2)}) collective-permute-start(bf16[128,1024]{1,0:T(8,128)(2,1)S(1)} %get-tuple-element.8), channel_id=1, source_target_pairs={{0,1},{1,0},{2,3},{3,2},{4,5},{5,4},{6,7},{7,6},{8,9},{9,8},{10,11... | collective-permute-start | bytes 786440 | tf_op jit(solution)/shard_map/ppermute | solution.py:173
  90.5 1.5 %collective-permute-done.6 = bf16[128,1024]{1,0:T(8,128)(2,1)S(1)} collective-permute-done((bf16[128,1024]{1,0:T(8,128)(2,1)S(1)}, bf16[128,1024]{1,0:T(8,128)(2,1)S(1)}, u32[]{:S(2)}, u32[]{:S(2)}) %collective-permute-start.6) | collective-permute-done | bytes 262176 | tf_op jit(solution)/shard_map/ppermute | solution.py:173
  92.1 21.4 %all_to_all.21 = bf16[16,8,1024]{2,1,0:T(8,128)(2,1)S(1)} all-to-all(bf16[16,8,1024]{2,1,0:T(8,128)(2,1)S(1)} %fusion), channel_id=1, replica_groups=mesh['g'=4,'b'=2,'a'=2,'z'=4,'x'=4,'c'=2] {'z','x'}, dimensions={0} | all-to-all | bytes 524288 | tf_op jit(solution)/shard_map/all_to_all | solution.py:177
  (29 shorter events, 6.7 us)
Async XLA Ops:
  0.0 0.7 copy-start
  0.7 1.2 %copy-start.5 = (bf16[1,4096,128]{2,1,0:T(8,128)(2,1)S(1)}, bf16[1,4096,128]{2,1,0:T(8,128)(2,1)}, u32[]{:S(2)}) copy-start(bf16[1,4096,128]{2,1,0:T(8,128)(2,1)} %param.10) | copy-start | bytes 3145732
  1.9 0.8 copy-start.6
  2.8 0.7 copy-start.7
  4.3 18.8 %copy-start.1 = (bf16[4368,128]{1,0:T(8,128)(2,1)}, bf16[4368,128]{1,0:T(8,128)(2,1)S(1)}, u32[]{:S(2)}) copy-start(bf16[4368,128]{1,0:T(8,128)(2,1)S(1)} %regroup.1.own_ref) | copy-start | bytes 3354628
  4.3 44.0 %collective-permute-start = (bf16[4368,128]{1,0:T(8,128)(2,1)S(1)}, bf16[4368,128]{1,0:T(8,128)(2,1)S(1)}, u32[]{:S(2)}, u32[]{:S(2)}) collective-permute-start(bf16[4368,128]{1,0:T(8,128)(2,1)S(1)} %regroup.1.own_ref), channel_id=1, source_target_pairs={{0,64},{64,0},{1,65},{65,1},{2,66},{66,2},{3,67},{67,3},{4,68},{68... | collective-permute-start | bytes 3354632 | tf_op jit(solution)/shard_map/ppermute | solution.py:173
  8.3 21.2 %all-to-all-start.1 = ((bf16[4,128,256]{2,1,0:T(8,128)(2,1)}), bf16[4,128,256]{2,1,0:T(8,128)(2,1)S(1)}, u32[]{:S(2)}, u32[]{:S(2)}) async-start(bf16[4,128,256]{2,1,0:T(8,128)(2,1)} %broadcast_in_dim.8), calls=%async_computation.1 | async-start | bytes 524288 | tf_op jit(solution)/shard_map/all_to_all | solution.py:177
  29.5 38.8 %all-to-all-start = ((bf16[128,24,128]{2,1,0:T(8,128)(2,1)}), bf16[128,24,128]{2,1,0:T(8,128)(2,1)S(1)}, u32[]{:S(2)}, u32[]{:S(2)}) async-start(bf16[128,24,128]{2,1,0:T(8,128)(2,1)} %bitcast.24), calls=%async_computation | async-start | bytes 1572864 | tf_op jit(solution)/shard_map/all_to_all | solution.py:177
  37.9 17.9 %collective-permute-start.2 = (bf16[512,256]{1,0:T(8,128)(2,1)S(1)}, bf16[512,256]{1,0:T(8,128)(2,1)S(1)}, u32[]{:S(2)}, u32[]{:S(2)}) collective-permute-start(bf16[512,256]{1,0:T(8,128)(2,1)S(1)} %bitcast.18), channel_id=1, source_target_pairs={{0,2},{2,0},{4,6},{6,4},{1,3},{3,1},{5,7},{7,5},{8,10},{10,8},{12,... | collective-permute-start | bytes 786440 | tf_op jit(solution)/shard_map/ppermute | solution.py:173
  41.3 22.2 %collective-permute-start.3 = (bf16[512,256]{1,0:T(8,128)(2,1)S(1)}, bf16[512,256]{1,0:T(8,128)(2,1)S(1)}, u32[]{:S(2)}, u32[]{:S(2)}) collective-permute-start(bf16[512,256]{1,0:T(8,128)(2,1)S(1)} %bitcast.19), channel_id=1, source_target_pairs={{0,4},{2,6},{4,0},{6,2},{1,5},{3,7},{5,1},{7,3},{8,12},{10,14},{12... | collective-permute-start | bytes 786440 | tf_op jit(solution)/shard_map/ppermute | solution.py:173
  45.9 20.3 %collective-permute-start.4 = (bf16[512,256]{1,0:T(8,128)(2,1)S(1)}, bf16[512,256]{1,0:T(8,128)(2,1)S(1)}, u32[]{:S(2)}, u32[]{:S(2)}) collective-permute-start(bf16[512,256]{1,0:T(8,128)(2,1)S(1)} %bitcast.20), channel_id=1, source_target_pairs={{0,6},{2,4},{4,2},{6,0},{1,7},{3,5},{5,3},{7,1},{8,14},{10,12},{12... | collective-permute-start | bytes 786440 | tf_op jit(solution)/shard_map/ppermute | solution.py:173
  48.4 1.0 copy-start.3
  49.4 1.2 %copy-start.2 = (bf16[4368,128]{1,0:T(8,128)(2,1)S(1)}, bf16[4368,128]{1,0:T(8,128)(2,1)}, u32[]{:S(2)}) copy-start(bf16[4368,128]{1,0:T(8,128)(2,1)} %copy-done.1) | copy-start | bytes 3354628
  50.6 1.2 %copy-start.4 = (bf16[4368,128]{1,0:T(8,128)(2,1)S(1)}, bf16[4368,128]{1,0:T(8,128)(2,1)}, u32[]{:S(2)}) copy-start(bf16[4368,128]{1,0:T(8,128)(2,1)} %copy-done.3) | copy-start | bytes 3354628
  52.2 31.5 %collective-permute-start.1 = (bf16[4640,128]{1,0:T(8,128)(2,1)S(1)}, bf16[4640,128]{1,0:T(8,128)(2,1)}, u32[]{:S(2)}, u32[]{:S(2)}) collective-permute-start(bf16[4640,128]{1,0:T(8,128)(2,1)S(1)} %add.26.own_ref.w0_ref), channel_id=1, source_target_pairs={{0,32},{32,0},{1,33},{33,1},{2,34},{34,2},{3,35},{35,3},{4,36},{36... | collective-permute-start | bytes 3563528 | tf_op jit(solution)/shard_map/ppermute | solution.py:173
  66.3 4.7 %collective-permute-start.5 = (bf16[2048,256]{1,0:T(8,128)(2,1)S(1)}, bf16[2048,256]{1,0:T(8,128)(2,1)}, u32[]{:S(2)}, u32[]{:S(2)}) collective-permute-start(bf16[2048,256]{1,0:T(8,128)(2,1)S(1)} %join.1.mine_ref), channel_id=1, source_target_pairs={{0,1},{1,0},{2,3},{3,2},{4,5},{5,4},{6,7},{7,6},{8,9},{9,8},{10,11... | collective-permute-start | bytes 3145736 | tf_op jit(solution)/shard_map/ppermute | solution.py:173
  73.4 13.5 %all-to-all-start.2 = ((bf16[4,96,256]{2,1,0:T(8,128)(2,1)}), bf16[4,96,256]{2,1,0:T(8,128)(2,1)S(1)}, u32[]{:S(2)}, u32[]{:S(2)}) async-start(bf16[4,96,256]{2,1,0:T(8,128)(2,1)} %right.1), calls=%async_computation.2 | async-start | bytes 393216 | tf_op jit(solution)/shard_map/all_to_all | solution.py:177
  88.6 3.4 %collective-permute-start.6 = (bf16[128,1024]{1,0:T(8,128)(2,1)S(1)}, bf16[128,1024]{1,0:T(8,128)(2,1)S(1)}, u32[]{:S(2)}, u32[]{:S(2)}) collective-permute-start(bf16[128,1024]{1,0:T(8,128)(2,1)S(1)} %get-tuple-element.8), channel_id=1, source_target_pairs={{0,1},{1,0},{2,3},{3,2},{4,5},{5,4},{6,7},{7,6},{8,9},{9,8},{10,11... | collective-permute-start | bytes 786440 | tf_op jit(solution)/shard_map/ppermute | solution.py:173

commit v3 on v2

v3 whole, which is shorter than its diff:
```python
import functools

import jax
import jax.numpy as jnp
from jax import lax
from jax.experimental import pallas as pl
from jax.experimental.pallas import tpu as pltpu
from jax.sharding import Mesh
from jax.sharding import PartitionSpec as P

PANEL = ("z", "x", "c")
LEAF = ("b", "a")
F32 = jnp.float32
BF16 = jnp.bfloat16
VM = pl.BlockSpec(memory_space=pltpu.VMEM)
SM = pl.BlockSpec(memory_space=pltpu.SMEM)
ANY = pl.BlockSpec(memory_space=pl.ANY)


def call(body, outs, specs, name, flops, *args):
    shapes = [jax.ShapeDtypeStruct(s, t) for s, t in outs]
    moved = sum(a.size * a.dtype.itemsize for a in args)
    return pl.pallas_call(
        body,
        out_shape=shapes,
        in_specs=specs,
        out_specs=[VM] * len(outs),
        compiler_params=pltpu.CompilerParams(vmem_limit_bytes=12 << 20),
        cost_estimate=pl.CostEstimate(flops=0, bytes_accessed=0, transcendentals=0),
        name=name,
    )(*args)


def dot(left, right):
    return jnp.dot(left, right, preferred_element_type=F32)


def coupling_body(
    cm_ref, cb_ref, ce_ref, pm_ref, pb_ref, pe_ref, u_ref, out_ref, child_ref, parent_ref
):
    step = pl.program_id(0)

    @pl.when(step == 0)
    def _():
        child_ref[...] = jnp.zeros_like(child_ref)
        parent_ref[...] = jnp.zeros_like(parent_ref)

    child_ref[...] += dot(cb_ref[...], cm_ref[...])
    parent_ref[...] += dot(pb_ref[...], pm_ref[...])

    @pl.when(step == pl.num_programs(0) - 1)
    def _():
        child = child_ref[...] * jnp.sqrt(ce_ref[...])
        parent = parent_ref[...] * jnp.sqrt(pe_ref[...])
        both = jnp.concatenate(
            [child.T.reshape(32, 16, 128), parent.T.reshape(32, 8, 128)], axis=1
        ).reshape(768, 128).astype(BF16)
        for z in range(4):
            out_ref[z, :192, :] = both[192 * z : 192 * (z + 1)]
            out_ref[z, 192:320, :] = u_ref[:, :128]
            out_ref[z, 320:, :] = u_ref[:, 128:]


def couple(*args):
    steps = 2
    depth = args[0].shape[0] // steps
    modes = lambda width: pl.BlockSpec((depth, width), lambda i: (i, 0))
    bound = pl.BlockSpec((128, depth), lambda i: (0, i))
    whole = lambda *shape: pl.BlockSpec(shape, lambda i: (0,) * len(shape))
    return pl.pallas_call(
        coupling_body,
        grid=(steps,),
        out_shape=jax.ShapeDtypeStruct((4, 448, 128), BF16),
        in_specs=[modes(512), bound, whole(1, 512), modes(256), bound, whole(1, 256), whole(128, 256)],
        out_specs=whole(4, 448, 128),
        scratch_shapes=[pltpu.VMEM((128, 512), F32), pltpu.VMEM((128, 256), F32)],
        compiler_params=pltpu.CompilerParams(vmem_limit_bytes=60 << 20),
        cost_estimate=pl.CostEstimate(flops=0, bytes_accessed=0, transcendentals=0),
        name="coupling",
    )(*args)


def regroup_body(stiff_ref, cmap_ref, pmap_ref, keep_ref, send_ref, sems):
    b = lax.axis_index("b")
    parent = 2 * lax.axis_index("g") + b
    for i in range(16):
        for k, (ref, half) in enumerate(((keep_ref, b), (send_ref, 1 - b))):
            row = cmap_ref[0, pmap_ref[parent, half * 16 + i]]
            pltpu.make_async_copy(
                stiff_ref.at[pl.ds(pl.multiple_of(row * 128, 128), 128)], ref.at[pl.ds(i * 128, 128)], sems.at[k]
            ).start()
    for k, ref in enumerate((keep_ref, send_ref)):
        pltpu.make_async_copy(stiff_ref.at[pl.ds(0, 2048)], ref, sems.at[k]).wait()


def regroup(*args):
    return pl.pallas_call(
        regroup_body,
        out_shape=[jax.ShapeDtypeStruct((2048, 128), BF16)] * 2,
        in_specs=[ANY, SM, SM],
        out_specs=[VM, VM],
        scratch_shapes=[pltpu.SemaphoreType.DMA((2,))],
        compiler_params=pltpu.CompilerParams(vmem_limit_bytes=12 << 20),
        cost_estimate=pl.CostEstimate(flops=0, bytes_accessed=0, transcendentals=0),
        name="regroup",
    )(*args)


def split_body(got_ref, out_ref):
    parts = [got_ref[z, :192, :].astype(F32).reshape(8, 24, 128) for z in range(4)]
    columns = jnp.concatenate(parts, axis=1).astype(BF16)
    for k in range(8):
        out_ref[k, :96, :] = columns[k]
        for z in range(4):
            at = 192 + 128 * (k % 2)
            out_ref[k, 96 + 128 * z : 224 + 128 * z, :] = got_ref[z, at : at + 128, :]


def repeat_body(one_ref, basis_ref, row_ref, near_ref, far_ref, out_ref, half_ref):
    half_ref[...] = (near_ref[...].astype(F32) + far_ref[...].astype(F32)).astype(BF16)
    row = jnp.concatenate([row_ref[...], jnp.zeros((1, 96), jnp.int32)], axis=1).astype(F32)
    basis = basis_ref[...].astype(F32)
    rest = jnp.concatenate([basis[:, :128], basis[:, 128:], jnp.broadcast_to(row, (32, 128))], axis=0)
    rest = rest.reshape(12, 24, 128).astype(BF16)
    columns = one_ref[:, :96, :].astype(F32).reshape(32, 24, 128).astype(BF16)
    for q in range(4):
        out_ref[q, :32] = columns
        out_ref[q, 32:] = rest


def column_index(panel):
    return lax.rem(panel, 8) * 4 + panel // 8


def fetch(source_ref, held_ref, sem):
    copy = pltpu.make_async_copy(source_ref, held_ref, sem)
    copy.start()
    return copy


def times_basis(left_ref, mine_ref, held_ref):
    total = jnp.zeros((left_ref.shape[1], 256), F32)
    for k in range(8):
        for h in (0, 1):
            rows = pl.ds(96 + 256 * h, 256)
            block = jnp.concatenate([mine_ref[k, rows, :], held_ref[k, rows, :]], axis=1)
            total = total + dot(left_ref[2 * k + h], block)
    return total


def in_order(total, ref, *at):
    for half in (0, 1):
        lanes = pl.ds(pl.multiple_of(128 * (lax.axis_index("c") ^ half), 128), 128)
        ref[(*at, lanes)] = total[:, 128 * half : 128 * (half + 1)]


def right_body(col_ref, mine_ref, other_ref, out_ref, held_ref, left_ref, sem):
    copy = fetch(other_ref, held_ref, sem)
    for n in range(16):
        cols = [col_ref[:, 2 * n + s].astype(F32).reshape(96, 128) for s in (0, 1)]
        left_ref[n] = jnp.concatenate(cols, axis=1).astype(BF16)
    copy.wait()
    total = times_basis(left_ref, mine_ref, held_ref).astype(BF16)
    for q in range(4):
        in_order(total, out_ref, q, slice(None))


def left_modes_body(cmaps_ref, pmaps_ref, col_ref, mine_ref, other_ref, out_ref, held_ref, left_ref, sem):
    copy = fetch(other_ref, held_ref, sem)
    first = 2 * lax.axis_index("g")
    for n in range(16):
        pair = []
        for s in (0, 1):
            panel = (2 * n + s) % 4 * 8 + n // 2
            for_leaf = []
            for leaf in range(4):
                row = pmaps_ref[first + leaf // 2, panel]
                for_leaf.append(col_ref[leaf, column_index(cmaps_ref[leaf, row])].astype(F32)[:16])
                for_leaf.append(col_ref[leaf, column_index(row)].astype(F32)[16:])
            pair.append(jnp.concatenate(for_leaf, axis=0))
        left_ref[n] = jnp.concatenate(pair, axis=1).astype(BF16)
    copy.wait()
    in_order(-times_basis(left_ref, mine_ref, held_ref), out_ref, slice(None))


def left_stiff_body(mine_ref, other_ref, half_ref, other_half_ref, after_ref, out_ref, low, high, held_ref, left_ref, sems):
    b = lax.axis_index("b")
    for k, ref in enumerate((half_ref, other_half_ref)):
        for value, rows in enumerate((low, high)):

            @pl.when((b ^ k) == value)
            def _(ref=ref, rows=rows, k=k):
                pltpu.make_async_copy(ref, rows, sems.at[k]).start()

    copy = fetch(other_ref, held_ref, sems.at[2])
    for k in (0, 1):
        pltpu.make_async_copy(half_ref, low, sems.at[k]).wait()
    for n in range(16):
        part = (low, high)[n % 2]
        rows = [part[pl.ds(128 * (8 * s + n // 2), 128), :].astype(F32).T for s in (0, 1)]
        left_ref[n] = jnp.concatenate(rows, axis=1).astype(BF16)
    copy.wait()
    in_order(times_basis(left_ref, mine_ref, held_ref), out_ref, slice(None))


HELD = pltpu.VMEM((8, 608, 128), BF16)


def project(body, out, dtype, specs, scratch, name, *args):
    return pl.pallas_call(
        body,
        out_shape=jax.ShapeDtypeStruct(out, dtype),
        in_specs=specs,
        out_specs=VM,
        scratch_shapes=scratch,
        compiler_params=pltpu.CompilerParams(vmem_limit_bytes=12 << 20),
        cost_estimate=pl.CostEstimate(flops=0, bytes_accessed=0, transcendentals=0),
        name=name,
    )(*args)


def final_body(stiff_ref, modes_ref, right_ref, col_ref, mine_ref, theirs_ref, all_ref):
    left = jnp.concatenate([stiff_ref[...], modes_ref[...]], axis=0).T.astype(BF16)
    for leaf in range(4):
        basis = col_ref[leaf, 32:].astype(F32).reshape(288, 128)
        basis = jnp.concatenate([basis[:128], basis[128:256]], axis=1)
        stacked = jnp.concatenate([basis, right_ref[leaf].astype(F32)], axis=0).astype(BF16)
        all_ref[:, 256 * leaf : 256 * (leaf + 1)] = dot(left, stacked)
    c = lax.axis_index("c")
    mine, theirs = [], []
    for t in range(16):
        mine.append(all_ref[pl.ds(pl.multiple_of(16 * t + 8 * c, 8), 8), :])
        theirs.append(all_ref[pl.ds(pl.multiple_of(16 * t + 8 * (1 - c), 8), 8), :])
    mine_ref[...] = jnp.concatenate(mine, axis=0)
    theirs_ref[...] = jnp.concatenate(theirs, axis=0).astype(BF16)


def swap(value, axis, mask):
    size = lax.axis_size(axis)
    return lax.ppermute(value, axis, [(i, i ^ mask) for i in range(size)])


def exchange(value, axis):
    return lax.all_to_all(value, axis, 0, 0, tiled=True)


def shards(
    child_stiff,
    child_bound,
    child_modes,
    child_inv_eig,
    child_map,
    parent_bound,
    parent_modes,
    parent_inv_eig,
    parent_map,
    interface_basis,
):
    own_basis = interface_basis[0]

    keep, send = regroup(child_stiff[0], child_map, parent_map)
    packed = couple(
        child_modes[0], child_bound[0], child_inv_eig, parent_modes[0], parent_bound[0], parent_inv_eig, own_basis
    )
    near = (keep.astype(F32) + swap(send, "b", 1).astype(F32)).astype(BF16)
    far = swap(near, "a", 1)
    (message,) = call(split_body, [((8, 608, 128), BF16)], [VM], "split", 1_000_000, exchange(packed, "z"))
    mine = exchange(message, ("x", "c"))
    other = swap(mine, "c", 1)
    copies, half = call(
        repeat_body, [((4, 44, 24, 128), BF16), ((2048, 128), BF16)], [VM] * 5, "repeat", 1_000_000,
        mine, own_basis, child_map, near, far,
    )
    other_half = swap(half, "b", 1)
    columns = exchange(copies.reshape(176, 24, 128), LEAF).reshape(4, 44, 24, 128)

    modes_left = pltpu.VMEM((16, 96, 256), BF16)
    one_sem = pltpu.SemaphoreType.DMA(())
    right = project(
        right_body, (4, 96, 256), BF16, [VM, VM, ANY], [HELD, modes_left, one_sem], "right", columns, mine, other
    )
    right = exchange(right.reshape(384, 256), LEAF).reshape(4, 96, 256)
    child_maps = columns[:, 42, 16, :32].astype(jnp.int32)
    modes = project(
        left_modes_body, (96, 256), F32, [SM, SM, VM, VM, ANY], [HELD, modes_left, one_sem], "left_modes",
        child_maps, parent_map, columns, mine, other,
    )
    stiff = project(
        left_stiff_body, (128, 256), F32, [VM, ANY, ANY, ANY, ANY],
        [pltpu.VMEM((2048, 128), BF16)] * 2 + [HELD, pltpu.VMEM((16, 128, 256), BF16), pltpu.SemaphoreType.DMA((3,))],
        "left_stiff", mine, other, half, other_half, modes,
    )
    kept, sent = pl.pallas_call(
        final_body,
        out_shape=[jax.ShapeDtypeStruct((128, 1024), F32), jax.ShapeDtypeStruct((128, 1024), BF16)],
        in_specs=[VM] * 4,
        out_specs=[VM, VM],
        scratch_shapes=[pltpu.VMEM((256, 1024), F32)],
        compiler_params=pltpu.CompilerParams(vmem_limit_bytes=12 << 20),
        cost_estimate=pl.CostEstimate(flops=0, bytes_accessed=0, transcendentals=0),
        name="product",
    )(stiff, modes, right, columns)
    total = (kept + swap(sent, "c", 1).astype(F32)).astype(BF16)
    pieces = exchange(total.reshape(16, 8, 1024), ("z", "x"))
    return jnp.sum(pieces.astype(F32), axis=0)[None]


def solution(mesh):
    names = ("g", "b", "a", "z", "x", "c")
    split = Mesh(mesh.devices.reshape(4, 2, 2, 4, 4, 2), names)
    leaf = ("g", "b", "a")
    placed = (
        P(leaf, None, PANEL),
        P(leaf, PANEL, None),
        P(leaf, None, None),
        P(leaf, None),
        P(leaf, None),
        P(leaf, PANEL, None),
        P(leaf, None, None),
        P(leaf, None),
        P(),
        P(leaf, PANEL, None),
    )
    return jax.shard_map(
        shards, mesh=split, in_specs=placed, out_specs=P(leaf, PANEL, None), check_vma=False
    )
```

time: 115 us -> 108 us (0.939)
  starting transfers between devices: 44.1 us -> 38.9 us
  waiting for transfers between devices: 27 us -> 31.8 us
  local copies, waits for them, and re-layouts: 8.33 us -> 3.66 us
  blocking collectives: 21.4 us -> 17.2 us
  Pallas kernels: 12.3 us -> 14.9 us
    all_to_all x3 -> x4, waiting for transfers between devices: 6.46 us -> 16.7 us  [exchange(): return lax.all_to_all(value, axis, 0, 0, tiled=True)]
    pallas_call x0 -> x4, Pallas kernels: none -> 8.53 us  [the longest x3 6.21 us: project(): pl.pallas_call(body, out_shape=jax.ShapeDtypeStruct(out, dtype), in_specs...]
    ppermute x7 -> x5, starting transfers between devices: 21.1 us -> 13.6 us  [swap(): return lax.ppermute(value, axis, [(i, i ^ mask) for i in range(size)])]
    ppermute x7 -> x5, waiting for transfers between devices: 20.5 us -> 15.1 us  [swap(): return lax.ppermute(value, axis, [(i, i ^ mask) for i in range(size)])]
    all_to_all x1, blocking collectives: 21.4 us -> 17.2 us  [exchange(): return lax.all_to_all(value, axis, 0, 0, tiled=True)]
    pallas_call x5 -> x2, Pallas kernels: 6.17 us -> 2.37 us  [call(): pl.pallas_call(body, out_shape=shapes, in_specs=specs, out_specs=[VM] * l...]
    unnamed x16, local copies, waits for them, and re-layouts: 6.9 us -> 3.66 us
    all_to_all x3 -> x4, starting transfers between devices: 23 us -> 25.3 us  [exchange(): return lax.all_to_all(value, axis, 0, 0, tiled=True)]
  transfers between devices with their start and end apart: 10 -> 9, of which waited for: 6 -> 6; matrix products, arithmetic and copies ran while one was open for 1% -> 0% of each run, Pallas kernels for 9% -> 9%
where the time goes in v3:
time: 108 us; the launch traced here: 107 us
  starting transfers between devices  38.9 us (36%)
  waiting for transfers between devices  31.8 us (29%)
  blocking collectives  17.2 us (16%)
  Pallas kernels  14.9 us (14%)
  local copies, waits for them, and re-layouts  3.66 us (3%)
    all_to_all x4, starting transfers between devices, exchange(): return lax.all_to_all(value, axis, 0, 0, tiled=True)  25.3 us
    all_to_all x1, blocking collectives, exchange(): return lax.all_to_all(value, axis, 0, 0, tiled=True)  17.2 us
    all_to_all x4, waiting for transfers between devices, exchange(): return lax.all_to_all(value, axis, 0, 0, tiled=True)  16.7 us
    ppermute x5, waiting for transfers between devices, swap(): return lax.ppermute(value, axis, [(i, i ^ mask) for i in range(size)])  15.1 us
    ppermute x5, starting transfers between devices, swap(): return lax.ppermute(value, axis, [(i, i ^ mask) for i in range(size)])  13.6 us
    pallas_call x3, Pallas kernels, project(): pl.pallas_call(body, out_shape=jax.ShapeDtypeStruct(out, dtype), in_specs...  6.21 us
    unnamed x16, local copies, waits for them, and re-layouts  3.66 us
    pallas_call x1, Pallas kernels, couple(): pl.pallas_call(coupling_body, grid=(steps,), out_shape=jax.ShapeDtypeStru...  3.56 us
  transfers between devices with their start and end apart: 9, of which 6 were waited for; matrix products, arithmetic and copies ran while one was open for 0% of the time, Pallas kernels for 9%

profile of v3, /device:TPU:56, one launch (start us, length us, event | category | flops | bytes accessed | tf_op | source)
XLA Modules:
  0.0 107.4 jit_solution(11901407466535476097)
XLA Ops:
  0.0 3.6 %coupling.1 = bf16[4,448,128]{2,1,0:T(8,128)(2,1)} custom-call(bf16[2048,512]{1,0:T(8,128)(2,1)} %bitcast.20, bf16[128,2048]{1,0:T(8,128)(2,1)} %bitcast.22, f32[1,512]{1,0:T(1,128)} %ce_ref.1, bf16[2048,256]{1,0:T(8,128)(2,1)} %bitcast.21, bf16[128,2048]{1,0:T(8,128)(2,1)} %bitcast.23, f32[1,256]{1,0:T(1,128)} %pe_ref.1, bf16[128,256]{1,0:T(8,128)(2,1)} %bitcast.17), custom_call_target="tpu_custom_call" | custom-call | tf_op jit(solution)/shard_map/coupling/pallas_call | solution.py:70
  3.6 10.3 %all-to-all-start = ((bf16[4,448,128]{2,1,0:T(8,128)(2,1)}), bf16[4,448,128]{2,1,0:T(8,128)(2,1)S(1)}, u32[]{:S(2)}, u32[]{:S(2)}) async-start(bf16[4,448,128]{2,1,0:T(8,128)(2,1)} %coupling.1), calls=%async_computation | async-start | bytes 917504 | tf_op jit(solution)/shard_map/all_to_all | solution.py:244
  13.9 2.3 %regroup.1 = (bf16[2048,128]{1,0:T(8,128)(2,1)S(1)}, bf16[2048,128]{1,0:T(8,128)(2,1)S(1)}) custom-call(bf16[4096,128]{1,0:T(8,128)(2,1)S(1)} %bitcast.16, s32[1,32]{1,0:T(1,128)S(1)} %copy-done.7, s32[8,32]{1,0:T(8,128)S(1)} %copy-done.6), custom_call_target="tpu_custom_call" | custom-call | tf_op jit(solution)/shard_map/regroup/pallas_call | solution.py:97
  16.2 3.3 %collective-permute-start.1 = (bf16[2048,128]{1,0:T(8,128)(2,1)S(1)}, bf16[2048,128]{1,0:T(8,128)(2,1)S(1)}, u32[]{:S(2)}, u32[]{:S(2)}) collective-permute-start(bf16[2048,128]{1,0:T(8,128)(2,1)S(1)} %get-tuple-element.12), channel_id=1, source_target_pairs={{0,64},{64,0},{1,65},{65,1},{2,66},{66,2},{3,67},{67,3},{4,68},{68... | collective-permute-start | bytes 1572872 | tf_op jit(solution)/shard_map/ppermute | solution.py:240
  19.5 8.4 %all-to-all-done.got_ref = bf16[4,448,128]{2,1,0:T(8,128)(2,1)S(1)} async-done(((bf16[4,448,128]{2,1,0:T(8,128)(2,1)}), bf16[4,448,128]{2,1,0:T(8,128)(2,1)S(1)}, u32[]{:S(2)}, u32[]{:S(2)}) %all-to-all-start) | async-done | bytes 458784 | tf_op jit(solution)/shard_map/all_to_all | solution.py:244
  27.9 1.2 %split.1 = bf16[8,608,128]{2,1,0:T(8,128)(2,1)} custom-call(bf16[4,448,128]{2,1,0:T(8,128)(2,1)S(1)} %all-to-all-done.got_ref), custom_call_target="tpu_custom_call" | custom-call | tf_op jit(solution)/shard_map/split/pallas_call | solution.py:23
  29.1 4.3 %all-to-all-start.1 = ((bf16[8,608,128]{2,1,0:T(8,128)(2,1)}), bf16[8,608,128]{2,1,0:T(8,128)(2,1)S(1)}, u32[]{:S(2)}, u32[]{:S(2)}) async-start(bf16[8,608,128]{2,1,0:T(8,128)(2,1)} %split.1), calls=%async_computation.1 | async-start | bytes 2490368 | tf_op jit(solution)/shard_map/all_to_all | solution.py:244
  33.6 4.6 %collective-permute-start.2 = (bf16[2048,128]{1,0:T(8,128)(2,1)S(1)}, bf16[2048,128]{1,0:T(8,128)(2,1)S(1)}, u32[]{:S(2)}, u32[]{:S(2)}) collective-permute-start(bf16[2048,128]{1,0:T(8,128)(2,1)S(1)} %add_convert_fusion.near_ref), channel_id=1, source_target_pairs={{0,32},{32,0},{1,33},{33,1},{2,34},{34,2},{3,35},{35,3},{4,36},{36... | collective-permute-start | bytes 1572872 | tf_op jit(solution)/shard_map/ppermute | solution.py:240
  38.1 12.6 %collective-permute-done.2.far_ref = bf16[2048,128]{1,0:T(8,128)(2,1)S(1)} collective-permute-done((bf16[2048,128]{1,0:T(8,128)(2,1)S(1)}, bf16[2048,128]{1,0:T(8,128)(2,1)S(1)}, u32[]{:S(2)}, u32[]{:S(2)}) %collective-permute-start.2) | collective-permute-done | bytes 524320 | tf_op jit(solution)/shard_map/ppermute | solution.py:240
  51.5 1.1 %repeat.1 = (bf16[4,44,24,128]{3,2,1,0:T(8,128)(2,1)}, bf16[2048,128]{1,0:T(8,128)(2,1)S(1)}) custom-call(bf16[8,608,128]{2,1,0:T(8,128)(2,1)S(1)} %all-to-all-done.1.one_ref.mine_ref, bf16[128,256]{1,0:T(8,128)(2,1)S(1)} %bitcast.18, s32[1,32]{1,0:T(1,128)S(1)} %copy-done.7, bf16[2048,128]{1,0:T(8,128)(2,1)S(1)} %add_convert_fusion.near_ref, ...), custom_call_target="tpu_custom_call" | custom-call | tf_op jit(solution)/shard_map/repeat/pallas_call | solution.py:23
  52.6 5.4 %all-to-all-start.2 = ((bf16[176,24,128]{2,1,0:T(8,128)(2,1)}), bf16[176,24,128]{2,1,0:T(8,128)(2,1)S(1)}, u32[]{:S(2)}, u32[]{:S(2)}) async-start(bf16[176,24,128]{2,1,0:T(8,128)(2,1)} %bitcast.6), calls=%async_computation.2 | async-start | bytes 2162688 | tf_op jit(solution)/shard_map/all_to_all | solution.py:244
  58.0 1.9 %collective-permute-start = (bf16[8,608,128]{2,1,0:T(8,128)(2,1)S(1)}, bf16[8,608,128]{2,1,0:T(8,128)(2,1)S(1)}, u32[]{:S(2)}, u32[]{:S(2)}) collective-permute-start(bf16[8,608,128]{2,1,0:T(8,128)(2,1)S(1)} %all-to-all-done.1.one_ref.mine_ref), channel_id=1, source_target_pairs={{0,1},{1,0},{2,3},{3,2},{4,5},{5,4},{6,7},{7,6},{8,9},{9,8},{10,11... | collective-permute-start | bytes 3735560 | tf_op jit(solution)/shard_map/ppermute | solution.py:240
  59.9 1.9 %collective-permute-start.3 = (bf16[2048,128]{1,0:T(8,128)(2,1)S(1)}, bf16[2048,128]{1,0:T(8,128)(2,1)}, u32[]{:S(2)}, u32[]{:S(2)}) collective-permute-start(bf16[2048,128]{1,0:T(8,128)(2,1)S(1)} %get-tuple-element.13.half_ref), channel_id=1, source_target_pairs={{0,64},{64,0},{1,65},{65,1},{2,66},{66,2},{3,67},{67,3},{4,68},{68... | collective-permute-start | bytes 1572872 | tf_op jit(solution)/shard_map/ppermute | solution.py:240
  62.8 1.1 copy-done
  63.9 7.5 %all-to-all-done.2 = bf16[176,24,128]{2,1,0:T(8,128)(2,1)S(1)} async-done(((bf16[176,24,128]{2,1,0:T(8,128)(2,1)}), bf16[176,24,128]{2,1,0:T(8,128)(2,1)S(1)}, u32[]{:S(2)}, u32[]{:S(2)}) %all-to-all-start.2) | async-done | bytes 1081376 | tf_op jit(solution)/shard_map/all_to_all | solution.py:244
  71.4 1.3 %copy-done.1 = bf16[8,608,128]{2,1,0:T(8,128)(2,1)S(1)} copy-done((bf16[8,608,128]{2,1,0:T(8,128)(2,1)S(1)}, bf16[8,608,128]{2,1,0:T(8,128)(2,1)}, u32[]{:S(2)}) %copy-start.1) | copy-done | bytes 1245208
  72.7 1.6 %right.1 = bf16[4,96,256]{2,1,0:T(8,128)(2,1)} custom-call(bf16[4,44,24,128]{3,2,1,0:T(8,128)(2,1)S(1)} %bitcast.12, bf16[8,608,128]{2,1,0:T(8,128)(2,1)S(1)} %all-to-all-done.1.one_ref.mine_ref, bf16[8,608,128]{2,1,0:T(8,128)(2,1)S(1)} %copy-done.1), custom_call_target="tpu_custom_call" | custom-call | tf_op jit(solution)/shard_map/right/pallas_call | solution.py:210
  74.3 5.3 %all-to-all-start.3 = ((bf16[4,96,256]{2,1,0:T(8,128)(2,1)}), bf16[4,96,256]{2,1,0:T(8,128)(2,1)S(1)}, u32[]{:S(2)}, u32[]{:S(2)}) async-start(bf16[4,96,256]{2,1,0:T(8,128)(2,1)} %right.1), calls=%async_computation.3 | async-start | bytes 393216 | tf_op jit(solution)/shard_map/all_to_all | solution.py:244
  79.7 1.3 %copy-done.2 = bf16[8,608,128]{2,1,0:T(8,128)(2,1)S(1)} copy-done((bf16[8,608,128]{2,1,0:T(8,128)(2,1)S(1)}, bf16[8,608,128]{2,1,0:T(8,128)(2,1)}, u32[]{:S(2)}) %copy-start.2) | copy-done | bytes 1245208
  81.0 2.6 %left_modes.1.after_ref.modes_ref = f32[96,256]{1,0:T(8,128)S(1)} custom-call(s32[4,32]{1,0:T(4,128)S(1)} %bitcast.19, s32[8,32]{1,0:T(8,128)S(1)} %copy-done.6, bf16[4,44,24,128]{3,2,1,0:T(8,128)(2,1)S(1)} %bitcast.14, bf16[8,608,128]{2,1,0:T(8,128)(2,1)S(1)} %all-to-all-done.1.one_ref.mine_ref, bf16[8,608,128]{2,1,0:T(8,128)(2,1)S(1)} %copy-done.2), custom_call_target="tpu_custom_call" | custom-call | tf_op jit(solution)/shard_map/left_modes/pallas_call | solution.py:210
  83.7 1.9 %left_stiff.1.stiff_ref = f32[128,256]{1,0:T(8,128)S(1)} custom-call(bf16[8,608,128]{2,1,0:T(8,128)(2,1)S(1)} %all-to-all-done.1.one_ref.mine_ref, bf16[8,608,128]{2,1,0:T(8,128)(2,1)S(1)} %copy-done.3, bf16[2048,128]{1,0:T(8,128)(2,1)S(1)} %get-tuple-element.13.half_ref, bf16[2048,128]{1,0:T(8,128)(2,1)} %collective-permute-done.3.other_half_ref, ...), custom_call_target="tpu_custom_call" | custom-call | tf_op jit(solution)/shard_map/left_stiff/pallas_call | solution.py:210
  86.1 1.9 %collective-permute-start.4 = (bf16[128,1024]{1,0:T(8,128)(2,1)S(1)}, bf16[128,1024]{1,0:T(8,128)(2,1)S(1)}, u32[]{:S(2)}, u32[]{:S(2)}) collective-permute-start(bf16[128,1024]{1,0:T(8,128)(2,1)S(1)} %get-tuple-element.16), channel_id=1, source_target_pairs={{0,1},{1,0},{2,3},{3,2},{4,5},{5,4},{6,7},{7,6},{8,9},{9,8},{10,11... | collective-permute-start | bytes 786440 | tf_op jit(solution)/shard_map/ppermute | solution.py:240
  88.0 1.5 %collective-permute-done.4 = bf16[128,1024]{1,0:T(8,128)(2,1)S(1)} collective-permute-done((bf16[128,1024]{1,0:T(8,128)(2,1)S(1)}, bf16[128,1024]{1,0:T(8,128)(2,1)S(1)}, u32[]{:S(2)}, u32[]{:S(2)}) %collective-permute-start.4) | collective-permute-done | bytes 262176 | tf_op jit(solution)/shard_map/ppermute | solution.py:240
  89.6 17.2 %all_to_all.26 = bf16[16,8,1024]{2,1,0:T(8,128)(2,1)S(1)} all-to-all(bf16[16,8,1024]{2,1,0:T(8,128)(2,1)S(1)} %fusion), channel_id=1, replica_groups=mesh['g'=4,'b'=2,'a'=2,'z'=4,'x'=4,'c'=2] {'z','x'}, dimensions={0} | all-to-all | bytes 524288 | tf_op jit(solution)/shard_map/all_to_all | solution.py:244
  (23 shorter events, 3.1 us)
Async XLA Ops:
  0.0 13.9 %copy-start.4 = (bf16[1,4096,128]{2,1,0:T(8,128)(2,1)S(1)}, bf16[1,4096,128]{2,1,0:T(8,128)(2,1)}, u32[]{:S(2)}) copy-start(bf16[1,4096,128]{2,1,0:T(8,128)(2,1)} %param.10) | copy-start | bytes 3145732
  0.0 13.9 %copy-start.6 = (s32[8,32]{1,0:T(8,128)S(1)}, s32[8,32]{1,0:T(8,128)}, u32[]{:S(2)}) copy-start(s32[8,32]{1,0:T(8,128)} %pmaps_ref.1) | copy-start | bytes 3076
  0.0 13.9 %copy-start.7 = (s32[1,32]{1,0:T(1,128)S(1)}, s32[1,32]{1,0:T(1,128)}, u32[]{:S(2)}) copy-start(s32[1,32]{1,0:T(1,128)} %row_ref.1) | copy-start | bytes 388
  3.6 24.3 %all-to-all-start = ((bf16[4,448,128]{2,1,0:T(8,128)(2,1)}), bf16[4,448,128]{2,1,0:T(8,128)(2,1)S(1)}, u32[]{:S(2)}, u32[]{:S(2)}) async-start(bf16[4,448,128]{2,1,0:T(8,128)(2,1)} %coupling.1), calls=%async_computation | async-start | bytes 917504 | tf_op jit(solution)/shard_map/all_to_all | solution.py:244
  16.2 17.2 %collective-permute-start.1 = (bf16[2048,128]{1,0:T(8,128)(2,1)S(1)}, bf16[2048,128]{1,0:T(8,128)(2,1)S(1)}, u32[]{:S(2)}, u32[]{:S(2)}) collective-permute-start(bf16[2048,128]{1,0:T(8,128)(2,1)S(1)} %get-tuple-element.12), channel_id=1, source_target_pairs={{0,64},{64,0},{1,65},{65,1},{2,66},{66,2},{3,67},{67,3},{4,68},{68... | collective-permute-start | bytes 1572872 | tf_op jit(solution)/shard_map/ppermute | solution.py:240
  29.1 22.4 %all-to-all-start.1 = ((bf16[8,608,128]{2,1,0:T(8,128)(2,1)}), bf16[8,608,128]{2,1,0:T(8,128)(2,1)S(1)}, u32[]{:S(2)}, u32[]{:S(2)}) async-start(bf16[8,608,128]{2,1,0:T(8,128)(2,1)} %split.1), calls=%async_computation.1 | async-start | bytes 2490368 | tf_op jit(solution)/shard_map/all_to_all | solution.py:244
  33.4 18.1 %copy-start.5 = (bf16[1,128,256]{2,1,0:T(8,128)(2,1)S(1)}, bf16[1,128,256]{2,1,0:T(8,128)(2,1)}, u32[]{:S(2)}) copy-start(bf16[1,128,256]{2,1,0:T(8,128)(2,1)} %param.19) | copy-start | bytes 196612
  33.6 17.1 %collective-permute-start.2 = (bf16[2048,128]{1,0:T(8,128)(2,1)S(1)}, bf16[2048,128]{1,0:T(8,128)(2,1)S(1)}, u32[]{:S(2)}, u32[]{:S(2)}) collective-permute-start(bf16[2048,128]{1,0:T(8,128)(2,1)S(1)} %add_convert_fusion.near_ref), channel_id=1, source_target_pairs={{0,32},{32,0},{1,33},{33,1},{2,34},{34,2},{3,35},{35,3},{4,36},{36... | collective-permute-start | bytes 1572872 | tf_op jit(solution)/shard_map/ppermute | solution.py:240
  52.6 18.8 %all-to-all-start.2 = ((bf16[176,24,128]{2,1,0:T(8,128)(2,1)}), bf16[176,24,128]{2,1,0:T(8,128)(2,1)S(1)}, u32[]{:S(2)}, u32[]{:S(2)}) async-start(bf16[176,24,128]{2,1,0:T(8,128)(2,1)} %bitcast.6), calls=%async_computation.2 | async-start | bytes 2162688 | tf_op jit(solution)/shard_map/all_to_all | solution.py:244
  58.0 4.8 %collective-permute-start = (bf16[8,608,128]{2,1,0:T(8,128)(2,1)S(1)}, bf16[8,608,128]{2,1,0:T(8,128)(2,1)S(1)}, u32[]{:S(2)}, u32[]{:S(2)}) collective-permute-start(bf16[8,608,128]{2,1,0:T(8,128)(2,1)S(1)} %all-to-all-done.1.one_ref.mine_ref), channel_id=1, source_target_pairs={{0,1},{1,0},{2,3},{3,2},{4,5},{5,4},{6,7},{7,6},{8,9},{9,8},{10,11... | collective-permute-start | bytes 3735560 | tf_op jit(solution)/shard_map/ppermute | solution.py:240
  59.9 23.7 %collective-permute-start.3 = (bf16[2048,128]{1,0:T(8,128)(2,1)S(1)}, bf16[2048,128]{1,0:T(8,128)(2,1)}, u32[]{:S(2)}, u32[]{:S(2)}) collective-permute-start(bf16[2048,128]{1,0:T(8,128)(2,1)S(1)} %get-tuple-element.13.half_ref), channel_id=1, source_target_pairs={{0,64},{64,0},{1,65},{65,1},{2,66},{66,2},{3,67},{67,3},{4,68},{68... | collective-permute-start | bytes 1572872 | tf_op jit(solution)/shard_map/ppermute | solution.py:240
  62.8 1.1 copy-start
  71.4 1.3 %copy-start.1 = (bf16[8,608,128]{2,1,0:T(8,128)(2,1)S(1)}, bf16[8,608,128]{2,1,0:T(8,128)(2,1)}, u32[]{:S(2)}) copy-start(bf16[8,608,128]{2,1,0:T(8,128)(2,1)} %copy-done) | copy-start | bytes 3735556
  74.3 11.3 %all-to-all-start.3 = ((bf16[4,96,256]{2,1,0:T(8,128)(2,1)}), bf16[4,96,256]{2,1,0:T(8,128)(2,1)S(1)}, u32[]{:S(2)}, u32[]{:S(2)}) async-start(bf16[4,96,256]{2,1,0:T(8,128)(2,1)} %right.1), calls=%async_computation.3 | async-start | bytes 393216 | tf_op jit(solution)/shard_map/all_to_all | solution.py:244
  79.7 1.3 %copy-start.2 = (bf16[8,608,128]{2,1,0:T(8,128)(2,1)S(1)}, bf16[8,608,128]{2,1,0:T(8,128)(2,1)}, u32[]{:S(2)}) copy-start(bf16[8,608,128]{2,1,0:T(8,128)(2,1)} %copy-done) | copy-start | bytes 3735556
  81.0 2.7 %copy-start.3 = (bf16[8,608,128]{2,1,0:T(8,128)(2,1)S(1)}, bf16[8,608,128]{2,1,0:T(8,128)(2,1)}, u32[]{:S(2)}) copy-start(bf16[8,608,128]{2,1,0:T(8,128)(2,1)} %copy-done) | copy-start | bytes 3735556
  86.1 3.4 %collective-permute-start.4 = (bf16[128,1024]{1,0:T(8,128)(2,1)S(1)}, bf16[128,1024]{1,0:T(8,128)(2,1)S(1)}, u32[]{:S(2)}, u32[]{:S(2)}) collective-permute-start(bf16[128,1024]{1,0:T(8,128)(2,1)S(1)} %get-tuple-element.16), channel_id=1, source_target_pairs={{0,1},{1,0},{2,3},{3,2},{4,5},{5,4},{6,7},{7,6},{8,9},{9,8},{10,11... | collective-permute-start | bytes 786440 | tf_op jit(solution)/shard_map/ppermute | solution.py:240

commit v4 on v3

--- a/solution.py
+++ b/solution.py
@@ -132,18 +132,12 @@
     return lax.rem(panel, 8) * 4 + panel // 8
 
 
-def fetch(source_ref, held_ref, sem):
-    copy = pltpu.make_async_copy(source_ref, held_ref, sem)
-    copy.start()
-    return copy
-
-
-def times_basis(left_ref, mine_ref, held_ref):
+def times_basis(left_ref, mine_ref, other_ref):
     total = jnp.zeros((left_ref.shape[1], 256), F32)
     for k in range(8):
         for h in (0, 1):
             rows = pl.ds(96 + 256 * h, 256)
-            block = jnp.concatenate([mine_ref[k, rows, :], held_ref[k, rows, :]], axis=1)
+            block = jnp.concatenate([mine_ref[k, rows, :], other_ref[k, rows, :]], axis=1)
             total = total + dot(left_ref[2 * k + h], block)
     return total
 
@@ -154,19 +148,16 @@
         ref[(*at, lanes)] = total[:, 128 * half : 128 * (half + 1)]
 
 
-def right_body(col_ref, mine_ref, other_ref, out_ref, held_ref, left_ref, sem):
-    copy = fetch(other_ref, held_ref, sem)
+def right_body(col_ref, mine_ref, other_ref, out_ref, left_ref):
     for n in range(16):
         cols = [col_ref[:, 2 * n + s].astype(F32).reshape(96, 128) for s in (0, 1)]
         left_ref[n] = jnp.concatenate(cols, axis=1).astype(BF16)
-    copy.wait()
-    total = times_basis(left_ref, mine_ref, held_ref).astype(BF16)
+    total = times_basis(left_ref, mine_ref, other_ref).astype(BF16)
     for q in range(4):
         in_order(total, out_ref, q, slice(None))
 
 
-def left_modes_body(cmaps_ref, pmaps_ref, col_ref, mine_ref, other_ref, out_ref, held_ref, left_ref, sem):
-    copy = fetch(other_ref, held_ref, sem)
+def left_modes_body(cmaps_ref, pmaps_ref, col_ref, mine_ref, other_ref, out_ref, left_ref):
     first = 2 * lax.axis_index("g")
     for n in range(16):
         pair = []
@@ -179,11 +170,10 @@
                 for_leaf.append(col_ref[leaf, column_index(row)].astype(F32)[16:])
             pair.append(jnp.concatenate(for_leaf, axis=0))
         left_ref[n] = jnp.concatenate(pair, axis=1).astype(BF16)
-    copy.wait()
-    in_order(-times_basis(left_ref, mine_ref, held_ref), out_ref, slice(None))
-
-
-def left_stiff_body(mine_ref, other_ref, half_ref, other_half_ref, after_ref, out_ref, low, high, held_ref, left_ref, sems):
+    in_order(-times_basis(left_ref, mine_ref, other_ref), out_ref, slice(None))
+
+
+def left_stiff_body(mine_ref, other_ref, half_ref, other_half_ref, after_ref, out_ref, low, high, left_ref, sems):
     b = lax.axis_index("b")
     for k, ref in enumerate((half_ref, other_half_ref)):
         for value, rows in enumerate((low, high)):
@@ -192,18 +182,13 @@
             def _(ref=ref, rows=rows, k=k):
                 pltpu.make_async_copy(ref, rows, sems.at[k]).start()
 
-    copy = fetch(other_ref, held_ref, sems.at[2])
     for k in (0, 1):
         pltpu.make_async_copy(half_ref, low, sems.at[k]).wait()
     for n in range(16):
         part = (low, high)[n % 2]
         rows = [part[pl.ds(128 * (8 * s + n // 2), 128), :].astype(F32).T for s in (0, 1)]
         left_ref[n] = jnp.concatenate(rows, axis=1).astype(BF16)
-    copy.wait()
-    in_order(times_basis(left_ref, mine_ref, held_ref), out_ref, slice(None))
-
-
-HELD = pltpu.VMEM((8, 608, 128), BF16)
+    in_order(times_basis(left_ref, mine_ref, other_ref), out_ref, slice(None))
 
 
 def project(body, out, dtype, specs, scratch, name, *args):
@@ -275,19 +260,18 @@
     columns = exchange(copies.reshape(176, 24, 128), LEAF).reshape(4, 44, 24, 128)
 
     modes_left = pltpu.VMEM((16, 96, 256), BF16)
-    one_sem = pltpu.SemaphoreType.DMA(())
     right = project(
-        right_body, (4, 96, 256), BF16, [VM, VM, ANY], [HELD, modes_left, one_sem], "right", columns, mine, other
+        right_body, (4, 96, 256), BF16, [VM, VM, VM], [modes_left], "right", columns, mine, other
     )
     right = exchange(right.reshape(384, 256), LEAF).reshape(4, 96, 256)
     child_maps = columns[:, 42, 16, :32].astype(jnp.int32)
     modes = project(
-        left_modes_body, (96, 256), F32, [SM, SM, VM, VM, ANY], [HELD, modes_left, one_sem], "left_modes",
+        left_modes_body, (96, 256), F32, [SM, SM, VM, VM, VM], [modes_left], "left_modes",
         child_maps, parent_map, columns, mine, other,
     )
     stiff = project(
-        left_stiff_body, (128, 256), F32, [VM, ANY, ANY, ANY, ANY],
-        [pltpu.VMEM((2048, 128), BF16)] * 2 + [HELD, pltpu.VMEM((16, 128, 256), BF16), pltpu.SemaphoreType.DMA((3,))],
+        left_stiff_body, (128, 256), F32, [VM, VM, ANY, ANY, ANY],
+        [pltpu.VMEM((2048, 128), BF16)] * 2 + [pltpu.VMEM((16, 128, 256), BF16), pltpu.SemaphoreType.DMA((2,))],
         "left_stiff", mine, other, half, other_half, modes,
     )
     kept, sent = pl.pallas_call(

time: 108 us -> 107 us (level)
  Pallas kernels: 14.9 us -> 13.5 us
    pallas_call x3, Pallas kernels: 6.21 us -> 4.81 us  [project(): pl.pallas_call(body, out_shape=jax.ShapeDtypeStruct(out, dtype), in_specs...]
  transfers between devices with their start and end apart: 9 -> 9, of which waited for: 6 -> 7; matrix products, arithmetic and copies ran while one was open for 0% -> 0% of each run, Pallas kernels for 9% -> 8%
where the time goes in v4:
time: 107 us; the launch traced here: 106 us
  starting transfers between devices  38.9 us (36%)
  waiting for transfers between devices  32.3 us (30%)
  blocking collectives  16.7 us (16%)
  Pallas kernels  13.5 us (13%)
  local copies, waits for them, and re-layouts  3.66 us (3%)
    all_to_all x4, starting transfers between devices, exchange(): return lax.all_to_all(value, axis, 0, 0, tiled=True)  25.3 us
    all_to_all x4, waiting for transfers between devices, exchange(): return lax.all_to_all(value, axis, 0, 0, tiled=True)  17.2 us
    all_to_all x1, blocking collectives, exchange(): return lax.all_to_all(value, axis, 0, 0, tiled=True)  16.7 us
    ppermute x5, waiting for transfers between devices, swap(): return lax.ppermute(value, axis, [(i, i ^ mask) for i in range(size)])  15.1 us
    ppermute x5, starting transfers between devices, swap(): return lax.ppermute(value, axis, [(i, i ^ mask) for i in range(size)])  13.6 us
    pallas_call x3, Pallas kernels, project(): pl.pallas_call(body, out_shape=jax.ShapeDtypeStruct(out, dtype), in_specs...  4.81 us
    unnamed x16, local copies, waits for them, and re-layouts  3.66 us
    pallas_call x1, Pallas kernels, couple(): pl.pallas_call(coupling_body, grid=(steps,), out_shape=jax.ShapeDtypeStru...  3.56 us
  transfers between devices with their start and end apart: 9, of which 7 were waited for; matrix products, arithmetic and copies ran while one was open for 0% of the time, Pallas kernels for 8%

profile of v4, /device:TPU:56, one launch (start us, length us, event | category | flops | bytes accessed | tf_op | source)
XLA Modules:
  0.0 106.0 jit_solution(4897859911790217763)
XLA Ops:
  0.0 3.6 %coupling.1 = bf16[4,448,128]{2,1,0:T(8,128)(2,1)} custom-call(bf16[2048,512]{1,0:T(8,128)(2,1)} %bitcast.20, bf16[128,2048]{1,0:T(8,128)(2,1)} %bitcast.22, f32[1,512]{1,0:T(1,128)} %ce_ref.1, bf16[2048,256]{1,0:T(8,128)(2,1)} %bitcast.21, bf16[128,2048]{1,0:T(8,128)(2,1)} %bitcast.23, f32[1,256]{1,0:T(1,128)} %pe_ref.1, bf16[128,256]{1,0:T(8,128)(2,1)} %bitcast.17), custom_call_target="tpu_custom_call" | custom-call | tf_op jit(solution)/shard_map/coupling/pallas_call | solution.py:70
  3.6 10.3 %all-to-all-start = ((bf16[4,448,128]{2,1,0:T(8,128)(2,1)}), bf16[4,448,128]{2,1,0:T(8,128)(2,1)S(1)}, u32[]{:S(2)}, u32[]{:S(2)}) async-start(bf16[4,448,128]{2,1,0:T(8,128)(2,1)} %coupling.1), calls=%async_computation | async-start | bytes 917504 | tf_op jit(solution)/shard_map/all_to_all | solution.py:229
  13.9 2.3 %regroup.1 = (bf16[2048,128]{1,0:T(8,128)(2,1)S(1)}, bf16[2048,128]{1,0:T(8,128)(2,1)S(1)}) custom-call(bf16[4096,128]{1,0:T(8,128)(2,1)S(1)} %bitcast.16, s32[1,32]{1,0:T(1,128)S(1)} %copy-done.7, s32[8,32]{1,0:T(8,128)S(1)} %copy-done.6), custom_call_target="tpu_custom_call" | custom-call | tf_op jit(solution)/shard_map/regroup/pallas_call | solution.py:97
  16.2 3.3 %collective-permute-start.1 = (bf16[2048,128]{1,0:T(8,128)(2,1)S(1)}, bf16[2048,128]{1,0:T(8,128)(2,1)S(1)}, u32[]{:S(2)}, u32[]{:S(2)}) collective-permute-start(bf16[2048,128]{1,0:T(8,128)(2,1)S(1)} %get-tuple-element.12), channel_id=1, source_target_pairs={{0,64},{64,0},{1,65},{65,1},{2,66},{66,2},{3,67},{67,3},{4,68},{68... | collective-permute-start | bytes 1572872 | tf_op jit(solution)/shard_map/ppermute | solution.py:225
  19.5 8.4 %all-to-all-done.got_ref = bf16[4,448,128]{2,1,0:T(8,128)(2,1)S(1)} async-done(((bf16[4,448,128]{2,1,0:T(8,128)(2,1)}), bf16[4,448,128]{2,1,0:T(8,128)(2,1)S(1)}, u32[]{:S(2)}, u32[]{:S(2)}) %all-to-all-start) | async-done | bytes 458784 | tf_op jit(solution)/shard_map/all_to_all | solution.py:229
  27.9 1.2 %split.1 = bf16[8,608,128]{2,1,0:T(8,128)(2,1)} custom-call(bf16[4,448,128]{2,1,0:T(8,128)(2,1)S(1)} %all-to-all-done.got_ref), custom_call_target="tpu_custom_call" | custom-call | tf_op jit(solution)/shard_map/split/pallas_call | solution.py:23
  29.1 4.3 %all-to-all-start.1 = ((bf16[8,608,128]{2,1,0:T(8,128)(2,1)}), bf16[8,608,128]{2,1,0:T(8,128)(2,1)S(1)}, u32[]{:S(2)}, u32[]{:S(2)}) async-start(bf16[8,608,128]{2,1,0:T(8,128)(2,1)} %split.1), calls=%async_computation.1 | async-start | bytes 2490368 | tf_op jit(solution)/shard_map/all_to_all | solution.py:229
  33.6 4.6 %collective-permute-start.2 = (bf16[2048,128]{1,0:T(8,128)(2,1)S(1)}, bf16[2048,128]{1,0:T(8,128)(2,1)S(1)}, u32[]{:S(2)}, u32[]{:S(2)}) collective-permute-start(bf16[2048,128]{1,0:T(8,128)(2,1)S(1)} %add_convert_fusion.near_ref), channel_id=1, source_target_pairs={{0,32},{32,0},{1,33},{33,1},{2,34},{34,2},{3,35},{35,3},{4,36},{36... | collective-permute-start | bytes 1572872 | tf_op jit(solution)/shard_map/ppermute | solution.py:225
  38.1 12.6 %collective-permute-done.2.far_ref = bf16[2048,128]{1,0:T(8,128)(2,1)S(1)} collective-permute-done((bf16[2048,128]{1,0:T(8,128)(2,1)S(1)}, bf16[2048,128]{1,0:T(8,128)(2,1)S(1)}, u32[]{:S(2)}, u32[]{:S(2)}) %collective-permute-start.2) | collective-permute-done | bytes 524320 | tf_op jit(solution)/shard_map/ppermute | solution.py:225
  51.5 1.1 %repeat.1 = (bf16[4,44,24,128]{3,2,1,0:T(8,128)(2,1)}, bf16[2048,128]{1,0:T(8,128)(2,1)S(1)}) custom-call(bf16[8,608,128]{2,1,0:T(8,128)(2,1)S(1)} %all-to-all-done.1.one_ref.mine_ref, bf16[128,256]{1,0:T(8,128)(2,1)S(1)} %bitcast.18, s32[1,32]{1,0:T(1,128)S(1)} %copy-done.7, bf16[2048,128]{1,0:T(8,128)(2,1)S(1)} %add_convert_fusion.near_ref, ...), custom_call_target="tpu_custom_call" | custom-call | tf_op jit(solution)/shard_map/repeat/pallas_call | solution.py:23
  52.6 5.4 %all-to-all-start.2 = ((bf16[176,24,128]{2,1,0:T(8,128)(2,1)}), bf16[176,24,128]{2,1,0:T(8,128)(2,1)S(1)}, u32[]{:S(2)}, u32[]{:S(2)}) async-start(bf16[176,24,128]{2,1,0:T(8,128)(2,1)} %bitcast.6), calls=%async_computation.2 | async-start | bytes 2162688 | tf_op jit(solution)/shard_map/all_to_all | solution.py:229
  58.0 1.9 %collective-permute-start = (bf16[8,608,128]{2,1,0:T(8,128)(2,1)S(1)}, bf16[8,608,128]{2,1,0:T(8,128)(2,1)S(1)}, u32[]{:S(2)}, u32[]{:S(2)}) collective-permute-start(bf16[8,608,128]{2,1,0:T(8,128)(2,1)S(1)} %all-to-all-done.1.one_ref.mine_ref), channel_id=1, source_target_pairs={{0,1},{1,0},{2,3},{3,2},{4,5},{5,4},{6,7},{7,6},{8,9},{9,8},{10,11... | collective-permute-start | bytes 3735560 | tf_op jit(solution)/shard_map/ppermute | solution.py:225
  59.9 1.9 %collective-permute-start.3 = (bf16[2048,128]{1,0:T(8,128)(2,1)S(1)}, bf16[2048,128]{1,0:T(8,128)(2,1)}, u32[]{:S(2)}, u32[]{:S(2)}) collective-permute-start(bf16[2048,128]{1,0:T(8,128)(2,1)S(1)} %get-tuple-element.13.half_ref), channel_id=1, source_target_pairs={{0,64},{64,0},{1,65},{65,1},{2,66},{66,2},{3,67},{67,3},{4,68},{68... | collective-permute-start | bytes 1572872 | tf_op jit(solution)/shard_map/ppermute | solution.py:225
  62.8 1.1 copy-done
  63.9 7.5 %all-to-all-done.2 = bf16[176,24,128]{2,1,0:T(8,128)(2,1)S(1)} async-done(((bf16[176,24,128]{2,1,0:T(8,128)(2,1)}), bf16[176,24,128]{2,1,0:T(8,128)(2,1)S(1)}, u32[]{:S(2)}, u32[]{:S(2)}) %all-to-all-start.2) | async-done | bytes 1081376 | tf_op jit(solution)/shard_map/all_to_all | solution.py:229
  71.4 1.3 %copy-done.1 = bf16[8,608,128]{2,1,0:T(8,128)(2,1)S(1)} copy-done((bf16[8,608,128]{2,1,0:T(8,128)(2,1)S(1)}, bf16[8,608,128]{2,1,0:T(8,128)(2,1)}, u32[]{:S(2)}) %copy-start.1) | copy-done | bytes 1245208
  72.7 1.2 %right.1 = bf16[4,96,256]{2,1,0:T(8,128)(2,1)} custom-call(bf16[4,44,24,128]{3,2,1,0:T(8,128)(2,1)S(1)} %bitcast.12, bf16[8,608,128]{2,1,0:T(8,128)(2,1)S(1)} %all-to-all-done.1.one_ref.mine_ref, bf16[8,608,128]{2,1,0:T(8,128)(2,1)S(1)} %copy-done.1), custom_call_target="tpu_custom_call" | custom-call | tf_op jit(solution)/shard_map/right/pallas_call | solution.py:195
  73.9 5.3 %all-to-all-start.3 = ((bf16[4,96,256]{2,1,0:T(8,128)(2,1)}), bf16[4,96,256]{2,1,0:T(8,128)(2,1)S(1)}, u32[]{:S(2)}, u32[]{:S(2)}) async-start(bf16[4,96,256]{2,1,0:T(8,128)(2,1)} %right.1), calls=%async_computation.3 | async-start | bytes 393216 | tf_op jit(solution)/shard_map/all_to_all | solution.py:229
  79.2 1.3 %copy-done.2 = bf16[8,608,128]{2,1,0:T(8,128)(2,1)S(1)} copy-done((bf16[8,608,128]{2,1,0:T(8,128)(2,1)S(1)}, bf16[8,608,128]{2,1,0:T(8,128)(2,1)}, u32[]{:S(2)}) %copy-start.2) | copy-done | bytes 1245208
  80.5 2.0 %left_modes.1.after_ref.modes_ref = f32[96,256]{1,0:T(8,128)S(1)} custom-call(s32[4,32]{1,0:T(4,128)S(1)} %bitcast.19, s32[8,32]{1,0:T(8,128)S(1)} %copy-done.6, bf16[4,44,24,128]{3,2,1,0:T(8,128)(2,1)S(1)} %bitcast.14, bf16[8,608,128]{2,1,0:T(8,128)(2,1)S(1)} %all-to-all-done.1.one_ref.mine_ref, bf16[8,608,128]{2,1,0:T(8,128)(2,1)S(1)} %copy-done.2), custom_call_target="tpu_custom_call" | custom-call | tf_op jit(solution)/shard_map/left_modes/pallas_call | solution.py:195
  82.5 1.7 %left_stiff.1.stiff_ref = f32[128,256]{1,0:T(8,128)S(1)} custom-call(bf16[8,608,128]{2,1,0:T(8,128)(2,1)S(1)} %all-to-all-done.1.one_ref.mine_ref, bf16[8,608,128]{2,1,0:T(8,128)(2,1)S(1)} %copy-done.3, bf16[2048,128]{1,0:T(8,128)(2,1)S(1)} %get-tuple-element.13.half_ref, bf16[2048,128]{1,0:T(8,128)(2,1)} %collective-permute-done.3.other_half_ref, ...), custom_call_target="tpu_custom_call" | custom-call | tf_op jit(solution)/shard_map/left_stiff/pallas_call | solution.py:195
  85.1 1.9 %collective-permute-start.4 = (bf16[128,1024]{1,0:T(8,128)(2,1)S(1)}, bf16[128,1024]{1,0:T(8,128)(2,1)S(1)}, u32[]{:S(2)}, u32[]{:S(2)}) collective-permute-start(bf16[128,1024]{1,0:T(8,128)(2,1)S(1)} %get-tuple-element.16), channel_id=1, source_target_pairs={{0,1},{1,0},{2,3},{3,2},{4,5},{5,4},{6,7},{7,6},{8,9},{9,8},{10,11... | collective-permute-start | bytes 786440 | tf_op jit(solution)/shard_map/ppermute | solution.py:225
  87.1 1.5 %collective-permute-done.4 = bf16[128,1024]{1,0:T(8,128)(2,1)S(1)} collective-permute-done((bf16[128,1024]{1,0:T(8,128)(2,1)S(1)}, bf16[128,1024]{1,0:T(8,128)(2,1)S(1)}, u32[]{:S(2)}, u32[]{:S(2)}) %collective-permute-start.4) | collective-permute-done | bytes 262176 | tf_op jit(solution)/shard_map/ppermute | solution.py:225
  88.6 16.7 %all_to_all.26 = bf16[16,8,1024]{2,1,0:T(8,128)(2,1)S(1)} all-to-all(bf16[16,8,1024]{2,1,0:T(8,128)(2,1)S(1)} %fusion), channel_id=1, replica_groups=mesh['g'=4,'b'=2,'a'=2,'z'=4,'x'=4,'c'=2] {'z','x'}, dimensions={0} | all-to-all | bytes 524288 | tf_op jit(solution)/shard_map/all_to_all | solution.py:229
  (23 shorter events, 3.6 us)
Async XLA Ops:
  0.0 13.9 %copy-start.4 = (bf16[1,4096,128]{2,1,0:T(8,128)(2,1)S(1)}, bf16[1,4096,128]{2,1,0:T(8,128)(2,1)}, u32[]{:S(2)}) copy-start(bf16[1,4096,128]{2,1,0:T(8,128)(2,1)} %param.10) | copy-start | bytes 3145732
  0.0 13.9 %copy-start.6 = (s32[8,32]{1,0:T(8,128)S(1)}, s32[8,32]{1,0:T(8,128)}, u32[]{:S(2)}) copy-start(s32[8,32]{1,0:T(8,128)} %pmaps_ref.1) | copy-start | bytes 3076
  0.0 13.9 %copy-start.7 = (s32[1,32]{1,0:T(1,128)S(1)}, s32[1,32]{1,0:T(1,128)}, u32[]{:S(2)}) copy-start(s32[1,32]{1,0:T(1,128)} %row_ref.1) | copy-start | bytes 388
  3.6 24.3 %all-to-all-start = ((bf16[4,448,128]{2,1,0:T(8,128)(2,1)}), bf16[4,448,128]{2,1,0:T(8,128)(2,1)S(1)}, u32[]{:S(2)}, u32[]{:S(2)}) async-start(bf16[4,448,128]{2,1,0:T(8,128)(2,1)} %coupling.1), calls=%async_computation | async-start | bytes 917504 | tf_op jit(solution)/shard_map/all_to_all | solution.py:229
  16.2 17.2 %collective-permute-start.1 = (bf16[2048,128]{1,0:T(8,128)(2,1)S(1)}, bf16[2048,128]{1,0:T(8,128)(2,1)S(1)}, u32[]{:S(2)}, u32[]{:S(2)}) collective-permute-start(bf16[2048,128]{1,0:T(8,128)(2,1)S(1)} %get-tuple-element.12), channel_id=1, source_target_pairs={{0,64},{64,0},{1,65},{65,1},{2,66},{66,2},{3,67},{67,3},{4,68},{68... | collective-permute-start | bytes 1572872 | tf_op jit(solution)/shard_map/ppermute | solution.py:225
  29.1 22.4 %all-to-all-start.1 = ((bf16[8,608,128]{2,1,0:T(8,128)(2,1)}), bf16[8,608,128]{2,1,0:T(8,128)(2,1)S(1)}, u32[]{:S(2)}, u32[]{:S(2)}) async-start(bf16[8,608,128]{2,1,0:T(8,128)(2,1)} %split.1), calls=%async_computation.1 | async-start | bytes 2490368 | tf_op jit(solution)/shard_map/all_to_all | solution.py:229
  33.4 18.1 %copy-start.5 = (bf16[1,128,256]{2,1,0:T(8,128)(2,1)S(1)}, bf16[1,128,256]{2,1,0:T(8,128)(2,1)}, u32[]{:S(2)}) copy-start(bf16[1,128,256]{2,1,0:T(8,128)(2,1)} %param.19) | copy-start | bytes 196612
  33.6 17.1 %collective-permute-start.2 = (bf16[2048,128]{1,0:T(8,128)(2,1)S(1)}, bf16[2048,128]{1,0:T(8,128)(2,1)S(1)}, u32[]{:S(2)}, u32[]{:S(2)}) collective-permute-start(bf16[2048,128]{1,0:T(8,128)(2,1)S(1)} %add_convert_fusion.near_ref), channel_id=1, source_target_pairs={{0,32},{32,0},{1,33},{33,1},{2,34},{34,2},{3,35},{35,3},{4,36},{36... | collective-permute-start | bytes 1572872 | tf_op jit(solution)/shard_map/ppermute | solution.py:225
  52.6 18.8 %all-to-all-start.2 = ((bf16[176,24,128]{2,1,0:T(8,128)(2,1)}), bf16[176,24,128]{2,1,0:T(8,128)(2,1)S(1)}, u32[]{:S(2)}, u32[]{:S(2)}) async-start(bf16[176,24,128]{2,1,0:T(8,128)(2,1)} %bitcast.6), calls=%async_computation.2 | async-start | bytes 2162688 | tf_op jit(solution)/shard_map/all_to_all | solution.py:229
  58.0 4.8 %collective-permute-start = (bf16[8,608,128]{2,1,0:T(8,128)(2,1)S(1)}, bf16[8,608,128]{2,1,0:T(8,128)(2,1)S(1)}, u32[]{:S(2)}, u32[]{:S(2)}) collective-permute-start(bf16[8,608,128]{2,1,0:T(8,128)(2,1)S(1)} %all-to-all-done.1.one_ref.mine_ref), channel_id=1, source_target_pairs={{0,1},{1,0},{2,3},{3,2},{4,5},{5,4},{6,7},{7,6},{8,9},{9,8},{10,11... | collective-permute-start | bytes 3735560 | tf_op jit(solution)/shard_map/ppermute | solution.py:225
  59.9 22.6 %collective-permute-start.3 = (bf16[2048,128]{1,0:T(8,128)(2,1)S(1)}, bf16[2048,128]{1,0:T(8,128)(2,1)}, u32[]{:S(2)}, u32[]{:S(2)}) collective-permute-start(bf16[2048,128]{1,0:T(8,128)(2,1)S(1)} %get-tuple-element.13.half_ref), channel_id=1, source_target_pairs={{0,64},{64,0},{1,65},{65,1},{2,66},{66,2},{3,67},{67,3},{4,68},{68... | collective-permute-start | bytes 1572872 | tf_op jit(solution)/shard_map/ppermute | solution.py:225
  62.8 1.1 copy-start
  71.4 1.3 %copy-start.1 = (bf16[8,608,128]{2,1,0:T(8,128)(2,1)S(1)}, bf16[8,608,128]{2,1,0:T(8,128)(2,1)}, u32[]{:S(2)}) copy-start(bf16[8,608,128]{2,1,0:T(8,128)(2,1)} %copy-done) | copy-start | bytes 3735556
  73.9 10.8 %all-to-all-start.3 = ((bf16[4,96,256]{2,1,0:T(8,128)(2,1)}), bf16[4,96,256]{2,1,0:T(8,128)(2,1)S(1)}, u32[]{:S(2)}, u32[]{:S(2)}) async-start(bf16[4,96,256]{2,1,0:T(8,128)(2,1)} %right.1), calls=%async_computation.3 | async-start | bytes 393216 | tf_op jit(solution)/shard_map/all_to_all | solution.py:229
  79.2 1.3 %copy-start.2 = (bf16[8,608,128]{2,1,0:T(8,128)(2,1)S(1)}, bf16[8,608,128]{2,1,0:T(8,128)(2,1)}, u32[]{:S(2)}) copy-start(bf16[8,608,128]{2,1,0:T(8,128)(2,1)} %copy-done) | copy-start | bytes 3735556
  80.5 2.0 %copy-start.3 = (bf16[8,608,128]{2,1,0:T(8,128)(2,1)S(1)}, bf16[8,608,128]{2,1,0:T(8,128)(2,1)}, u32[]{:S(2)}) copy-start(bf16[8,608,128]{2,1,0:T(8,128)(2,1)} %copy-done) | copy-start | bytes 3735556
  85.1 3.4 %collective-permute-start.4 = (bf16[128,1024]{1,0:T(8,128)(2,1)S(1)}, bf16[128,1024]{1,0:T(8,128)(2,1)S(1)}, u32[]{:S(2)}, u32[]{:S(2)}) collective-permute-start(bf16[128,1024]{1,0:T(8,128)(2,1)S(1)} %get-tuple-element.16), channel_id=1, source_target_pairs={{0,1},{1,0},{2,3},{3,2},{4,5},{5,4},{6,7},{7,6},{8,9},{9,8},{10,11... | collective-permute-start | bytes 786440 | tf_op jit(solution)/shard_map/ppermute | solution.py:225

commit v5 on v4

--- a/solution.py
+++ b/solution.py
@@ -148,16 +148,27 @@
         ref[(*at, lanes)] = total[:, 128 * half : 128 * (half + 1)]
 
 
-def right_body(col_ref, mine_ref, other_ref, out_ref, left_ref):
+def right_half(col_ref, basis_ref):
+    total = jnp.zeros((96, 128), F32)
     for n in range(16):
         cols = [col_ref[:, 2 * n + s].astype(F32).reshape(96, 128) for s in (0, 1)]
-        left_ref[n] = jnp.concatenate(cols, axis=1).astype(BF16)
-    total = times_basis(left_ref, mine_ref, other_ref).astype(BF16)
+        block = basis_ref[n // 2, pl.ds(96 + 256 * (n % 2), 256), :]
+        total = total + dot(jnp.concatenate(cols, axis=1).astype(BF16), block)
+    return total
+
+
+def right_mine_body(col_ref, mine_ref, out_ref):
+    out_ref[...] = right_half(col_ref, mine_ref)
+
+
+def right_other_body(col_ref, other_ref, part_ref, out_ref):
+    total = jnp.concatenate([part_ref[...], right_half(col_ref, other_ref)], axis=1).astype(BF16)
     for q in range(4):
         in_order(total, out_ref, q, slice(None))
 
 
-def left_modes_body(cmaps_ref, pmaps_ref, col_ref, mine_ref, other_ref, out_ref, left_ref):
+def left_modes_body(cmaps_ref, pmaps_ref, col_ref, mine_ref, other_ref, half_ref, out_ref, near_ref, left_ref):
+    near_ref[...] = stiff_part(half_ref, lax.axis_index("b"), mine_ref, other_ref)
     first = 2 * lax.axis_index("g")
     for n in range(16):
         pair = []
@@ -173,22 +184,19 @@
     in_order(-times_basis(left_ref, mine_ref, other_ref), out_ref, slice(None))
 
 
-def left_stiff_body(mine_ref, other_ref, half_ref, other_half_ref, after_ref, out_ref, low, high, left_ref, sems):
-    b = lax.axis_index("b")
-    for k, ref in enumerate((half_ref, other_half_ref)):
-        for value, rows in enumerate((low, high)):
-
-            @pl.when((b ^ k) == value)
-            def _(ref=ref, rows=rows, k=k):
-                pltpu.make_async_copy(ref, rows, sems.at[k]).start()
-
-    for k in (0, 1):
-        pltpu.make_async_copy(half_ref, low, sems.at[k]).wait()
-    for n in range(16):
-        part = (low, high)[n % 2]
-        rows = [part[pl.ds(128 * (8 * s + n // 2), 128), :].astype(F32).T for s in (0, 1)]
-        left_ref[n] = jnp.concatenate(rows, axis=1).astype(BF16)
-    in_order(times_basis(left_ref, mine_ref, other_ref), out_ref, slice(None))
+def stiff_part(rows_ref, side, mine_ref, other_ref):
+    total = jnp.zeros((128, 256), F32)
+    for k in range(8):
+        rows = [rows_ref[pl.ds(128 * (8 * s + k), 128), :].astype(F32).T for s in (0, 1)]
+        at = pl.ds(pl.multiple_of(96 + 256 * side, 32), 256)
+        block = jnp.concatenate([mine_ref[k, at, :], other_ref[k, at, :]], axis=1)
+        total = total + dot(jnp.concatenate(rows, axis=1).astype(BF16), block)
+    return total
+
+
+def left_stiff_body(mine_ref, other_ref, other_half_ref, near_ref, out_ref):
+    total = near_ref[...] + stiff_part(other_half_ref, 1 - lax.axis_index("b"), mine_ref, other_ref)
+    in_order(total, out_ref, slice(None))
 
 
 def project(body, out, dtype, specs, scratch, name, *args):
@@ -260,19 +268,22 @@
     columns = exchange(copies.reshape(176, 24, 128), LEAF).reshape(4, 44, 24, 128)
 
     modes_left = pltpu.VMEM((16, 96, 256), BF16)
-    right = project(
-        right_body, (4, 96, 256), BF16, [VM, VM, VM], [modes_left], "right", columns, mine, other
-    )
+    part = project(right_mine_body, (96, 128), F32, [VM, VM], [], "right_mine", columns, mine)
+    right = project(right_other_body, (4, 96, 256), BF16, [VM] * 3, [], "right_other", columns, other, part)
     right = exchange(right.reshape(384, 256), LEAF).reshape(4, 96, 256)
     child_maps = columns[:, 42, 16, :32].astype(jnp.int32)
-    modes = project(
-        left_modes_body, (96, 256), F32, [SM, SM, VM, VM, VM], [modes_left], "left_modes",
-        child_maps, parent_map, columns, mine, other,
-    )
+    modes, near_stiff = pl.pallas_call(
+        left_modes_body,
+        out_shape=[jax.ShapeDtypeStruct((96, 256), F32), jax.ShapeDtypeStruct((128, 256), F32)],
+        in_specs=[SM, SM] + [VM] * 4,
+        out_specs=[VM, VM],
+        scratch_shapes=[modes_left],
+        compiler_params=pltpu.CompilerParams(vmem_limit_bytes=12 << 20),
+        cost_estimate=pl.CostEstimate(flops=0, bytes_accessed=0, transcendentals=0),
+        name="left_modes",
+    )(child_maps, parent_map, columns, mine, other, half)
     stiff = project(
-        left_stiff_body, (128, 256), F32, [VM, VM, ANY, ANY, ANY],
-        [pltpu.VMEM((2048, 128), BF16)] * 2 + [pltpu.VMEM((16, 128, 256), BF16), pltpu.SemaphoreType.DMA((2,))],
-        "left_stiff", mine, other, half, other_half, modes,
+        left_stiff_body, (128, 256), F32, [VM] * 4, [], "left_stiff", mine, other, other_half, near_stiff
     )
     kept, sent = pl.pallas_call(
         final_body,

time: 107 us -> 107 us (level)
  local copies, waits for them, and re-layouts: 3.66 us -> 0.01 us
  Pallas kernels: 13.5 us -> 15.9 us
  waiting for transfers between devices: 32.3 us -> 33.5 us
    unnamed x16 -> x8, local copies, waits for them, and re-layouts: 3.66 us -> 0.01 us
    pallas_call x0 -> x1, Pallas kernels: none -> 2.64 us  [shards(): pl.pallas_call(left_modes_body, out_shape=[jax.ShapeDtypeStruct((96, 256)...]
    all_to_all x4, waiting for transfers between devices: 17.2 us -> 19.2 us  [exchange(): return lax.all_to_all(value, axis, 0, 0, tiled=True)]
  transfers between devices with their start and end apart: 9 -> 9, of which waited for: 7 -> 7; matrix products, arithmetic and copies ran while one was open for 0% -> 0% of each run, Pallas kernels for 8% -> 10%
where the time goes in v5:
time: 107 us; the launch traced here: 106 us
  starting transfers between devices  38.9 us (36%)
  waiting for transfers between devices  33.5 us (31%)
  blocking collectives  16.8 us (16%)
  Pallas kernels  15.9 us (15%)
    all_to_all x4, starting transfers between devices, exchange(): return lax.all_to_all(value, axis, 0, 0, tiled=True)  25.3 us
    all_to_all x4, waiting for transfers between devices, exchange(): return lax.all_to_all(value, axis, 0, 0, tiled=True)  19.2 us
    all_to_all x1, blocking collectives, exchange(): return lax.all_to_all(value, axis, 0, 0, tiled=True)  16.8 us
    ppermute x5, waiting for transfers between devices, swap(): return lax.ppermute(value, axis, [(i, i ^ mask) for i in range(size)])  14.3 us
    ppermute x5, starting transfers between devices, swap(): return lax.ppermute(value, axis, [(i, i ^ mask) for i in range(size)])  13.6 us
    pallas_call x3, Pallas kernels, project(): pl.pallas_call(body, out_shape=jax.ShapeDtypeStruct(out, dtype), in_specs...  4.56 us
    pallas_call x1, Pallas kernels, couple(): pl.pallas_call(coupling_body, grid=(steps,), out_shape=jax.ShapeDtypeStru...  3.56 us
    pallas_call x1, Pallas kernels, shards(): pl.pallas_call(left_modes_body, out_shape=[jax.ShapeDtypeStruct((96, 256)...  2.64 us
  transfers between devices with their start and end apart: 9, of which 7 were waited for; matrix products, arithmetic and copies ran while one was open for 0% of the time, Pallas kernels for 10%

profile of v5, /device:TPU:56, one launch (start us, length us, event | category | flops | bytes accessed | tf_op | source)
XLA Modules:
  0.0 106.1 jit_solution(7012559606613685944)
XLA Ops:
  0.0 3.6 %coupling.1 = bf16[4,448,128]{2,1,0:T(8,128)(2,1)} custom-call(bf16[2048,512]{1,0:T(8,128)(2,1)} %bitcast.21, bf16[128,2048]{1,0:T(8,128)(2,1)} %bitcast.23, f32[1,512]{1,0:T(1,128)} %ce_ref.1, bf16[2048,256]{1,0:T(8,128)(2,1)} %bitcast.22, bf16[128,2048]{1,0:T(8,128)(2,1)} %bitcast.24, f32[1,256]{1,0:T(1,128)} %pe_ref.1, bf16[128,256]{1,0:T(8,128)(2,1)} %bitcast.18), custom_call_target="tpu_custom_call" | custom-call | tf_op jit(solution)/shard_map/coupling/pallas_call | solution.py:70
  3.6 10.3 %all-to-all-start = ((bf16[4,448,128]{2,1,0:T(8,128)(2,1)}), bf16[4,448,128]{2,1,0:T(8,128)(2,1)S(1)}, u32[]{:S(2)}, u32[]{:S(2)}) async-start(bf16[4,448,128]{2,1,0:T(8,128)(2,1)} %coupling.1), calls=%async_computation | async-start | bytes 917504 | tf_op jit(solution)/shard_map/all_to_all | solution.py:237
  13.9 2.3 %regroup.1 = (bf16[2048,128]{1,0:T(8,128)(2,1)S(1)}, bf16[2048,128]{1,0:T(8,128)(2,1)S(1)}) custom-call(bf16[4096,128]{1,0:T(8,128)(2,1)S(1)} %bitcast.17, s32[1,32]{1,0:T(1,128)S(1)} %copy-done.3, s32[8,32]{1,0:T(8,128)S(1)} %copy-done.2), custom_call_target="tpu_custom_call" | custom-call | tf_op jit(solution)/shard_map/regroup/pallas_call | solution.py:97
  16.2 3.3 %collective-permute-start.1 = (bf16[2048,128]{1,0:T(8,128)(2,1)S(1)}, bf16[2048,128]{1,0:T(8,128)(2,1)S(1)}, u32[]{:S(2)}, u32[]{:S(2)}) collective-permute-start(bf16[2048,128]{1,0:T(8,128)(2,1)S(1)} %get-tuple-element.14), channel_id=1, source_target_pairs={{0,64},{64,0},{1,65},{65,1},{2,66},{66,2},{3,67},{67,3},{4,68},{68... | collective-permute-start | bytes 1572872 | tf_op jit(solution)/shard_map/ppermute | solution.py:233
  19.5 8.4 %all-to-all-done.got_ref = bf16[4,448,128]{2,1,0:T(8,128)(2,1)S(1)} async-done(((bf16[4,448,128]{2,1,0:T(8,128)(2,1)}), bf16[4,448,128]{2,1,0:T(8,128)(2,1)S(1)}, u32[]{:S(2)}, u32[]{:S(2)}) %all-to-all-start) | async-done | bytes 458784 | tf_op jit(solution)/shard_map/all_to_all | solution.py:237
  27.9 1.2 %split.1 = bf16[8,608,128]{2,1,0:T(8,128)(2,1)} custom-call(bf16[4,448,128]{2,1,0:T(8,128)(2,1)S(1)} %all-to-all-done.got_ref), custom_call_target="tpu_custom_call" | custom-call | tf_op jit(solution)/shard_map/split/pallas_call | solution.py:23
  29.1 4.3 %all-to-all-start.1 = ((bf16[8,608,128]{2,1,0:T(8,128)(2,1)}), bf16[8,608,128]{2,1,0:T(8,128)(2,1)S(1)}, u32[]{:S(2)}, u32[]{:S(2)}) async-start(bf16[8,608,128]{2,1,0:T(8,128)(2,1)} %split.1), calls=%async_computation.1 | async-start | bytes 2490368 | tf_op jit(solution)/shard_map/all_to_all | solution.py:237
  33.6 4.6 %collective-permute-start.2 = (bf16[2048,128]{1,0:T(8,128)(2,1)S(1)}, bf16[2048,128]{1,0:T(8,128)(2,1)S(1)}, u32[]{:S(2)}, u32[]{:S(2)}) collective-permute-start(bf16[2048,128]{1,0:T(8,128)(2,1)S(1)} %add_convert_fusion.near_ref), channel_id=1, source_target_pairs={{0,32},{32,0},{1,33},{33,1},{2,34},{34,2},{3,35},{35,3},{4,36},{36... | collective-permute-start | bytes 1572872 | tf_op jit(solution)/shard_map/ppermute | solution.py:233
  38.1 12.6 %collective-permute-done.2.far_ref = bf16[2048,128]{1,0:T(8,128)(2,1)S(1)} collective-permute-done((bf16[2048,128]{1,0:T(8,128)(2,1)S(1)}, bf16[2048,128]{1,0:T(8,128)(2,1)S(1)}, u32[]{:S(2)}, u32[]{:S(2)}) %collective-permute-start.2) | collective-permute-done | bytes 524320 | tf_op jit(solution)/shard_map/ppermute | solution.py:233
  50.7 0.8 all-to-all-done.1.one_ref.mine_ref
  51.5 1.2 %repeat.1 = (bf16[4,44,24,128]{3,2,1,0:T(8,128)(2,1)}, bf16[2048,128]{1,0:T(8,128)(2,1)S(1)}) custom-call(bf16[8,608,128]{2,1,0:T(8,128)(2,1)S(1)} %all-to-all-done.1.one_ref.mine_ref, bf16[128,256]{1,0:T(8,128)(2,1)S(1)} %bitcast.19, s32[1,32]{1,0:T(1,128)S(1)} %copy-done.3, bf16[2048,128]{1,0:T(8,128)(2,1)S(1)} %add_convert_fusion.near_ref, ...), custom_call_target="tpu_custom_call" | custom-call | tf_op jit(solution)/shard_map/repeat/pallas_call | solution.py:23
  52.6 5.4 %all-to-all-start.2 = ((bf16[176,24,128]{2,1,0:T(8,128)(2,1)}), bf16[176,24,128]{2,1,0:T(8,128)(2,1)S(1)}, u32[]{:S(2)}, u32[]{:S(2)}) async-start(bf16[176,24,128]{2,1,0:T(8,128)(2,1)} %bitcast.6), calls=%async_computation.2 | async-start | bytes 2162688 | tf_op jit(solution)/shard_map/all_to_all | solution.py:237
  58.0 1.9 %collective-permute-start = (bf16[8,608,128]{2,1,0:T(8,128)(2,1)S(1)}, bf16[8,608,128]{2,1,0:T(8,128)(2,1)}, u32[]{:S(2)}, u32[]{:S(2)}) collective-permute-start(bf16[8,608,128]{2,1,0:T(8,128)(2,1)S(1)} %all-to-all-done.1.one_ref.mine_ref), channel_id=1, source_target_pairs={{0,1},{1,0},{2,3},{3,2},{4,5},{5,4},{6,7},{7,6},{8,9},{9,8},{10,11... | collective-permute-start | bytes 3735560 | tf_op jit(solution)/shard_map/ppermute | solution.py:233
  59.9 1.9 %collective-permute-start.3 = (bf16[2048,128]{1,0:T(8,128)(2,1)S(1)}, bf16[2048,128]{1,0:T(8,128)(2,1)}, u32[]{:S(2)}, u32[]{:S(2)}) collective-permute-start(bf16[2048,128]{1,0:T(8,128)(2,1)S(1)} %get-tuple-element.15.half_ref), channel_id=1, source_target_pairs={{0,64},{64,0},{1,65},{65,1},{2,66},{66,2},{3,67},{67,3},{4,68},{68... | collective-permute-start | bytes 1572872 | tf_op jit(solution)/shard_map/ppermute | solution.py:233
  61.9 9.6 %all-to-all-done.2 = bf16[176,24,128]{2,1,0:T(8,128)(2,1)S(1)} async-done(((bf16[176,24,128]{2,1,0:T(8,128)(2,1)}), bf16[176,24,128]{2,1,0:T(8,128)(2,1)S(1)}, u32[]{:S(2)}, u32[]{:S(2)}) %all-to-all-start.2) | async-done | bytes 1081376 | tf_op jit(solution)/shard_map/all_to_all | solution.py:237
  71.8 2.4 %right_other.1 = bf16[4,96,256]{2,1,0:T(8,128)(2,1)} custom-call(bf16[4,44,24,128]{3,2,1,0:T(8,128)(2,1)S(1)} %bitcast.13, bf16[8,608,128]{2,1,0:T(8,128)(2,1)} %collective-permute-done.other_ref, f32[96,128]{1,0:T(8,128)S(1)} %right_mine.1.part_ref), custom_call_target="tpu_custom_call" | custom-call | tf_op jit(solution)/shard_map/right_other/pallas_call | solution.py:203
  74.2 5.3 %all-to-all-start.3 = ((bf16[4,96,256]{2,1,0:T(8,128)(2,1)}), bf16[4,96,256]{2,1,0:T(8,128)(2,1)S(1)}, u32[]{:S(2)}, u32[]{:S(2)}) async-start(bf16[4,96,256]{2,1,0:T(8,128)(2,1)} %right_other.1), calls=%async_computation.3 | async-start | bytes 393216 | tf_op jit(solution)/shard_map/all_to_all | solution.py:237
  79.6 2.6 %left_modes.1 = (f32[96,256]{1,0:T(8,128)S(1)}, f32[128,256]{1,0:T(8,128)S(1)}) custom-call(s32[4,32]{1,0:T(4,128)S(1)} %bitcast.20, s32[8,32]{1,0:T(8,128)S(1)} %copy-done.2, bf16[4,44,24,128]{3,2,1,0:T(8,128)(2,1)S(1)} %bitcast.15, bf16[8,608,128]{2,1,0:T(8,128)(2,1)S(1)} %all-to-all-done.1.one_ref.mine_ref, ...), custom_call_target="tpu_custom_call" | custom-call | tf_op jit(solution)/shard_map/left_modes/pallas_call | solution.py:275
  82.5 1.8 %left_stiff.1.stiff_ref = f32[128,256]{1,0:T(8,128)S(1)} custom-call(bf16[8,608,128]{2,1,0:T(8,128)(2,1)S(1)} %all-to-all-done.1.one_ref.mine_ref, bf16[8,608,128]{2,1,0:T(8,128)(2,1)} %collective-permute-done.other_ref, bf16[2048,128]{1,0:T(8,128)(2,1)} %collective-permute-done.3.other_half_ref, f32[128,256]{1,0:T(8,128)S(1)} %get-tuple-element.17.near_ref), custom_call_target="tpu_custom_call" | custom-call | tf_op jit(solution)/shard_map/left_stiff/pallas_call | solution.py:203
  84.3 0.4 all-to-all-done.3.right_ref
  85.1 1.9 %collective-permute-start.4 = (bf16[128,1024]{1,0:T(8,128)(2,1)S(1)}, bf16[128,1024]{1,0:T(8,128)(2,1)S(1)}, u32[]{:S(2)}, u32[]{:S(2)}) collective-permute-start(bf16[128,1024]{1,0:T(8,128)(2,1)S(1)} %get-tuple-element.20), channel_id=1, source_target_pairs={{0,1},{1,0},{2,3},{3,2},{4,5},{5,4},{6,7},{7,6},{8,9},{9,8},{10,11... | collective-permute-start | bytes 786440 | tf_op jit(solution)/shard_map/ppermute | solution.py:233
  87.1 1.5 %collective-permute-done.4 = bf16[128,1024]{1,0:T(8,128)(2,1)S(1)} collective-permute-done((bf16[128,1024]{1,0:T(8,128)(2,1)S(1)}, bf16[128,1024]{1,0:T(8,128)(2,1)S(1)}, u32[]{:S(2)}, u32[]{:S(2)}) %collective-permute-start.4) | collective-permute-done | bytes 262176 | tf_op jit(solution)/shard_map/ppermute | solution.py:233
  88.6 16.8 %all_to_all.26 = bf16[16,8,1024]{2,1,0:T(8,128)(2,1)S(1)} all-to-all(bf16[16,8,1024]{2,1,0:T(8,128)(2,1)S(1)} %fusion), channel_id=1, replica_groups=mesh['g'=4,'b'=2,'a'=2,'z'=4,'x'=4,'c'=2] {'z','x'}, dimensions={0} | all-to-all | bytes 524288 | tf_op jit(solution)/shard_map/all_to_all | solution.py:237
  105.4 0.7 convert_reduce_fusion
  (16 shorter events, 1.3 us)
Async XLA Ops:
  0.0 13.9 %copy-start = (bf16[1,4096,128]{2,1,0:T(8,128)(2,1)S(1)}, bf16[1,4096,128]{2,1,0:T(8,128)(2,1)}, u32[]{:S(2)}) copy-start(bf16[1,4096,128]{2,1,0:T(8,128)(2,1)} %param.10) | copy-start | bytes 3145732
  0.0 13.9 %copy-start.2 = (s32[8,32]{1,0:T(8,128)S(1)}, s32[8,32]{1,0:T(8,128)}, u32[]{:S(2)}) copy-start(s32[8,32]{1,0:T(8,128)} %pmaps_ref.1) | copy-start | bytes 3076
  0.0 13.9 %copy-start.3 = (s32[1,32]{1,0:T(1,128)S(1)}, s32[1,32]{1,0:T(1,128)}, u32[]{:S(2)}) copy-start(s32[1,32]{1,0:T(1,128)} %row_ref.1) | copy-start | bytes 388
  3.6 24.3 %all-to-all-start = ((bf16[4,448,128]{2,1,0:T(8,128)(2,1)}), bf16[4,448,128]{2,1,0:T(8,128)(2,1)S(1)}, u32[]{:S(2)}, u32[]{:S(2)}) async-start(bf16[4,448,128]{2,1,0:T(8,128)(2,1)} %coupling.1), calls=%async_computation | async-start | bytes 917504 | tf_op jit(solution)/shard_map/all_to_all | solution.py:237
  16.2 17.2 %collective-permute-start.1 = (bf16[2048,128]{1,0:T(8,128)(2,1)S(1)}, bf16[2048,128]{1,0:T(8,128)(2,1)S(1)}, u32[]{:S(2)}, u32[]{:S(2)}) collective-permute-start(bf16[2048,128]{1,0:T(8,128)(2,1)S(1)} %get-tuple-element.14), channel_id=1, source_target_pairs={{0,64},{64,0},{1,65},{65,1},{2,66},{66,2},{3,67},{67,3},{4,68},{68... | collective-permute-start | bytes 1572872 | tf_op jit(solution)/shard_map/ppermute | solution.py:233
  29.1 22.4 %all-to-all-start.1 = ((bf16[8,608,128]{2,1,0:T(8,128)(2,1)}), bf16[8,608,128]{2,1,0:T(8,128)(2,1)S(1)}, u32[]{:S(2)}, u32[]{:S(2)}) async-start(bf16[8,608,128]{2,1,0:T(8,128)(2,1)} %split.1), calls=%async_computation.1 | async-start | bytes 2490368 | tf_op jit(solution)/shard_map/all_to_all | solution.py:237
  33.4 18.1 %copy-start.1 = (bf16[1,128,256]{2,1,0:T(8,128)(2,1)S(1)}, bf16[1,128,256]{2,1,0:T(8,128)(2,1)}, u32[]{:S(2)}) copy-start(bf16[1,128,256]{2,1,0:T(8,128)(2,1)} %param.19) | copy-start | bytes 196612
  33.6 17.1 %collective-permute-start.2 = (bf16[2048,128]{1,0:T(8,128)(2,1)S(1)}, bf16[2048,128]{1,0:T(8,128)(2,1)S(1)}, u32[]{:S(2)}, u32[]{:S(2)}) collective-permute-start(bf16[2048,128]{1,0:T(8,128)(2,1)S(1)} %add_convert_fusion.near_ref), channel_id=1, source_target_pairs={{0,32},{32,0},{1,33},{33,1},{2,34},{34,2},{3,35},{35,3},{4,36},{36... | collective-permute-start | bytes 1572872 | tf_op jit(solution)/shard_map/ppermute | solution.py:233
  52.6 18.8 %all-to-all-start.2 = ((bf16[176,24,128]{2,1,0:T(8,128)(2,1)}), bf16[176,24,128]{2,1,0:T(8,128)(2,1)S(1)}, u32[]{:S(2)}, u32[]{:S(2)}) async-start(bf16[176,24,128]{2,1,0:T(8,128)(2,1)} %bitcast.6), calls=%async_computation.2 | async-start | bytes 2162688 | tf_op jit(solution)/shard_map/all_to_all | solution.py:237
  58.0 13.8 %collective-permute-start = (bf16[8,608,128]{2,1,0:T(8,128)(2,1)S(1)}, bf16[8,608,128]{2,1,0:T(8,128)(2,1)}, u32[]{:S(2)}, u32[]{:S(2)}) collective-permute-start(bf16[8,608,128]{2,1,0:T(8,128)(2,1)S(1)} %all-to-all-done.1.one_ref.mine_ref), channel_id=1, source_target_pairs={{0,1},{1,0},{2,3},{3,2},{4,5},{5,4},{6,7},{7,6},{8,9},{9,8},{10,11... | collective-permute-start | bytes 3735560 | tf_op jit(solution)/shard_map/ppermute | solution.py:233
  59.9 22.5 %collective-permute-start.3 = (bf16[2048,128]{1,0:T(8,128)(2,1)S(1)}, bf16[2048,128]{1,0:T(8,128)(2,1)}, u32[]{:S(2)}, u32[]{:S(2)}) collective-permute-start(bf16[2048,128]{1,0:T(8,128)(2,1)S(1)} %get-tuple-element.15.half_ref), channel_id=1, source_target_pairs={{0,64},{64,0},{1,65},{65,1},{2,66},{66,2},{3,67},{67,3},{4,68},{68... | collective-permute-start | bytes 1572872 | tf_op jit(solution)/shard_map/ppermute | solution.py:233
  74.2 10.5 %all-to-all-start.3 = ((bf16[4,96,256]{2,1,0:T(8,128)(2,1)}), bf16[4,96,256]{2,1,0:T(8,128)(2,1)S(1)}, u32[]{:S(2)}, u32[]{:S(2)}) async-start(bf16[4,96,256]{2,1,0:T(8,128)(2,1)} %right_other.1), calls=%async_computation.3 | async-start | bytes 393216 | tf_op jit(solution)/shard_map/all_to_all | solution.py:237
  85.1 3.4 %collective-permute-start.4 = (bf16[128,1024]{1,0:T(8,128)(2,1)S(1)}, bf16[128,1024]{1,0:T(8,128)(2,1)S(1)}, u32[]{:S(2)}, u32[]{:S(2)}) collective-permute-start(bf16[128,1024]{1,0:T(8,128)(2,1)S(1)} %get-tuple-element.20), channel_id=1, source_target_pairs={{0,1},{1,0},{2,3},{3,2},{4,5},{5,4},{6,7},{7,6},{8,9},{9,8},{10,11... | collective-permute-start | bytes 786440 | tf_op jit(solution)/shard_map/ppermute | solution.py:233

commit v6 on v5

--- a/solution.py
+++ b/solution.py
@@ -194,8 +194,21 @@
     return total
 
 
-def left_stiff_body(mine_ref, other_ref, other_half_ref, near_ref, out_ref):
-    total = near_ref[...] + stiff_part(other_half_ref, 1 - lax.axis_index("b"), mine_ref, other_ref)
+def left_stiff_body(mine_ref, other_ref, other_half_ref, near_ref, out_ref, rows_ref, held_ref, sems):
+    at = pl.ds(pl.multiple_of(96 + 256 * (1 - lax.axis_index("b")), 32), 256)
+    copies = [
+        pltpu.make_async_copy(other_half_ref, rows_ref, sems.at[0]),
+        pltpu.make_async_copy(other_ref.at[:, at, :], held_ref, sems.at[1]),
+    ]
+    for copy in copies:
+        copy.start()
+    for copy in copies:
+        copy.wait()
+    total = near_ref[...]
+    for k in range(8):
+        rows = [rows_ref[pl.ds(128 * (8 * s + k), 128), :].astype(F32).T for s in (0, 1)]
+        block = jnp.concatenate([mine_ref[k, at, :], held_ref[k]], axis=1)
+        total = total + dot(jnp.concatenate(rows, axis=1).astype(BF16), block)
     in_order(total, out_ref, slice(None))
 
 
@@ -283,7 +296,9 @@
         name="left_modes",
     )(child_maps, parent_map, columns, mine, other, half)
     stiff = project(
-        left_stiff_body, (128, 256), F32, [VM] * 4, [], "left_stiff", mine, other, other_half, near_stiff
+        left_stiff_body, (128, 256), F32, [VM, ANY, ANY, VM],
+        [pltpu.VMEM((2048, 128), BF16), pltpu.VMEM((8, 256, 128), BF16), pltpu.SemaphoreType.DMA((2,))],
+        "left_stiff", mine, other, other_half, near_stiff
     )
     kept, sent = pl.pallas_call(
         final_body,

time: 107 us -> 107 us (level)
  no operation moved by 1% of the time
where the time goes in v6:
time: 107 us; the launch traced here: 106 us
  starting transfers between devices  38.9 us (36%)
  waiting for transfers between devices  33.7 us (31%)
  blocking collectives  16.6 us (16%)
  Pallas kernels  15.7 us (15%)
    all_to_all x4, starting transfers between devices, exchange(): return lax.all_to_all(value, axis, 0, 0, tiled=True)  25.3 us
    all_to_all x4, waiting for transfers between devices, exchange(): return lax.all_to_all(value, axis, 0, 0, tiled=True)  19.4 us
    all_to_all x1, blocking collectives, exchange(): return lax.all_to_all(value, axis, 0, 0, tiled=True)  16.6 us
    ppermute x5, waiting for transfers between devices, swap(): return lax.ppermute(value, axis, [(i, i ^ mask) for i in range(size)])  14.3 us
    ppermute x5, starting transfers between devices, swap(): return lax.ppermute(value, axis, [(i, i ^ mask) for i in range(size)])  13.6 us
    pallas_call x3, Pallas kernels, project(): pl.pallas_call(body, out_shape=jax.ShapeDtypeStruct(out, dtype), in_specs...  4.35 us
    pallas_call x1, Pallas kernels, couple(): pl.pallas_call(coupling_body, grid=(steps,), out_shape=jax.ShapeDtypeStru...  3.56 us
    pallas_call x1, Pallas kernels, shards(): pl.pallas_call(left_modes_body, out_shape=[jax.ShapeDtypeStruct((96, 256)...  2.64 us
  transfers between devices with their start and end apart: 9, of which 7 were waited for; matrix products, arithmetic and copies ran while one was open for 0% of the time, Pallas kernels for 10%

profile of v6, /device:TPU:56, one launch (start us, length us, event | category | flops | bytes accessed | tf_op | source)
XLA Modules:
  0.0 105.9 jit_solution(869765076583642194)
XLA Ops:
  0.0 3.6 %coupling.1 = bf16[4,448,128]{2,1,0:T(8,128)(2,1)} custom-call(bf16[2048,512]{1,0:T(8,128)(2,1)} %bitcast.21, bf16[128,2048]{1,0:T(8,128)(2,1)} %bitcast.23, f32[1,512]{1,0:T(1,128)} %ce_ref.1, bf16[2048,256]{1,0:T(8,128)(2,1)} %bitcast.22, bf16[128,2048]{1,0:T(8,128)(2,1)} %bitcast.24, f32[1,256]{1,0:T(1,128)} %pe_ref.1, bf16[128,256]{1,0:T(8,128)(2,1)} %bitcast.18), custom_call_target="tpu_custom_call" | custom-call | tf_op jit(solution)/shard_map/coupling/pallas_call | solution.py:70
  3.6 10.3 %all-to-all-start = ((bf16[4,448,128]{2,1,0:T(8,128)(2,1)}), bf16[4,448,128]{2,1,0:T(8,128)(2,1)S(1)}, u32[]{:S(2)}, u32[]{:S(2)}) async-start(bf16[4,448,128]{2,1,0:T(8,128)(2,1)} %coupling.1), calls=%async_computation | async-start | bytes 917504 | tf_op jit(solution)/shard_map/all_to_all | solution.py:250
  13.9 2.3 %regroup.1 = (bf16[2048,128]{1,0:T(8,128)(2,1)S(1)}, bf16[2048,128]{1,0:T(8,128)(2,1)S(1)}) custom-call(bf16[4096,128]{1,0:T(8,128)(2,1)S(1)} %bitcast.17, s32[1,32]{1,0:T(1,128)S(1)} %copy-done.3, s32[8,32]{1,0:T(8,128)S(1)} %copy-done.2), custom_call_target="tpu_custom_call" | custom-call | tf_op jit(solution)/shard_map/regroup/pallas_call | solution.py:97
  16.2 3.3 %collective-permute-start.1 = (bf16[2048,128]{1,0:T(8,128)(2,1)S(1)}, bf16[2048,128]{1,0:T(8,128)(2,1)S(1)}, u32[]{:S(2)}, u32[]{:S(2)}) collective-permute-start(bf16[2048,128]{1,0:T(8,128)(2,1)S(1)} %get-tuple-element.14), channel_id=1, source_target_pairs={{0,64},{64,0},{1,65},{65,1},{2,66},{66,2},{3,67},{67,3},{4,68},{68... | collective-permute-start | bytes 1572872 | tf_op jit(solution)/shard_map/ppermute | solution.py:246
  19.5 8.4 %all-to-all-done.got_ref = bf16[4,448,128]{2,1,0:T(8,128)(2,1)S(1)} async-done(((bf16[4,448,128]{2,1,0:T(8,128)(2,1)}), bf16[4,448,128]{2,1,0:T(8,128)(2,1)S(1)}, u32[]{:S(2)}, u32[]{:S(2)}) %all-to-all-start) | async-done | bytes 458784 | tf_op jit(solution)/shard_map/all_to_all | solution.py:250
  27.9 1.2 %split.1 = bf16[8,608,128]{2,1,0:T(8,128)(2,1)} custom-call(bf16[4,448,128]{2,1,0:T(8,128)(2,1)S(1)} %all-to-all-done.got_ref), custom_call_target="tpu_custom_call" | custom-call | tf_op jit(solution)/shard_map/split/pallas_call | solution.py:23
  29.1 4.3 %all-to-all-start.1 = ((bf16[8,608,128]{2,1,0:T(8,128)(2,1)}), bf16[8,608,128]{2,1,0:T(8,128)(2,1)S(1)}, u32[]{:S(2)}, u32[]{:S(2)}) async-start(bf16[8,608,128]{2,1,0:T(8,128)(2,1)} %split.1), calls=%async_computation.1 | async-start | bytes 2490368 | tf_op jit(solution)/shard_map/all_to_all | solution.py:250
  33.6 4.6 %collective-permute-start.2 = (bf16[2048,128]{1,0:T(8,128)(2,1)S(1)}, bf16[2048,128]{1,0:T(8,128)(2,1)S(1)}, u32[]{:S(2)}, u32[]{:S(2)}) collective-permute-start(bf16[2048,128]{1,0:T(8,128)(2,1)S(1)} %add_convert_fusion.near_ref), channel_id=1, source_target_pairs={{0,32},{32,0},{1,33},{33,1},{2,34},{34,2},{3,35},{35,3},{4,36},{36... | collective-permute-start | bytes 1572872 | tf_op jit(solution)/shard_map/ppermute | solution.py:246
  38.1 12.6 %collective-permute-done.2.far_ref = bf16[2048,128]{1,0:T(8,128)(2,1)S(1)} collective-permute-done((bf16[2048,128]{1,0:T(8,128)(2,1)S(1)}, bf16[2048,128]{1,0:T(8,128)(2,1)S(1)}, u32[]{:S(2)}, u32[]{:S(2)}) %collective-permute-start.2) | collective-permute-done | bytes 524320 | tf_op jit(solution)/shard_map/ppermute | solution.py:246
  50.7 0.8 all-to-all-done.1.one_ref.mine_ref
  51.5 1.2 %repeat.1 = (bf16[4,44,24,128]{3,2,1,0:T(8,128)(2,1)}, bf16[2048,128]{1,0:T(8,128)(2,1)S(1)}) custom-call(bf16[8,608,128]{2,1,0:T(8,128)(2,1)S(1)} %all-to-all-done.1.one_ref.mine_ref, bf16[128,256]{1,0:T(8,128)(2,1)S(1)} %bitcast.19, s32[1,32]{1,0:T(1,128)S(1)} %copy-done.3, bf16[2048,128]{1,0:T(8,128)(2,1)S(1)} %add_convert_fusion.near_ref, ...), custom_call_target="tpu_custom_call" | custom-call | tf_op jit(solution)/shard_map/repeat/pallas_call | solution.py:23
  52.6 5.4 %all-to-all-start.2 = ((bf16[176,24,128]{2,1,0:T(8,128)(2,1)}), bf16[176,24,128]{2,1,0:T(8,128)(2,1)S(1)}, u32[]{:S(2)}, u32[]{:S(2)}) async-start(bf16[176,24,128]{2,1,0:T(8,128)(2,1)} %bitcast.6), calls=%async_computation.2 | async-start | bytes 2162688 | tf_op jit(solution)/shard_map/all_to_all | solution.py:250
  58.0 1.9 %collective-permute-start = (bf16[8,608,128]{2,1,0:T(8,128)(2,1)S(1)}, bf16[8,608,128]{2,1,0:T(8,128)(2,1)}, u32[]{:S(2)}, u32[]{:S(2)}) collective-permute-start(bf16[8,608,128]{2,1,0:T(8,128)(2,1)S(1)} %all-to-all-done.1.one_ref.mine_ref), channel_id=1, source_target_pairs={{0,1},{1,0},{2,3},{3,2},{4,5},{5,4},{6,7},{7,6},{8,9},{9,8},{10,11... | collective-permute-start | bytes 3735560 | tf_op jit(solution)/shard_map/ppermute | solution.py:246
  59.9 1.9 %collective-permute-start.3 = (bf16[2048,128]{1,0:T(8,128)(2,1)S(1)}, bf16[2048,128]{1,0:T(8,128)(2,1)}, u32[]{:S(2)}, u32[]{:S(2)}) collective-permute-start(bf16[2048,128]{1,0:T(8,128)(2,1)S(1)} %get-tuple-element.15.half_ref), channel_id=1, source_target_pairs={{0,64},{64,0},{1,65},{65,1},{2,66},{66,2},{3,67},{67,3},{4,68},{68... | collective-permute-start | bytes 1572872 | tf_op jit(solution)/shard_map/ppermute | solution.py:246
  61.9 9.6 %all-to-all-done.2 = bf16[176,24,128]{2,1,0:T(8,128)(2,1)S(1)} async-done(((bf16[176,24,128]{2,1,0:T(8,128)(2,1)}), bf16[176,24,128]{2,1,0:T(8,128)(2,1)S(1)}, u32[]{:S(2)}, u32[]{:S(2)}) %all-to-all-start.2) | async-done | bytes 1081376 | tf_op jit(solution)/shard_map/all_to_all | solution.py:250
  71.8 2.4 %right_other.1 = bf16[4,96,256]{2,1,0:T(8,128)(2,1)} custom-call(bf16[4,44,24,128]{3,2,1,0:T(8,128)(2,1)S(1)} %bitcast.13, bf16[8,608,128]{2,1,0:T(8,128)(2,1)} %collective-permute-done.other_ref, f32[96,128]{1,0:T(8,128)S(1)} %right_mine.1.part_ref), custom_call_target="tpu_custom_call" | custom-call | tf_op jit(solution)/shard_map/right_other/pallas_call | solution.py:216
  74.2 5.3 %all-to-all-start.3 = ((bf16[4,96,256]{2,1,0:T(8,128)(2,1)}), bf16[4,96,256]{2,1,0:T(8,128)(2,1)S(1)}, u32[]{:S(2)}, u32[]{:S(2)}) async-start(bf16[4,96,256]{2,1,0:T(8,128)(2,1)} %right_other.1), calls=%async_computation.3 | async-start | bytes 393216 | tf_op jit(solution)/shard_map/all_to_all | solution.py:250
  79.6 2.6 %left_modes.1 = (f32[96,256]{1,0:T(8,128)S(1)}, f32[128,256]{1,0:T(8,128)S(1)}) custom-call(s32[4,32]{1,0:T(4,128)S(1)} %bitcast.20, s32[8,32]{1,0:T(8,128)S(1)} %copy-done.2, bf16[4,44,24,128]{3,2,1,0:T(8,128)(2,1)S(1)} %bitcast.15, bf16[8,608,128]{2,1,0:T(8,128)(2,1)S(1)} %all-to-all-done.1.one_ref.mine_ref, ...), custom_call_target="tpu_custom_call" | custom-call | tf_op jit(solution)/shard_map/left_modes/pallas_call | solution.py:288
  82.5 1.6 %left_stiff.1.stiff_ref = f32[128,256]{1,0:T(8,128)S(1)} custom-call(bf16[8,608,128]{2,1,0:T(8,128)(2,1)S(1)} %all-to-all-done.1.one_ref.mine_ref, bf16[8,608,128]{2,1,0:T(8,128)(2,1)} %collective-permute-done.other_ref, bf16[2048,128]{1,0:T(8,128)(2,1)} %collective-permute-done.3.other_half_ref, f32[128,256]{1,0:T(8,128)S(1)} %get-tuple-element.17.near_ref), custom_call_target="tpu_custom_call" | custom-call | tf_op jit(solution)/shard_map/left_stiff/pallas_call | solution.py:216
  84.1 0.7 all-to-all-done.3.right_ref
  85.1 1.9 %collective-permute-start.4 = (bf16[128,1024]{1,0:T(8,128)(2,1)S(1)}, bf16[128,1024]{1,0:T(8,128)(2,1)S(1)}, u32[]{:S(2)}, u32[]{:S(2)}) collective-permute-start(bf16[128,1024]{1,0:T(8,128)(2,1)S(1)} %get-tuple-element.20), channel_id=1, source_target_pairs={{0,1},{1,0},{2,3},{3,2},{4,5},{5,4},{6,7},{7,6},{8,9},{9,8},{10,11... | collective-permute-start | bytes 786440 | tf_op jit(solution)/shard_map/ppermute | solution.py:246
  87.1 1.5 %collective-permute-done.4 = bf16[128,1024]{1,0:T(8,128)(2,1)S(1)} collective-permute-done((bf16[128,1024]{1,0:T(8,128)(2,1)S(1)}, bf16[128,1024]{1,0:T(8,128)(2,1)S(1)}, u32[]{:S(2)}, u32[]{:S(2)}) %collective-permute-start.4) | collective-permute-done | bytes 262176 | tf_op jit(solution)/shard_map/ppermute | solution.py:246
  88.6 16.6 %all_to_all.26 = bf16[16,8,1024]{2,1,0:T(8,128)(2,1)S(1)} all-to-all(bf16[16,8,1024]{2,1,0:T(8,128)(2,1)S(1)} %fusion), channel_id=1, replica_groups=mesh['g'=4,'b'=2,'a'=2,'z'=4,'x'=4,'c'=2] {'z','x'}, dimensions={0} | all-to-all | bytes 524288 | tf_op jit(solution)/shard_map/all_to_all | solution.py:250
  105.2 0.7 convert_reduce_fusion
  (16 shorter events, 1.3 us)
Async XLA Ops:
  0.0 13.9 %copy-start = (bf16[1,4096,128]{2,1,0:T(8,128)(2,1)S(1)}, bf16[1,4096,128]{2,1,0:T(8,128)(2,1)}, u32[]{:S(2)}) copy-start(bf16[1,4096,128]{2,1,0:T(8,128)(2,1)} %param.10) | copy-start | bytes 3145732
  0.0 13.9 %copy-start.2 = (s32[8,32]{1,0:T(8,128)S(1)}, s32[8,32]{1,0:T(8,128)}, u32[]{:S(2)}) copy-start(s32[8,32]{1,0:T(8,128)} %pmaps_ref.1) | copy-start | bytes 3076
  0.0 13.9 %copy-start.3 = (s32[1,32]{1,0:T(1,128)S(1)}, s32[1,32]{1,0:T(1,128)}, u32[]{:S(2)}) copy-start(s32[1,32]{1,0:T(1,128)} %row_ref.1) | copy-start | bytes 388
  3.6 24.3 %all-to-all-start = ((bf16[4,448,128]{2,1,0:T(8,128)(2,1)}), bf16[4,448,128]{2,1,0:T(8,128)(2,1)S(1)}, u32[]{:S(2)}, u32[]{:S(2)}) async-start(bf16[4,448,128]{2,1,0:T(8,128)(2,1)} %coupling.1), calls=%async_computation | async-start | bytes 917504 | tf_op jit(solution)/shard_map/all_to_all | solution.py:250
  16.2 17.2 %collective-permute-start.1 = (bf16[2048,128]{1,0:T(8,128)(2,1)S(1)}, bf16[2048,128]{1,0:T(8,128)(2,1)S(1)}, u32[]{:S(2)}, u32[]{:S(2)}) collective-permute-start(bf16[2048,128]{1,0:T(8,128)(2,1)S(1)} %get-tuple-element.14), channel_id=1, source_target_pairs={{0,64},{64,0},{1,65},{65,1},{2,66},{66,2},{3,67},{67,3},{4,68},{68... | collective-permute-start | bytes 1572872 | tf_op jit(solution)/shard_map/ppermute | solution.py:246
  29.1 22.4 %all-to-all-start.1 = ((bf16[8,608,128]{2,1,0:T(8,128)(2,1)}), bf16[8,608,128]{2,1,0:T(8,128)(2,1)S(1)}, u32[]{:S(2)}, u32[]{:S(2)}) async-start(bf16[8,608,128]{2,1,0:T(8,128)(2,1)} %split.1), calls=%async_computation.1 | async-start | bytes 2490368 | tf_op jit(solution)/shard_map/all_to_all | solution.py:250
  33.4 18.1 %copy-start.1 = (bf16[1,128,256]{2,1,0:T(8,128)(2,1)S(1)}, bf16[1,128,256]{2,1,0:T(8,128)(2,1)}, u32[]{:S(2)}) copy-start(bf16[1,128,256]{2,1,0:T(8,128)(2,1)} %param.19) | copy-start | bytes 196612
  33.6 17.1 %collective-permute-start.2 = (bf16[2048,128]{1,0:T(8,128)(2,1)S(1)}, bf16[2048,128]{1,0:T(8,128)(2,1)S(1)}, u32[]{:S(2)}, u32[]{:S(2)}) collective-permute-start(bf16[2048,128]{1,0:T(8,128)(2,1)S(1)} %add_convert_fusion.near_ref), channel_id=1, source_target_pairs={{0,32},{32,0},{1,33},{33,1},{2,34},{34,2},{3,35},{35,3},{4,36},{36... | collective-permute-start | bytes 1572872 | tf_op jit(solution)/shard_map/ppermute | solution.py:246
  52.6 18.8 %all-to-all-start.2 = ((bf16[176,24,128]{2,1,0:T(8,128)(2,1)}), bf16[176,24,128]{2,1,0:T(8,128)(2,1)S(1)}, u32[]{:S(2)}, u32[]{:S(2)}) async-start(bf16[176,24,128]{2,1,0:T(8,128)(2,1)} %bitcast.6), calls=%async_computation.2 | async-start | bytes 2162688 | tf_op jit(solution)/shard_map/all_to_all | solution.py:250
  58.0 13.8 %collective-permute-start = (bf16[8,608,128]{2,1,0:T(8,128)(2,1)S(1)}, bf16[8,608,128]{2,1,0:T(8,128)(2,1)}, u32[]{:S(2)}, u32[]{:S(2)}) collective-permute-start(bf16[8,608,128]{2,1,0:T(8,128)(2,1)S(1)} %all-to-all-done.1.one_ref.mine_ref), channel_id=1, source_target_pairs={{0,1},{1,0},{2,3},{3,2},{4,5},{5,4},{6,7},{7,6},{8,9},{9,8},{10,11... | collective-permute-start | bytes 3735560 | tf_op jit(solution)/shard_map/ppermute | solution.py:246
  59.9 22.5 %collective-permute-start.3 = (bf16[2048,128]{1,0:T(8,128)(2,1)S(1)}, bf16[2048,128]{1,0:T(8,128)(2,1)}, u32[]{:S(2)}, u32[]{:S(2)}) collective-permute-start(bf16[2048,128]{1,0:T(8,128)(2,1)S(1)} %get-tuple-element.15.half_ref), channel_id=1, source_target_pairs={{0,64},{64,0},{1,65},{65,1},{2,66},{66,2},{3,67},{67,3},{4,68},{68... | collective-permute-start | bytes 1572872 | tf_op jit(solution)/shard_map/ppermute | solution.py:246
  74.2 10.5 %all-to-all-start.3 = ((bf16[4,96,256]{2,1,0:T(8,128)(2,1)}), bf16[4,96,256]{2,1,0:T(8,128)(2,1)S(1)}, u32[]{:S(2)}, u32[]{:S(2)}) async-start(bf16[4,96,256]{2,1,0:T(8,128)(2,1)} %right_other.1), calls=%async_computation.3 | async-start | bytes 393216 | tf_op jit(solution)/shard_map/all_to_all | solution.py:250
  85.1 3.4 %collective-permute-start.4 = (bf16[128,1024]{1,0:T(8,128)(2,1)S(1)}, bf16[128,1024]{1,0:T(8,128)(2,1)S(1)}, u32[]{:S(2)}, u32[]{:S(2)}) collective-permute-start(bf16[128,1024]{1,0:T(8,128)(2,1)S(1)} %get-tuple-element.20), channel_id=1, source_target_pairs={{0,1},{1,0},{2,3},{3,2},{4,5},{5,4},{6,7},{7,6},{8,9},{9,8},{10,11... | collective-permute-start | bytes 786440 | tf_op jit(solution)/shard_map/ppermute | solution.py:246
